TPU v7x, 128 devices: a whole 4x4x4 slice. The times are simulated.
128 devices in a mesh: group: 4 (over z), dev: 32 (over y, x, core).
Axes of the slice: x: 4, y: 4, z: 4, core: 2. Of those that a mesh axis runs over, the one named last changes fastest.
Arguments:
- query_hidden: bfloat16 [256, 32, 768], P(('group', 'dev')), may hold values from -6 to 6
- passage_hidden: bfloat16 [16384, 48, 768], P(('group', 'dev')), may hold values from -6 to 6
- head_weight: bfloat16 [768, 128], replicated, may hold values from -0.21875 to 0.21875
- teacher: float32 [256, 64], P(('group', 'dev')), may hold values from -9 to 9
- candidates: int32 [256, 64], P(('group', 'dev')), may hold values from 0 to 4095, as said below
- storage: int32 [4, 4096], P('group'), may hold values from 0 to 4095, as said below
- lengths: int32 [4, 4096], P('group'), may hold values from 12 to 48
Outputs:
- query_loss: float32 [256], P(('group', 'dev'))
- head_grad: float32 [768, 128], replicated
- query_grad: bfloat16 [256, 32, 768], P(('group', 'dev'))
- passage_grad: bfloat16 [16384, 48, 768], P(('group', 'dev'))
Inputs may be any that keep to these rules, and one draw needn't show every extreme that they name: Of the candidates of the 2 queries on one device, at most 12 have a storage position on any one device of the group (storage position // 128); in every group one device stores exactly 12 of the candidates of every device of that group. Each row is a permutation: row g gives each passage of group g its storage position within the group.
All inputs are finite; a program needn't handle non-finite values.
Results may differ from a plain program's by a relative error of at most 0.0082.
Values may be sent and summed in bfloat16 or wider, within the bound.
No kernel may reach another device: no remote copies, remote signals or barrier semaphores. Data moves between devices by JAX's collectives and lax.ppermute only.
A program may use at most 128 MiB of HBM per device.

v0:
```python
import jax
import jax.numpy as jnp
from jax import lax
from jax.sharding import PartitionSpec as P

TAU = 0.0625
LOSS_SCALE = 32768.0
EPS = 1e-06


def normalize(hidden, weight):
    projected = jnp.dot(hidden, weight, preferred_element_type=jnp.float32)
    inverse = lax.rsqrt(jnp.sum(projected * projected, axis=-1, keepdims=True) + EPS)
    return (projected * inverse, inverse)


def unnormalize(upstream, unit_rows, inverse):
    radial = jnp.sum(unit_rows * upstream, axis=-1, keepdims=True)
    return ((upstream - unit_rows * radial) * inverse).astype(jnp.bfloat16)


def soft_scores(queries, passages, valid_mask):
    similar = jnp.einsum("rik,rjk->rij", queries, passages, preferred_element_type=jnp.float32)
    exponent = jnp.exp(similar / TAU) * valid_mask[:, None, :].astype(jnp.float32)
    denominator = jnp.sum(exponent, axis=-1)
    return (TAU * jnp.sum(jnp.log(denominator), axis=-1), exponent / denominator[:, :, None])


def distill(scores, teacher):
    teach_log = teacher - jnp.log(jnp.sum(jnp.exp(teacher), axis=-1, keepdims=True))
    student_log = scores - jnp.log(jnp.sum(jnp.exp(scores), axis=-1, keepdims=True))
    teach_prob = jnp.exp(teach_log)
    query_loss = jnp.sum(teach_prob * (teach_log - student_log), axis=-1)
    return (query_loss, LOSS_SCALE * (jnp.exp(student_log) - teach_prob))


def on_device(query_hidden, passage_hidden, head_weight, teacher, candidates, storage, lengths):
    dev_count = lax.axis_size("dev")
    stored_count, passage_len, hidden_width = passage_hidden.shape
    query_count, query_len, _ = query_hidden.shape
    per_query = candidates.shape[1]
    embed_dim = head_weight.shape[1]
    requests = query_count * per_query
    capacity = max(2, 3 * requests // dev_count)
    slots_all = dev_count * capacity
    stored_len = lengths[0]
    position = jnp.take(storage[0], candidates.reshape(-1))
    owner_dev = position // stored_count
    slot_index = position % stored_count
    request_order = jnp.arange(requests, dtype=jnp.int32)
    query_of = request_order // per_query
    before = (owner_dev[:, None] == owner_dev[None, :]) & (
        request_order[None, :] < request_order[:, None]
    )
    rank_within = jnp.sum(before.astype(jnp.int32), axis=1)
    target = owner_dev * capacity + rank_within
    coded = slot_index + stored_count * query_of
    send_ids = (
        jnp.full((slots_all,), -1, jnp.int32).at[target].set(coded).reshape(dev_count, capacity)
    )
    wanted_code = lax.all_to_all(send_ids, "dev", split_axis=0, concat_axis=0, tiled=True).reshape(
        slots_all
    )
    empty_slot = wanted_code < 0
    taken = jnp.maximum(wanted_code, 0) % stored_count
    wanted = jnp.where(empty_slot, -1, taken)
    flat_hidden = passage_hidden.reshape(stored_count * passage_len, hidden_width)
    pass_unit, pass_inverse = normalize(flat_hidden, head_weight)
    encoded = pass_unit.astype(jnp.bfloat16).reshape(stored_count, passage_len, embed_dim)
    query_flat = query_hidden.reshape(query_count * query_len, hidden_width)
    query_unit, query_inverse = normalize(query_flat, head_weight)
    query_enc = query_unit.astype(jnp.bfloat16).reshape(query_count, query_len, embed_dim)
    token_steps = jnp.arange(passage_len, dtype=jnp.int32)
    onehot = (jnp.arange(stored_count, dtype=jnp.int32)[:, None] == wanted[None, :]).astype(
        jnp.bfloat16
    )
    query_copies = jnp.repeat(query_enc, per_query, axis=0)
    outgoing = jnp.take(encoded, taken, axis=0).reshape(dev_count, capacity, passage_len, embed_dim)
    arrived = lax.all_to_all(outgoing, "dev", split_axis=0, concat_axis=0, tiled=True).reshape(
        slots_all, passage_len, embed_dim
    )
    cand_embed = jnp.take(arrived, target, axis=0)
    req_valid = token_steps[None, :] < jnp.take(stored_len, position)[:, None]
    scores, weights = soft_scores(query_copies, cand_embed, req_valid)
    query_loss, score_pull = distill(scores.reshape(query_count, per_query), teacher)
    mixed = (score_pull.reshape(-1)[:, None, None] * weights).astype(jnp.bfloat16)
    cand_delta = jnp.einsum(
        "rij,rik->rjk", mixed, query_copies, preferred_element_type=jnp.float32
    ).astype(jnp.bfloat16)
    query_terms = jnp.einsum("rij,rjk->rik", mixed, cand_embed, preferred_element_type=jnp.float32)
    query_delta = jnp.sum(query_terms.reshape(query_count, per_query, query_len, embed_dim), axis=1)
    grad_buffer = (
        jnp.zeros((slots_all, passage_len, embed_dim), jnp.bfloat16).at[target].set(cand_delta)
    )
    received = lax.all_to_all(
        grad_buffer.reshape(dev_count, capacity, passage_len, embed_dim),
        "dev",
        split_axis=0,
        concat_axis=0,
        tiled=True,
    ).reshape(slots_all, passage_len, embed_dim)
    stored_delta = jnp.dot(
        onehot,
        received.reshape(slots_all, passage_len * embed_dim),
        preferred_element_type=jnp.float32,
    )
    stored_preact = unnormalize(
        stored_delta.reshape(stored_count * passage_len, embed_dim), pass_unit, pass_inverse
    )
    query_preact = unnormalize(
        query_delta.reshape(query_count * query_len, embed_dim), query_unit, query_inverse
    )
    transposed = (((1,), (1,)), ((), ()))
    contraction = (((0,), (0,)), ((), ()))
    passage_grad = lax.dot_general(
        stored_preact, head_weight, transposed, preferred_element_type=jnp.float32
    )
    query_grad = lax.dot_general(
        query_preact, head_weight, transposed, preferred_element_type=jnp.float32
    )
    local_head = lax.dot_general(
        flat_hidden, stored_preact, contraction, preferred_element_type=jnp.float32
    )
    local_head = local_head + lax.dot_general(
        query_flat, query_preact, contraction, preferred_element_type=jnp.float32
    )
    head_grad = lax.psum(local_head, ("group", "dev"))
    return (
        query_loss,
        head_grad,
        query_grad.astype(jnp.bfloat16).reshape(query_count, query_len, hidden_width),
        passage_grad.astype(jnp.bfloat16).reshape(stored_count, passage_len, hidden_width),
    )


def solution(mesh):
    return jax.shard_map(
        on_device,
        mesh=mesh,
        in_specs=(
            P(("group", "dev"), None, None),
            P(("group", "dev"), None, None),
            P(),
            P(("group", "dev"), None),
            P(("group", "dev"), None),
            P("group", None),
            P("group", None),
        ),
        out_specs=(
            P(("group", "dev")),
            P(),
            P(("group", "dev"), None, None),
            P(("group", "dev"), None, None),
        ),
        check_vma=False,
    )
```

profile of v0, /device:TPU:1, one launch (start us, length us, event | category | flops | bytes accessed | tf_op | source)
XLA Modules:
  0.0 382.1 jit_solution(12745543098865975046)
XLA Ops:
  14.3 8.6 %all-to-all-start = ((s32[32,1,12]{2,1,0:T(1,128)}), s32[32,1,12]{2,1,0:T(1,128)S(1)}, u32[]{:S(2)}, u32[]{:S(2)}) async-start(s32[32,1,12]{2,1,0:T(1,128)} %bitcast.4), calls=%async_computation | async-start | bytes 32768 | tf_op jit(solution)/shard_map/all_to_all | solution.py:61
  22.9 5.3 %multiply_reduce_fusion.1 = (f32[6144]{0:T(1024)S(1)}, f32[6144,128]{1,0:T(8,128)S(1)}) fusion(bf16[6144,768]{1,0:T(8,128)(2,1)} %bitcast.51, bf16[768,128]{1,0:T(8,128)(2,1)S(1)} %copy-done), kind=kOutput, calls=%fused_computation.13 | convolution fusion | flops 1209526272 | bytes 12804096 | tf_op jit(solution)/shard_map/dot_general | solution.py:12
  28.2 1.9 multiply_convert_fusion.1
  30.4 4.8 %gather_fusion = bf16[384,48,128]{2,1,0:T(8,128)(2,1)} fusion(bf16[128,48,128]{2,1,0:T(8,128)(2,1)} %bitcast.54, s32[1024]{0:T(1024)S(1)} %pad_clamp_fusion.2), kind=kCustom, calls=%fused_computation.2 | custom fusion | bytes 9438720 | tf_op jit(solution)/shard_map/jit(_take)/gather | solution.py:78
  35.1 5.6 %broadcast_select_fusion = bf16[32,12,48,128]{3,2,1,0:T(8,128)(2,1)} fusion(bf16[32,12,48,128]{3,2,1,0:T(8,128)(2,1)} %bitcast.56, pred[32,12]{1,0:T(8,128)(4,1)S(1)} %compare_and_fusion), kind=kLoop, calls=%fused_computation.10 | loop fusion | flops 2359296 | bytes 9437568 | tf_op jit(solution)/shard_map/jit(_take)/select_n | solution.py:78
  40.8 7.6 %all-to-all-start.1 = ((bf16[32,12,48,128]{3,2,1,0:T(8,128)(2,1)}), bf16[32,12,48,128]{3,2,1,0:T(8,128)(2,1)}, u32[]{:S(2)}, u32[]{:S(2)}) async-start(bf16[32,12,48,128]{3,2,1,0:T(8,128)(2,1)} %broadcast_select_fusion), calls=%async_computation.1 | async-start | bytes 9437184 | tf_op jit(solution)/shard_map/all_to_all | solution.py:79
  51.3 52.9 %all-to-all-done.1 = bf16[32,12,48,128]{3,2,1,0:T(8,128)(2,1)} async-done(((bf16[32,12,48,128]{3,2,1,0:T(8,128)(2,1)}), bf16[32,12,48,128]{3,2,1,0:T(8,128)(2,1)}, u32[]{:S(2)}, u32[]{:S(2)}) %all-to-all-start.1) | async-done | bytes 4718624 | tf_op jit(solution)/shard_map/all_to_all | solution.py:79
  104.1 4.3 %gather_fusion.1 = bf16[128,48,128]{2,1,0:T(8,128)(2,1)} fusion(bf16[384,48,128]{2,1,0:T(8,128)(2,1)} %bitcast.9, s32[1024]{0:T(1024)S(1)} %pad_clamp_fusion.1), kind=kCustom, calls=%fused_computation.3 | custom fusion | bytes 3146240 | tf_op jit(solution)/shard_map/jit(_take)/gather | solution.py:82
  109.5 3.8 fusion.3
  115.0 2.3 multiply_convert_fusion.2
  118.3 1.8 convolution_convert_fusion.1
  120.1 2.8 broadcast_in_dim.64
  122.9 17.4 %scatter_fusion = bf16[384,48,128]{2,1,0:T(8,128)(2,1)} fusion(bf16[384,48,128]{2,1,0:T(8,128)(2,1)} %broadcast_in_dim.64, s32[128]{0:T(128)S(1)} %get-tuple-element.24, bf16[128,48,128]{2,1,0:T(8,128)(2,1)} %convolution_convert_fusion.1), kind=kCustom, calls=%fused_computation.5 | custom fusion | bytes 4719104 | tf_op jit(solution)/shard_map/scatter | solution.py:93
  140.3 8.8 %all-to-all-start.2 = ((bf16[32,12,48,128]{3,2,1,0:T(8,128)(2,1)}), bf16[32,12,48,128]{3,2,1,0:T(8,128)(2,1)}, u32[]{:S(2)}, u32[]{:S(2)}) async-start(bf16[32,12,48,128]{3,2,1,0:T(8,128)(2,1)} %bitcast.53), calls=%async_computation.2 | async-start | bytes 9437184 | tf_op jit(solution)/shard_map/all_to_all | solution.py:95
  149.7 2.4 bitcast_reduce_fusion
  153.2 51.8 %all-to-all-done.2 = bf16[32,12,48,128]{3,2,1,0:T(8,128)(2,1)} async-done(((bf16[32,12,48,128]{3,2,1,0:T(8,128)(2,1)}), bf16[32,12,48,128]{3,2,1,0:T(8,128)(2,1)}, u32[]{:S(2)}, u32[]{:S(2)}) %all-to-all-start.2) | async-done | bytes 4718624 | tf_op jit(solution)/shard_map/all_to_all | solution.py:95
  205.0 5.0 %fusion = f32[128,6144]{1,0:T(8,128)} fusion(bf16[48,8,48,128]{3,2,1,0:T(8,128)(2,1)} %bitcast.19, s32[384]{0:T(512)S(1)} %fusion.13), kind=kOutput, calls=%fused_computation.7 | convolution fusion | flops 604028928 | bytes 7865856 | tf_op jit(solution)/shard_map/dot_general | solution.py:102
  210.0 4.3 %reshape.199 = f32[6144,128]{1,0:T(8,128)} reshape(f32[128,6144]{1,0:T(8,128)} %fusion) | data formatting | bytes 6291456 | tf_op jit(solution)/shard_map/reshape | solution.py:108
  214.2 3.4 multiply_reduce_fusion
  217.6 3.5 multiply_convert_fusion
  221.2 5.7 %fusion.22 = f32[128,768]{1,0:T(8,128)S(1)} fusion(bf16[6144,128]{1,0:T(8,128)(2,1)S(1)} %multiply_convert_fusion, bf16[6144,768]{1,0:T(8,128)(2,1)} %bitcast.52), kind=kOutput, calls=%fused_computation.84 | convolution fusion | flops 1207959552 | bytes 11403264 | tf_op jit(solution)/shard_map/dot_general | solution.py:121
  227.9 7.8 %convolution_convert_fusion = bf16[6144,768]{1,0:T(8,128)(2,1)} fusion(bf16[6144,128]{1,0:T(8,128)(2,1)} %copy-done.2, bf16[768,128]{1,0:T(8,128)(2,1)S(1)} %copy-done), kind=kOutput, calls=%fused_computation.6 | convolution fusion | flops 1212678144 | bytes 11206656 | tf_op jit(solution)/shard_map/dot_general | solution.py:115
  235.7 137.6 %all-reduce.2.cloned.1.call-done = f32[768,128]{0,1:T(8,128)} async-done(((f32[768,128]{0,1:T(8,128)}), f32[768,128]{0,1:T(8,128)}) %all-reduce.2.cloned.1.call-update) | async-done | bytes 393232 | tf_op jit(solution)/shard_map/psum | solution.py:127
  373.3 1.9 copy.16
  (72 shorter events, 16.7 us)
Async XLA Ops:
  7.2 15.7 %copy-start = (bf16[768,128]{1,0:T(8,128)(2,1)S(1)}, bf16[768,128]{1,0:T(8,128)(2,1)}, u32[]{:S(2)}) copy-start(bf16[768,128]{1,0:T(8,128)(2,1)} %param.11) | copy-start | bytes 589828
  14.3 15.8 %all-to-all-start = ((s32[32,1,12]{2,1,0:T(1,128)}), s32[32,1,12]{2,1,0:T(1,128)S(1)}, u32[]{:S(2)}, u32[]{:S(2)}) async-start(s32[32,1,12]{2,1,0:T(1,128)} %bitcast.4), calls=%async_computation | async-start | bytes 32768 | tf_op jit(solution)/shard_map/all_to_all | solution.py:61
  40.8 7.6 %copy-start.10 = (f32[2,64]{1,0:T(2,128)S(1)}, f32[2,64]{1,0:T(2,128)}, u32[]{:S(2)}) copy-start(f32[2,64]{1,0:T(2,128)} %param.12) | copy-start | bytes 1540
  40.8 8.2 %copy-start.6 = (bf16[2,32,768]{2,1,0:T(8,128)(2,1)S(1)}, bf16[2,32,768]{2,1,0:T(8,128)(2,1)}, u32[]{:S(2)}) copy-start(bf16[2,32,768]{2,1,0:T(8,128)(2,1)} %param.9) | copy-start | bytes 294916
  40.8 63.4 %all-to-all-start.1 = ((bf16[32,12,48,128]{3,2,1,0:T(8,128)(2,1)}), bf16[32,12,48,128]{3,2,1,0:T(8,128)(2,1)}, u32[]{:S(2)}, u32[]{:S(2)}) async-start(bf16[32,12,48,128]{3,2,1,0:T(8,128)(2,1)} %broadcast_select_fusion), calls=%async_computation.1 | async-start | bytes 9437184 | tf_op jit(solution)/shard_map/all_to_all | solution.py:79
  49.3 0.5 copy-start.8
  108.4 5.9 %copy-start.11 = (f32[2,64]{1,0:T(2,128)S(1)}, f32[2,64]{1,0:T(2,128)}, u32[]{:S(2)}) copy-start(f32[2,64]{1,0:T(2,128)} %param.12) | copy-start | bytes 1540
  108.5 1.0 copy-start.4
  108.5 5.7 %copy-start.12 = (f32[2]{0:T(128)S(1)}, f32[2]{0:T(128)}, u32[]{:S(2)}) copy-start(f32[2]{0:T(128)} %log.19) | copy-start | bytes 28
  113.3 0.6 copy-start.7
  115.0 3.3 copy-start.5
  117.3 1.0 copy-start.3
  140.3 9.4 %copy-start.13 = (pred[128]{0:T(512)(128)(4,1)S(1)}, pred[128]{0:T(512)(128)(4,1)}, u32[]{:S(2)}) copy-start(pred[128]{0:T(512)(128)(4,1)} %get-tuple-element.23) | copy-start | bytes 388
  140.3 64.7 %all-to-all-start.2 = ((bf16[32,12,48,128]{3,2,1,0:T(8,128)(2,1)}), bf16[32,12,48,128]{3,2,1,0:T(8,128)(2,1)}, u32[]{:S(2)}, u32[]{:S(2)}) async-start(bf16[32,12,48,128]{3,2,1,0:T(8,128)(2,1)} %bitcast.53), calls=%async_computation.2 | async-start | bytes 9437184 | tf_op jit(solution)/shard_map/all_to_all | solution.py:95
  149.1 2.9 copy-start.9
  149.1 224.2 %all-reduce.2.cloned.1.call-start = ((), (), s32[]{:S(2)}) async-start(), calls=%async_computation.3 | async-start | bytes 786432 | tf_op jit(solution)/shard_map/psum | solution.py:127
  214.2 3.4 copy-start.1
  221.2 5.8 %copy-start.2 = (bf16[6144,128]{1,0:T(8,128)(2,1)}, bf16[6144,128]{1,0:T(8,128)(2,1)S(1)}, u32[]{:S(2)}) copy-start(bf16[6144,128]{1,0:T(8,128)(2,1)S(1)} %multiply_convert_fusion) | copy-start | bytes 4718596
Sparse Core Ops, SparseCore 0:
  228.1 145.2 all-reduce.1
where the time goes:
time: 383 us; the launch traced here: 382 us
  waiting for transfers between devices  242 us (63%)
  local copies, waits for them, and re-layouts  45.4 us (12%)
  matrix products  33.8 us (9%)
  starting transfers between devices  25.2 us (7%)
  other arithmetic  21 us (5%)
  between operations  14.3 us (4%)
    psum x1, waiting for transfers between devices, on_device(): head_grad = lax.psum(local_head, ('group', 'dev'))  138 us
    all_to_all x1, waiting for transfers between devices, on_device(): lax.all_to_all(outgoing, 'dev', split_axis=0, concat_axis=0, tiled=True)  52.9 us
    all_to_all x1, waiting for transfers between devices, on_device(): lax.all_to_all(grad_buffer.reshape(dev_count, capacity, passage_len, embe...  51.8 us
    scatter x1, local copies, waits for them, and re-layouts, on_device(): jnp.zeros((slots_all, passage_len, embed_dim), jnp.bfloat16).at[target]  17.4 us
    all_to_all x1, starting transfers between devices, on_device(): lax.all_to_all(grad_buffer.reshape(dev_count, capacity, passage_len, embe...  8.84 us
    all_to_all x1, starting transfers between devices, on_device(): lax.all_to_all(send_ids, 'dev', split_axis=0, concat_axis=0, tiled=True)  8.59 us
    dot_general x1, matrix products, on_device(): lax.dot_general(stored_preact, head_weight, transposed, preferred_element...  7.77 us
  transfers between devices with their start and end apart: 4, of which 3 were waited for; matrix products, arithmetic and copies ran while one was open for 6% of the time, Pallas kernels for 0%

commit v1 on v0

v1 whole, which is shorter than its diff:
```python
import jax
import jax.numpy as jnp
from jax import lax
from jax.experimental import pallas as pl
from jax.experimental.pallas import tpu as pltpu
from jax.sharding import PartitionSpec as P

TAU = 0.0625
LOSS_SCALE = 32768.0
EPS = 1e-06

N_DEV = 32
N_ALL = 128
STORED = 128
PLEN = 48
QLEN = 32
D = 768
DIM = 128
PER_QUERY = 64
CAP = 12
SLOTS = 16
WIDE = CAP * PLEN
QROWS = 2 * QLEN
META = 16
CHUNK = 4
BLOCK = 768
STEPS = STORED * PLEN // BLOCK
HEAD_TILES = D // 8

BF = jnp.bfloat16
F32 = jnp.float32
ROWS_ROWS = (((0,), (0,)), ((), ()))
COLS_COLS = (((1,), (1,)), ((), ()))
VMEM = pl.BlockSpec(memory_space=pltpu.VMEM)
SMEM = pl.BlockSpec(memory_space=pltpu.SMEM)


def params():
    return pltpu.CompilerParams(vmem_limit_bytes=50 * 1024 * 1024)


def dot(a, b, dims=(((1,), (0,)), ((), ()))):
    return lax.dot_general(a, b, dims, preferred_element_type=F32)


def iota(shape, axis):
    return lax.broadcasted_iota(jnp.int32, shape, axis)


def split3(x):
    hi = x.astype(BF).astype(F32)
    mid = (x - hi).astype(BF).astype(F32)
    return hi, mid, (x - hi - mid)


def expander(copies):
    row = iota((DIM, WIDE), 0)
    slot = (row & (SLOTS - 1)) * PLEN
    lane = iota((DIM, WIDE), 1)
    hit = (lane >= slot) & (lane < slot + PLEN) & (row < copies * SLOTS)
    return jnp.where(hit, 1.0, 0.0)


def request_kernel(hidden_ref, weight_ref, teacher_ref, cand_ref, storage_ref, lengths_ref,
                   send_ref, proj_ref, const_ref, place_ref, length_ref):
    for i in range(N_DEV):
        place_ref[i : i + 1, :] = storage_ref[0:1, i * STORED : (i + 1) * STORED]
        length_ref[i : i + 1, :] = lengths_ref[0:1, i * STORED : (i + 1) * STORED]
    proj = dot(hidden_ref[...], weight_ref[...])
    proj_ref[...] = proj
    inverse = lax.rsqrt(jnp.sum(proj * proj, axis=-1, keepdims=True) + EPS)
    embed = (proj * inverse).astype(BF)

    teacher = teacher_ref[...]
    log_t = teacher - jnp.log(jnp.sum(jnp.exp(teacher), axis=-1, keepdims=True))
    prob = jnp.exp(log_t)
    const = jnp.sum(prob * log_t, axis=-1, keepdims=True)
    const_ref[...] = jnp.concatenate(
        [jnp.broadcast_to(const, (2, DIM)), jnp.zeros((6, DIM), F32)], axis=0
    )
    prob_row = jnp.concatenate([prob[0:1], prob[1:2]], axis=1)
    cand = cand_ref[...]
    cand_row = jnp.concatenate([cand[0:1], cand[1:2]], axis=1)

    place = place_ref[...]
    owner_table = (place >> 7).astype(F32).astype(BF)
    slot_table = (place & (STORED - 1)).astype(F32).astype(BF)
    length_table = length_ref[...].astype(F32).astype(BF)
    sub32 = iota((N_DEV, DIM), 0)
    sub128 = iota((DIM, DIM), 0)
    lane128 = iota((DIM, DIM), 1)
    high = jnp.where(sub32 == (cand_row >> 7), 1.0, 0.0).astype(BF)
    low = sub128 == (cand_row & (STORED - 1))
    owner = jnp.sum(jnp.where(low, dot(owner_table, high, ROWS_ROWS), 0.0), axis=0, keepdims=True)
    slot = jnp.sum(jnp.where(low, dot(slot_table, high, ROWS_ROWS), 0.0), axis=0, keepdims=True)
    match = jnp.where(sub32 == owner.astype(jnp.int32), 1.0, 0.0)
    match_bf = match.astype(BF)
    at_slot = sub128 == slot.astype(jnp.int32)
    length = jnp.sum(
        jnp.where(at_slot, dot(length_table, match_bf, ROWS_ROWS), 0.0), axis=0, keepdims=True
    )
    earlier = jnp.where(sub128 < lane128, 1.0, 0.0).astype(BF)
    rank = jnp.sum(match * dot(match_bf, earlier), axis=0, keepdims=True).astype(jnp.int32)
    t_hi, t_mid, t_lo = split3(prob_row)
    which = jnp.where(iota((1, DIM), 1) >= PER_QUERY, 1.0, 0.0)
    fields = (slot, which, length, t_hi, t_mid, t_lo, jnp.ones((1, DIM), F32))
    field_of = sub128 >> 4
    values = jnp.zeros((DIM, DIM), F32)
    for f, row in enumerate(fields):
        values = jnp.where(field_of == f, row, values)
    values = jnp.where((sub128 & (SLOTS - 1)) == rank, values, 0.0).astype(BF)
    meta = dot(match_bf, values, COLS_COLS)
    for s in range(N_DEV):
        send_ref[s, 0:QROWS, :] = embed
        send_ref[s, QROWS : QROWS + META, :] = jnp.broadcast_to(meta[s : s + 1], (META, DIM)).astype(BF)


def encode_kernel(hidden_ref, weight_ref, proj_ref, embed_ref):
    proj = dot(hidden_ref[...], weight_ref[...])
    proj_ref[...] = proj
    inverse = lax.rsqrt(jnp.sum(proj * proj, axis=-1, keepdims=True) + EPS)
    embed_ref[...] = (proj * inverse).astype(BF)


def stored_rows(embed_ref, place_ref, s):
    parts = []
    for k in range(CAP):
        start = pl.multiple_of(place_ref[s, k], 16)
        parts.append(embed_ref[pl.ds(start, PLEN), :])
    return jnp.concatenate(parts, axis=0)


def score_kernel(recv_ref, embed_ref, expo_ref, recip_ref, sums_ref, table_ref, second_ref, place_ref,
                 meta_ref, limit_ref, smem_ref, sem):
    for s in range(N_DEV):
        rows = recv_ref[s, QROWS : QROWS + META, :].astype(F32)
        meta_ref[s : s + 1, :] = rows[0:1, :]
    meta = meta_ref[...]
    place_ref[...] = meta.astype(jnp.int32) * PLEN
    copy = pltpu.make_async_copy(place_ref, smem_ref, sem)
    copy.start()
    meta_bf = meta.astype(BF)
    spread = expander(1)
    second_ref[...] = dot(pltpu.roll(meta, DIM - SLOTS, 1).astype(BF), spread.astype(BF))
    length = dot(pltpu.roll(meta, DIM - 2 * SLOTS, 1).astype(BF), spread.astype(BF))
    lane = iota((1, WIDE), 1)
    token = lane
    for k in range(1, CAP):
        token = token - jnp.where(lane >= k * PLEN, PLEN, 0)
    limit_ref[...] = jnp.where(token.astype(F32) < length, 1.0, 0.0)
    copy.wait()

    def chunk(i, carry):
        for u in range(CHUNK):
            s = i * CHUNK + u
            queries = recv_ref[s, 0:QROWS, :]
            sims = dot(queries, stored_rows(embed_ref, smem_ref, s), COLS_COLS)
            second = second_ref[pl.ds(s, 1), :]
            valid = limit_ref[pl.ds(s, 1), :]
            mine = jnp.where(second > 0.5, sims[QLEN:QROWS], sims[0:QLEN])
            expo = jnp.where(valid > 0.5, jnp.exp(mine * (1.0 / TAU)), 0.0)
            expo_ref[pl.ds(pl.multiple_of(s * QLEN, QLEN), QLEN), :] = expo.astype(BF)
        return carry

    lax.fori_loop(0, N_DEV // CHUNK, chunk, 0)
    total = dot(expo_ref[...], spread.astype(BF), COLS_COLS)
    total = jnp.where(total > 0.0, total, 1.0)
    recip_ref[...] = 1.0 / total
    scores = TAU * jnp.sum(jnp.log(total).reshape(N_DEV, QLEN, DIM), axis=1)
    lane = iota((N_DEV, DIM), 1)
    present = (pltpu.roll(meta, DIM - 6 * SLOTS, 1) > 0.5) & (lane < SLOTS)
    teach = (
        pltpu.roll(meta, DIM - 3 * SLOTS, 1)
        + pltpu.roll(meta, DIM - 4 * SLOTS, 1)
        + pltpu.roll(meta, DIM - 5 * SLOTS, 1)
    )
    teach = jnp.where(present, teach, 0.0)
    student = jnp.where(present, jnp.exp(scores), 0.0)
    which = pltpu.roll(meta, DIM - SLOTS, 1) > 0.5
    table_ref[0] = student
    table_ref[1] = teach
    table_ref[2] = jnp.where(which, 1.0, 0.0)
    gain = teach * scores
    columns = []
    for value in (student, gain):
        columns.append(jnp.sum(jnp.where(which, 0.0, value), axis=-1, keepdims=True))
        columns.append(jnp.sum(jnp.where(which, value, 0.0), axis=-1, keepdims=True))
    mixed = jnp.zeros((N_DEV, DIM), F32)
    for j, column in enumerate(columns):
        mixed = jnp.where(lane == j, column, mixed)
    mixed = jnp.concatenate([mixed, jnp.zeros((DIM - N_DEV, DIM), F32)], axis=0)
    part = jnp.transpose(mixed)[0:8, :]
    for s in range(N_DEV):
        sums_ref[s] = part


def query_kernel(sums_ref, const_ref, me_ref, table_ref, second_ref, expo_ref, recip_ref, embed_ref, place_ref,
                 send_ref, mixed_ref, loss_ref, pull_ref):
    sums = jnp.sum(sums_ref[...], axis=0)
    log_sum = jnp.log(jnp.where(sums > 0.0, sums, 1.0))
    loss = const_ref[0:2, :] + log_sum[0:2, :] - sums[2:4, :]
    picked = jnp.where(iota((2, DIM), 1) == me_ref[0], loss, 0.0)
    loss_ref[...] = jnp.broadcast_to(jnp.sum(picked, axis=-1, keepdims=True), (2, DIM))
    turned = jnp.transpose(jnp.concatenate([sums, jnp.zeros((DIM - 8, DIM), F32)], axis=0))[0:N_DEV, :]
    normal = jnp.where(table_ref[2] > 0.5, turned[:, 1:2], turned[:, 0:1])
    pull_ref[...] = LOSS_SCALE * (table_ref[0] / normal - table_ref[1])
    spread = expander(2).astype(BF)
    lane = iota((QLEN, DIM), 1)

    def chunk(i, carry):
        scaled = []
        for u in range(CHUNK):
            s = i * CHUNK + u
            rows = pl.ds(pl.multiple_of(s * QLEN, QLEN), QLEN)
            factor = recip_ref[rows, :] * pull_ref[pl.ds(s, 1), :]
            hi = factor.astype(BF).astype(F32)
            lo = factor - hi
            scaled.append(jnp.where(lane < SLOTS, hi, pltpu.roll(lo, SLOTS, 1)).astype(BF))
        wide = dot(jnp.concatenate(scaled, axis=0), spread)
        rows = pl.ds(pl.multiple_of(i * (CHUNK * QLEN), CHUNK * QLEN), CHUNK * QLEN)
        mixed = expo_ref[rows, :].astype(F32) * wide
        mixed_ref[rows, :] = mixed.astype(BF)
        for u in range(CHUNK):
            s = i * CHUNK + u
            one = mixed[u * QLEN : (u + 1) * QLEN]
            second = second_ref[pl.ds(s, 1), :] > 0.5
            both = jnp.concatenate(
                [jnp.where(second, 0.0, one).astype(BF), jnp.where(second, one, 0.0).astype(BF)], axis=0
            )
            send_ref[s] = dot(both, stored_rows(embed_ref, place_ref, s)).astype(BF)
        return carry

    lax.fori_loop(0, N_DEV // CHUNK, chunk, 0)


def stored_kernel(place_ref, hidden_ref, proj_ref, weight_ref, recv_ref, mixed_ref, second_ref,
                  grad_ref, head_ref, delta_ref, acc_ref):
    step = pl.program_id(0)

    @pl.when(step == 0)
    def _():
        delta_ref[...] = jnp.zeros_like(delta_ref)
        acc_ref[...] = jnp.zeros_like(acc_ref)

        def chunk(i, carry):
            for u in range(CHUNK):
                s = i * CHUNK + u
                one = mixed_ref[pl.ds(pl.multiple_of(s * QLEN, QLEN), QLEN), :].astype(F32)
                second = second_ref[pl.ds(s, 1), :] > 0.5
                both = jnp.concatenate(
                    [jnp.where(second, 0.0, one).astype(BF), jnp.where(second, one, 0.0).astype(BF)], axis=0
                )
                part = dot(both, recv_ref[s, 0:QROWS, :], ROWS_ROWS)
                for k in range(CAP):
                    at = pl.ds(pl.multiple_of(place_ref[s, k], 16), PLEN)
                    delta_ref[at, :] += part[k * PLEN : (k + 1) * PLEN]
            return carry

        lax.fori_loop(0, N_DEV // CHUNK, chunk, 0)

    proj = proj_ref[...]
    delta = delta_ref[pl.ds(pl.multiple_of(step * BLOCK, BLOCK), BLOCK), :]
    inverse = lax.rsqrt(jnp.sum(proj * proj, axis=-1, keepdims=True) + EPS)
    unit = proj * inverse
    radial = jnp.sum(unit * delta, axis=-1, keepdims=True)
    preact = ((delta - unit * radial) * inverse).astype(BF)
    grad_ref[...] = dot(preact, weight_ref[...], COLS_COLS).astype(BF)
    acc_ref[...] += dot(preact, hidden_ref[...], ROWS_ROWS)

    @pl.when(step == STEPS - 1)
    def _():
        head_ref[...] = jnp.transpose(acc_ref[...])


def finish_kernel(recv_ref, hidden_ref, weight_ref, proj_ref, head_ref, grad_ref, send_ref):
    delta = jnp.sum(recv_ref[...].astype(F32), axis=0)
    proj = proj_ref[...]
    inverse = lax.rsqrt(jnp.sum(proj * proj, axis=-1, keepdims=True) + EPS)
    unit = proj * inverse
    radial = jnp.sum(unit * delta, axis=-1, keepdims=True)
    preact = ((delta - unit * radial) * inverse).astype(BF)
    grad_ref[...] = dot(preact, weight_ref[...], COLS_COLS).astype(BF)
    head = head_ref[...] + dot(hidden_ref[...], preact, ROWS_ROWS)
    send_ref[0:HEAD_TILES] = head.reshape(HEAD_TILES, 8, DIM).astype(BF)
    send_ref[HEAD_TILES:N_ALL] = jnp.zeros((N_ALL - HEAD_TILES, 8, DIM), BF)


def reduce_kernel(recv_ref, send_ref):
    total = jnp.sum(recv_ref[...].astype(F32), axis=0).astype(BF)
    send_ref[...] = jnp.broadcast_to(total[None], (N_ALL, 8, DIM))


def shape(dims, kind):
    return jax.ShapeDtypeStruct(dims, kind)


def exchange(x, axes):
    return lax.all_to_all(x, axes, split_axis=0, concat_axis=0, tiled=True)


def on_device(query_hidden, passage_hidden, head_weight, teacher, candidates, storage, lengths):
    query_flat = query_hidden.reshape(QROWS, D)
    flat_hidden = passage_hidden.reshape(STORED * PLEN, D)
    send, query_proj, const = pl.pallas_call(
        request_kernel,
        out_shape=(
            shape((N_DEV, QROWS + META, DIM), BF),
            shape((QROWS, DIM), F32),
            shape((8, DIM), F32),
        ),
        in_specs=[VMEM] * 6,
        out_specs=(VMEM,) * 3,
        scratch_shapes=[pltpu.VMEM((N_DEV, DIM), jnp.int32)] * 2,
        compiler_params=params(),
        name="request",
    )(query_flat, head_weight, teacher, candidates, storage, lengths)
    recv = exchange(send, "dev")

    proj, embed = pl.pallas_call(
        encode_kernel,
        grid=(STEPS,),
        out_shape=(shape((STORED * PLEN, DIM), F32), shape((STORED * PLEN, DIM), BF)),
        in_specs=[
            pl.BlockSpec((BLOCK, D), lambda i: (i, 0)),
            pl.BlockSpec((D, DIM), lambda i: (0, 0)),
        ],
        out_specs=(
            pl.BlockSpec((BLOCK, DIM), lambda i: (i, 0)),
            pl.BlockSpec((BLOCK, DIM), lambda i: (i, 0)),
        ),
        cost_estimate=pl.CostEstimate(flops=2 * 6144 * D * DIM, bytes_accessed=15_000_000, transcendentals=0),
        compiler_params=params(),
        name="encode",
    )(flat_hidden, head_weight)

    expo, recip, sums, table, second, place = pl.pallas_call(
        score_kernel,
        out_shape=(
            shape((N_DEV * QLEN, WIDE), BF),
            shape((N_DEV * QLEN, DIM), F32),
            shape((N_DEV, 8, DIM), F32),
            shape((3, N_DEV, DIM), F32),
            shape((N_DEV, WIDE), F32),
            shape((N_DEV, DIM), jnp.int32),
        ),
        in_specs=[VMEM] * 2,
        out_specs=(VMEM,) * 6,
        scratch_shapes=[
            pltpu.VMEM((N_DEV, DIM), F32),
            pltpu.VMEM((N_DEV, WIDE), F32),
            pltpu.SMEM((N_DEV, DIM), jnp.int32),
            pltpu.SemaphoreType.DMA,
        ],
        compiler_params=params(),
        name="score",
    )(recv, embed)
    all_sums = exchange(sums, "dev")

    me = lax.axis_index("dev").astype(jnp.int32).reshape(1)
    send_delta, mixed, loss = pl.pallas_call(
        query_kernel,
        out_shape=(
            shape((N_DEV, QROWS, DIM), BF),
            shape((N_DEV * QLEN, WIDE), BF),
            shape((2, DIM), F32),
        ),
        in_specs=[VMEM, VMEM, SMEM, VMEM, VMEM, VMEM, VMEM, VMEM, SMEM],
        out_specs=(VMEM,) * 3,
        scratch_shapes=[pltpu.VMEM((N_DEV, DIM), F32)],
        compiler_params=params(),
        name="query",
    )(all_sums, const, me, table, second, expo, recip, embed, place)
    recv_delta = exchange(send_delta, "dev")

    whole = lambda *dims: pl.BlockSpec(dims, lambda i: (0,) * len(dims))
    passage_grad, head = pl.pallas_call(
        stored_kernel,
        grid=(STEPS,),
        out_shape=(shape((STORED * PLEN, D), BF), shape((D, DIM), F32)),
        in_specs=[
            SMEM,
            pl.BlockSpec((BLOCK, D), lambda i: (i, 0)),
            pl.BlockSpec((BLOCK, DIM), lambda i: (i, 0)),
            whole(D, DIM),
            whole(N_DEV, QROWS + META, DIM),
            whole(N_DEV * QLEN, WIDE),
            whole(N_DEV, WIDE),
        ],
        out_specs=(pl.BlockSpec((BLOCK, D), lambda i: (i, 0)), whole(D, DIM)),
        scratch_shapes=[pltpu.VMEM((STORED * PLEN, DIM), F32), pltpu.VMEM((DIM, D), F32)],
        cost_estimate=pl.CostEstimate(flops=6 * 6144 * D * DIM, bytes_accessed=24_000_000, transcendentals=0),
        compiler_params=params(),
        name="stored",
    )(place, flat_hidden, proj, head_weight, recv, mixed, second)

    query_grad, send_head = pl.pallas_call(
        finish_kernel,
        out_shape=(shape((QROWS, D), BF), shape((N_ALL, 8, DIM), BF)),
        in_specs=[VMEM] * 5,
        out_specs=(VMEM,) * 2,
        compiler_params=params(),
        name="finish",
    )(recv_delta, query_flat, head_weight, query_proj, head)
    recv_head = exchange(send_head, ("group", "dev"))
    send_total = pl.pallas_call(
        reduce_kernel,
        out_shape=shape((N_ALL, 8, DIM), BF),
        in_specs=[VMEM],
        out_specs=VMEM,
        compiler_params=params(),
        name="reduce",
    )(recv_head)
    head_all = exchange(send_total, ("group", "dev"))
    head_grad = head_all[:HEAD_TILES].reshape(D, DIM).astype(F32)
    return (
        loss[:, 0],
        head_grad,
        query_grad.reshape(2, QLEN, D),
        passage_grad.reshape(STORED, PLEN, D),
    )


def solution(mesh):
    return jax.shard_map(
        on_device,
        mesh=mesh,
        in_specs=(
            P(("group", "dev"), None, None),
            P(("group", "dev"), None, None),
            P(),
            P(("group", "dev"), None),
            P(("group", "dev"), None),
            P("group", None),
            P("group", None),
        ),
        out_specs=(
            P(("group", "dev")),
            P(),
            P(("group", "dev"), None, None),
            P(("group", "dev"), None, None),
        ),
        check_vma=False,
    )
```

time: 383 us -> 125 us (0.33)
  waiting for transfers between devices: 242 us -> 19.9 us
  Pallas kernels: 0 us -> 40.9 us
  matrix products: 33.8 us -> 0 us
  local copies, waits for them, and re-layouts: 45.4 us -> 17.4 us
  blocking collectives: 0 us -> 21.4 us
  other arithmetic: 21 us -> 0.77 us
  between operations: 14.3 us -> 0.78 us
    psum x1 -> x0, waiting for transfers between devices: 138 us -> none  [on_device(): head_grad = lax.psum(local_head, ('group', 'dev'))]
    all_to_all x3 -> x4, waiting for transfers between devices: 105 us -> 19.9 us  [exchange(): return lax.all_to_all(x, axes, split_axis=0, concat_axis=0, tiled=True)]
    pallas_call x0 -> x7, Pallas kernels: none -> 40.9 us  [the longest x1 17 us: on_device(): pl.pallas_call(stored_kernel, grid=(STEPS,), out_shape=(shape((STORED * P...]
    dot_general x10 -> x0, matrix products: 33.8 us -> none  [the longest x1 7.77 us: on_device(): lax.dot_general(stored_preact, head_weight, transposed, preferred_element...]
    all_to_all x0 -> x1, blocking collectives: none -> 21.4 us  [exchange(): return lax.all_to_all(x, axes, split_axis=0, concat_axis=0, tiled=True)]
    scatter x2 -> x0, local copies, waits for them, and re-layouts: 18.3 us -> none  [the longest x1 17.4 us: on_device(): jnp.zeros((slots_all, passage_len, embed_dim), jnp.bfloat16).at[target]]
    gather x4 -> x0, local copies, waits for them, and re-layouts: 12.3 us -> none  [the longest x1 4.78 us: on_device(): jnp.take(encoded, taken, axis=0)]
    unnamed x29 -> x52, local copies, waits for them, and re-layouts: 5.07 us -> 16.7 us
  transfers between devices with their start and end apart: 4 -> 4, of which waited for: 3 -> 3; matrix products, arithmetic and copies ran while one was open for 6% -> 1% of each run, Pallas kernels for 0% -> 21%
where the time goes in v1:
time: 125 us; the launch traced here: 124 us
  Pallas kernels  40.9 us (33%)
  starting transfers between devices  22.4 us (18%)
  blocking collectives  21.4 us (17%)
  waiting for transfers between devices  19.9 us (16%)
  local copies, waits for them, and re-layouts  17.4 us (14%)
    all_to_all x4, starting transfers between devices, exchange(): return lax.all_to_all(x, axes, split_axis=0, concat_axis=0, tiled=True)  22.4 us
    all_to_all x1, blocking collectives, exchange(): return lax.all_to_all(x, axes, split_axis=0, concat_axis=0, tiled=True)  21.4 us
    all_to_all x4, waiting for transfers between devices, exchange(): return lax.all_to_all(x, axes, split_axis=0, concat_axis=0, tiled=True)  19.9 us
    pallas_call x1, Pallas kernels, on_device(): pl.pallas_call(stored_kernel, grid=(STEPS,), out_shape=(shape((STORED * P...  17 us
    unnamed x52, local copies, waits for them, and re-layouts  16.7 us
    pallas_call x1, Pallas kernels, on_device(): pl.pallas_call(encode_kernel, grid=(STEPS,), out_shape=(shape((STORED * P...  9.05 us
    pallas_call x1, Pallas kernels, on_device(): pl.pallas_call(score_kernel, out_shape=(shape((N_DEV * QLEN, WIDE), BF),...  6.35 us
    pallas_call x1, Pallas kernels, on_device(): pl.pallas_call(query_kernel, out_shape=(shape((N_DEV, QROWS, DIM), BF), s...  5.25 us
  transfers between devices with their start and end apart: 4, of which 3 were waited for; matrix products, arithmetic and copies ran while one was open for 1% of the time, Pallas kernels for 21%

profile of v1, /device:TPU:1, one launch (start us, length us, event | category | flops | bytes accessed | tf_op | source)
XLA Modules:
  0.0 123.5 jit_solution(10182053641914600610)
XLA Ops:
  0.6 0.9 copy-done.1
  1.6 0.9 copy-done.9
  5.2 1.4 %request.1 = (bf16[32,80,128]{2,1,0:T(8,128)(2,1)}, f32[64,128]{1,0:T(8,128)S(1)}, f32[8,128]{1,0:T(8,128)S(1)}) custom-call(bf16[64,768]{1,0:T(8,128)(2,1)S(1)} %bitcast.10, bf16[768,128]{1,0:T(8,128)(2,1)S(1)} %copy-done.1, f32[2,64]{1,0:T(2,128)S(1)} %copy-done.22, s32[2,64]{1,0:T(2,128)S(1)} %copy-done.23, s32[1,4096]{1,0:T(1,128)S(1)} %copy-done.18, ...), custom_call_target="tpu_custom_call" | custom-call | tf_op jit(solution)/shard_map/request/pallas_call | solution.py:304
  7.8 8.6 %all-to-all-start = ((bf16[32,80,128]{2,1,0:T(8,128)(2,1)}), bf16[32,80,128]{2,1,0:T(8,128)(2,1)S(1)}, u32[]{:S(2)}, u32[]{:S(2)}) async-start(bf16[32,80,128]{2,1,0:T(8,128)(2,1)} %get-tuple-element.22), calls=%async_computation | async-start | bytes 1310720 | tf_op jit(solution)/shard_map/all_to_all | solution.py:298
  16.4 0.9 copy-done.2
  17.3 9.1 %encode.1 = (f32[6144,128]{1,0:T(8,128)}, bf16[6144,128]{1,0:T(8,128)(2,1)S(1)}) custom-call(bf16[6144,768]{1,0:T(8,128)(2,1)} %bitcast.12, bf16[768,128]{1,0:T(8,128)(2,1)S(1)} %copy-done.2), custom_call_target="tpu_custom_call" | custom-call | flops 1207959552 | bytes 15000000 | tf_op jit(solution)/shard_map/encode/pallas_call | solution.py:319
  26.4 1.1 copy-done
  27.5 1.8 %all-to-all-done.recv_ref = bf16[32,80,128]{2,1,0:T(8,128)(2,1)S(1)} async-done(((bf16[32,80,128]{2,1,0:T(8,128)(2,1)}), bf16[32,80,128]{2,1,0:T(8,128)(2,1)S(1)}, u32[]{:S(2)}, u32[]{:S(2)}) %all-to-all-start) | async-done | bytes 655392 | tf_op jit(solution)/shard_map/all_to_all | solution.py:298
  29.3 6.4 %score.1 = (bf16[1024,576]{1,0:T(8,128)(2,1)S(1)}, f32[1024,128]{1,0:T(8,128)S(1)}, f32[32,8,128]{2,1,0:T(8,128)}, f32[3,32,128]{2,1,0:T(8,128)S(1)}, f32[32,576]{1,0:T(8,128)S(1)}, /*index=5*/s32[32,128]{1,0:T(8,128)S(1)}) custom-call(bf16[32,80,128]{2,1,0:T(8,128)(2,1)S(1)} %all-to-all-done.recv_ref, bf16[6144,128]{1,0:T(8,128)(2,1)} %copy-done), custom_call_target="tpu_custom_call" | custom-call | tf_op jit(solution)/shard_map/score/pallas_call | solution.py:336
  35.7 0.8 copy-done.4
  37.7 5.6 %all-to-all-start.1 = ((f32[32,8,128]{2,1,0:T(8,128)}), f32[32,8,128]{2,1,0:T(8,128)S(1)}, u32[]{:S(2)}, u32[]{:S(2)}) async-start(f32[32,8,128]{2,1,0:T(8,128)} %get-tuple-element.24), calls=%async_computation.1 | async-start | bytes 262144 | tf_op jit(solution)/shard_map/all_to_all | solution.py:298
  43.3 7.6 %all-to-all-done.1.sums_ref = f32[32,8,128]{2,1,0:T(8,128)S(1)} async-done(((f32[32,8,128]{2,1,0:T(8,128)}), f32[32,8,128]{2,1,0:T(8,128)S(1)}, u32[]{:S(2)}, u32[]{:S(2)}) %all-to-all-start.1) | async-done | bytes 131104 | tf_op jit(solution)/shard_map/all_to_all | solution.py:298
  51.6 1.0 copy-done.5
  52.6 0.9 copy-done.7
  54.2 0.8 copy-done.15
  55.7 5.3 %query.1 = (bf16[32,64,128]{2,1,0:T(8,128)(2,1)S(1)}, bf16[1024,576]{1,0:T(8,128)(2,1)S(1)}, f32[2,128]{1,0:T(2,128)S(1)}) custom-call(f32[32,8,128]{2,1,0:T(8,128)S(1)} %copy-done.7, f32[8,128]{1,0:T(8,128)S(1)} %copy-done.21, s32[1]{0:T(128)} %bitcast.2.me_ref, f32[3,32,128]{2,1,0:T(8,128)S(1)} %copy-done.15, f32[32,576]{1,0:T(8,128)S(1)} %get-tuple-element.27.second_ref, ...), custom_call_target="tpu_custom_call" | custom-call | tf_op jit(solution)/shard_map/query/pallas_call | solution.py:360
  61.0 0.8 copy-done.8
  62.3 3.9 %all-to-all-start.2 = ((bf16[32,64,128]{2,1,0:T(8,128)(2,1)}), bf16[32,64,128]{2,1,0:T(8,128)(2,1)S(1)}, u32[]{:S(2)}, u32[]{:S(2)}) async-start(bf16[32,64,128]{2,1,0:T(8,128)(2,1)} %copy-done.8), calls=%async_computation.2 | async-start | bytes 1048576 | tf_op jit(solution)/shard_map/all_to_all | solution.py:298
  67.0 17.0 %stored.1 = (bf16[6144,768]{1,0:T(8,128)(2,1)}, f32[768,128]{1,0:T(8,128)S(1)}) custom-call(s32[32,128]{1,0:T(8,128)S(1)} %copy-done.13, bf16[6144,768]{1,0:T(8,128)(2,1)} %bitcast.13, f32[6144,128]{1,0:T(8,128)} %get-tuple-element.34.proj_ref, bf16[768,128]{1,0:T(8,128)(2,1)S(1)} %copy-done.3, bf16[32,80,128]{2,1,0:T(8,128)(2,1)S(1)} %all-to-all-done.recv_ref, ...), custom_call_target="tpu_custom_call" | custom-call | flops 3623878656 | bytes 24000000 | tf_op jit(solution)/shard_map/stored/pallas_call | solution.py:376
  84.0 1.0 finish.1
  85.1 21.4 %all_to_all.25.recv_ref = bf16[128,8,128]{2,1,0:T(8,128)(2,1)S(1)} all-to-all(bf16[128,8,128]{2,1,0:T(8,128)(2,1)S(1)} %get-tuple-element.37), channel_id=1, replica_groups=mesh['group'=4,'dev'=32] {'group','dev'}, dimensions={0} | all-to-all | bytes 524288 | tf_op jit(solution)/shard_map/all_to_all | solution.py:298
  106.5 0.9 reduce.3
  107.3 4.3 %all-to-all-start.4 = ((bf16[128,8,128]{2,1,0:T(8,128)(2,1)}), bf16[128,8,128]{2,1,0:T(8,128)(2,1)S(1)}, u32[]{:S(2)}, u32[]{:S(2)}) async-start(bf16[128,8,128]{2,1,0:T(8,128)(2,1)} %reduce.3), calls=%async_computation.4 | async-start | bytes 524288 | tf_op jit(solution)/shard_map/all_to_all | solution.py:298
  112.3 10.5 %all-to-all-done.4 = bf16[128,8,128]{2,1,0:T(8,128)(2,1)S(1)} async-done(((bf16[128,8,128]{2,1,0:T(8,128)(2,1)}), bf16[128,8,128]{2,1,0:T(8,128)(2,1)S(1)}, u32[]{:S(2)}, u32[]{:S(2)}) %all-to-all-start.4) | async-done | bytes 262176 | tf_op jit(solution)/shard_map/all_to_all | solution.py:298
  (46 shorter events, 10.0 us)
Async XLA Ops:
  0.6 0.9 copy-start.1
  1.6 0.9 copy-start.9
  2.5 0.7 copy-start.18
  3.2 0.7 copy-start.19
  3.9 0.7 copy-start.22
  4.6 0.7 copy-start.23
  7.8 21.5 %all-to-all-start = ((bf16[32,80,128]{2,1,0:T(8,128)(2,1)}), bf16[32,80,128]{2,1,0:T(8,128)(2,1)S(1)}, u32[]{:S(2)}, u32[]{:S(2)}) async-start(bf16[32,80,128]{2,1,0:T(8,128)(2,1)} %get-tuple-element.22), calls=%async_computation | async-start | bytes 1310720 | tf_op jit(solution)/shard_map/all_to_all | solution.py:298
  16.4 0.9 copy-start.2
  26.4 1.1 copy-start
  29.3 37.0 %copy-start.3 = (bf16[768,128]{1,0:T(8,128)(2,1)S(1)}, bf16[768,128]{1,0:T(8,128)(2,1)}, u32[]{:S(2)}) copy-start(bf16[768,128]{1,0:T(8,128)(2,1)} %weight_ref.7) | copy-start | bytes 589828
  35.7 0.8 copy-start.4
  37.7 13.2 %all-to-all-start.1 = ((f32[32,8,128]{2,1,0:T(8,128)}), f32[32,8,128]{2,1,0:T(8,128)S(1)}, u32[]{:S(2)}, u32[]{:S(2)}) async-start(f32[32,8,128]{2,1,0:T(8,128)} %get-tuple-element.24), calls=%async_computation.1 | async-start | bytes 262144 | tf_op jit(solution)/shard_map/all_to_all | solution.py:298
  51.6 1.0 copy-start.5
  52.6 0.9 copy-start.7
  53.5 0.7 copy-start.12
  54.2 0.8 copy-start.15
  55.0 0.7 copy-start.21
  61.0 0.8 copy-start.8
  62.3 21.7 %all-to-all-start.2 = ((bf16[32,64,128]{2,1,0:T(8,128)(2,1)}), bf16[32,64,128]{2,1,0:T(8,128)(2,1)S(1)}, u32[]{:S(2)}, u32[]{:S(2)}) async-start(bf16[32,64,128]{2,1,0:T(8,128)(2,1)} %copy-done.8), calls=%async_computation.2 | async-start | bytes 1048576 | tf_op jit(solution)/shard_map/all_to_all | solution.py:298
  66.3 0.7 copy-start.13
  67.0 17.0 %copy-start.10 = (bf16[2,32,768]{2,1,0:T(8,128)(2,1)S(1)}, bf16[2,32,768]{2,1,0:T(8,128)(2,1)}, u32[]{:S(2)}) copy-start(bf16[2,32,768]{2,1,0:T(8,128)(2,1)} %param.7) | copy-start | bytes 294916
  67.0 17.0 %copy-start.17 = (f32[64,128]{1,0:T(8,128)S(1)}, f32[64,128]{1,0:T(8,128)}, u32[]{:S(2)}) copy-start(f32[64,128]{1,0:T(8,128)} %copy-done.16) | copy-start | bytes 98308
  67.0 44.6 %copy-start.25 = (f32[2,128]{1,0:T(2,128)S(1)}, f32[2,128]{1,0:T(2,128)}, u32[]{:S(2)}) copy-start(f32[2,128]{1,0:T(2,128)} %copy-done.24) | copy-start | bytes 3076
  107.3 15.4 %all-to-all-start.4 = ((bf16[128,8,128]{2,1,0:T(8,128)(2,1)}), bf16[128,8,128]{2,1,0:T(8,128)(2,1)S(1)}, u32[]{:S(2)}, u32[]{:S(2)}) async-start(bf16[128,8,128]{2,1,0:T(8,128)(2,1)} %reduce.3), calls=%async_computation.4 | async-start | bytes 524288 | tf_op jit(solution)/shard_map/all_to_all | solution.py:298
  (6 other events, 3.6 us)

commit v2 on v1

v2 whole, which is shorter than its diff:
```python
import jax
import jax.numpy as jnp
from jax import lax
from jax.experimental import pallas as pl
from jax.experimental.pallas import tpu as pltpu
from jax.sharding import PartitionSpec as P

TAU = 0.0625
LOSS_SCALE = 32768.0
EPS = 1e-06

N_DEV = 32
N_ALL = 128
STORED = 128
PLEN = 48
QLEN = 32
D = 768
DIM = 128
PER_QUERY = 64
CAP = 12
SLOTS = 16
WIDE = CAP * PLEN
QROWS = 2 * QLEN
META = 16
CHUNK = 4
TOKENS = STORED * PLEN
BLOCK = 1536
STEPS = TOKENS // BLOCK
LANES = 4
PART = 768
PARTS = TOKENS // PART
AHEAD = 3
HEAD_TILES = D // 8

BF = jnp.bfloat16
F32 = jnp.float32
ROWS_ROWS = (((0,), (0,)), ((), ()))
COLS_COLS = (((1,), (1,)), ((), ()))
VMEM = pl.BlockSpec(memory_space=pltpu.VMEM)
SMEM = pl.BlockSpec(memory_space=pltpu.SMEM)
HBM = pl.BlockSpec(memory_space=pltpu.HBM)


def params(mib):
    return pltpu.CompilerParams(vmem_limit_bytes=mib * 1024 * 1024)


def dot(a, b, dims=(((1,), (0,)), ((), ()))):
    return lax.dot_general(a, b, dims, preferred_element_type=F32)


def iota(shape, axis):
    return lax.broadcasted_iota(jnp.int32, shape, axis)


def start_copies(pairs, sems):
    copies = [pltpu.make_async_copy(a, b, sems.at[i]) for i, (a, b) in enumerate(pairs)]
    for copy in copies:
        copy.start()
    return copies


def wait_copies(copies):
    for copy in copies:
        copy.wait()


def split3(x):
    hi = x.astype(BF).astype(F32)
    mid = (x - hi).astype(BF).astype(F32)
    return hi, mid, (x - hi - mid)


def expander(copies):
    row = iota((DIM, WIDE), 0)
    slot = (row & (SLOTS - 1)) * PLEN
    lane = iota((DIM, WIDE), 1)
    hit = (lane >= slot) & (lane < slot + PLEN) & (row < copies * SLOTS)
    return jnp.where(hit, 1.0, 0.0)


def request_kernel(hidden_hbm, weight_hbm, teacher_hbm, cand_hbm, storage_hbm, lengths_hbm,
                   send_ref, proj_hbm, const_hbm,
                   hidden_ref, weight_ref, teacher_ref, cand_ref, storage_ref, lengths_ref,
                   place_ref, length_ref, proj_ref, const_ref, sems, out_sems):
    small = start_copies(
        (
            (cand_hbm, cand_ref),
            (storage_hbm, storage_ref),
            (lengths_hbm, lengths_ref),
            (teacher_hbm, teacher_ref),
            (weight_hbm, weight_ref),
            (hidden_hbm, hidden_ref),
        ),
        sems,
    )
    wait_copies(small)
    for i in range(N_DEV):
        place_ref[i : i + 1, :] = storage_ref[0:1, i * STORED : (i + 1) * STORED]
        length_ref[i : i + 1, :] = lengths_ref[0:1, i * STORED : (i + 1) * STORED]
    proj = dot(hidden_ref[...], weight_ref[...])
    proj_ref[...] = proj
    inverse = lax.rsqrt(jnp.sum(proj * proj, axis=-1, keepdims=True) + EPS)
    embed = (proj * inverse).astype(BF)

    teacher = teacher_ref[...]
    log_t = teacher - jnp.log(jnp.sum(jnp.exp(teacher), axis=-1, keepdims=True))
    prob = jnp.exp(log_t)
    const = jnp.sum(prob * log_t, axis=-1, keepdims=True)
    const_ref[...] = jnp.concatenate(
        [jnp.broadcast_to(const, (2, DIM)), jnp.zeros((6, DIM), F32)], axis=0
    )
    outs = start_copies(((proj_ref, proj_hbm), (const_ref, const_hbm)), out_sems)
    prob_row = jnp.concatenate([prob[0:1], prob[1:2]], axis=1)
    cand = cand_ref[...]
    cand_row = jnp.concatenate([cand[0:1], cand[1:2]], axis=1)

    place = place_ref[...]
    owner_table = (place >> 7).astype(F32).astype(BF)
    slot_table = (place & (STORED - 1)).astype(F32).astype(BF)
    length_table = length_ref[...].astype(F32).astype(BF)
    sub32 = iota((N_DEV, DIM), 0)
    sub128 = iota((DIM, DIM), 0)
    lane128 = iota((DIM, DIM), 1)
    high = jnp.where(sub32 == (cand_row >> 7), 1.0, 0.0).astype(BF)
    low = sub128 == (cand_row & (STORED - 1))
    owner = jnp.sum(jnp.where(low, dot(owner_table, high, ROWS_ROWS), 0.0), axis=0, keepdims=True)
    slot = jnp.sum(jnp.where(low, dot(slot_table, high, ROWS_ROWS), 0.0), axis=0, keepdims=True)
    match = jnp.where(sub32 == owner.astype(jnp.int32), 1.0, 0.0)
    match_bf = match.astype(BF)
    at_slot = sub128 == slot.astype(jnp.int32)
    length = jnp.sum(
        jnp.where(at_slot, dot(length_table, match_bf, ROWS_ROWS), 0.0), axis=0, keepdims=True
    )
    earlier = jnp.where(sub128 < lane128, 1.0, 0.0).astype(BF)
    rank = jnp.sum(match * dot(match_bf, earlier), axis=0, keepdims=True).astype(jnp.int32)
    t_hi, t_mid, t_lo = split3(prob_row)
    which = jnp.where(iota((1, DIM), 1) >= PER_QUERY, 1.0, 0.0)
    fields = (slot, which, length, t_hi, t_mid, t_lo, jnp.ones((1, DIM), F32))
    field_of = sub128 >> 4
    values = jnp.zeros((DIM, DIM), F32)
    for f, row in enumerate(fields):
        values = jnp.where(field_of == f, row, values)
    values = jnp.where((sub128 & (SLOTS - 1)) == rank, values, 0.0).astype(BF)
    meta = dot(match_bf, values, COLS_COLS)
    for s in range(N_DEV):
        send_ref[s, 0:QROWS, :] = embed
        send_ref[s, QROWS : QROWS + META, :] = jnp.broadcast_to(meta[s : s + 1], (META, DIM)).astype(BF)
    wait_copies(outs)


def token_copies(hidden_hbm, hidden_ref, sems):
    copies = []
    for i in range(PARTS):
        rows = pl.ds(i * PART, PART)
        copies.append(pltpu.make_async_copy(hidden_hbm.at[rows], hidden_ref.at[rows], sems.at[i]))
    return copies


def encode_kernel(hidden_hbm, weight_hbm, proj_hbm, embed_ref, hidden_ref, weight_ref, proj_ref, sems, out_sems):
    weight_copy = pltpu.make_async_copy(weight_hbm, weight_ref, sems.at[PARTS])
    weight_copy.start()
    copies = token_copies(hidden_hbm, hidden_ref, sems)
    for copy in copies[:AHEAD]:
        copy.start()
    weight_copy.wait()
    outs = []
    for i, copy in enumerate(copies):
        rows = pl.ds(i * PART, PART)
        copy.wait()
        if i + AHEAD < PARTS:
            copies[i + AHEAD].start()
        proj = dot(hidden_ref[rows, :], weight_ref[...])
        proj_ref[rows, :] = proj
        outs.append(pltpu.make_async_copy(proj_ref.at[rows], proj_hbm.at[rows], out_sems.at[i]))
        outs[-1].start()
        inverse = lax.rsqrt(jnp.sum(proj * proj, axis=-1, keepdims=True) + EPS)
        embed_ref[rows, :] = (proj * inverse).astype(BF)
    for out in outs:
        out.wait()


def stored_rows(embed_ref, place_ref, s):
    parts = []
    for k in range(CAP):
        start = pl.multiple_of(place_ref[s, k], 16)
        parts.append(embed_ref[pl.ds(start, PLEN), :])
    return jnp.concatenate(parts, axis=0)


def score_kernel(recv_ref, embed_ref, expo_hbm, recip_hbm, sums_ref, table_hbm, second_hbm, place_hbm,
                 recip_ref, table_ref, second_ref, place_ref, meta_ref, limit_ref, expo_ref, round_ref,
                 smem_ref, sem, expo_sems, out_sems):
    for s in range(N_DEV):
        rows = recv_ref[s, QROWS : QROWS + META, :].astype(F32)
        meta_ref[s : s + 1, :] = rows[0:1, :]
    meta = meta_ref[...]
    place_ref[...] = meta.astype(jnp.int32) * PLEN
    copy = pltpu.make_async_copy(place_ref, smem_ref, sem)
    copy.start()
    outs = start_copies(((place_ref, place_hbm),), out_sems)
    meta_bf = meta.astype(BF)
    spread = expander(1)
    second_ref[...] = dot(pltpu.roll(meta, DIM - SLOTS, 1).astype(BF), spread.astype(BF))
    length = dot(pltpu.roll(meta, DIM - 2 * SLOTS, 1).astype(BF), spread.astype(BF))
    lane = iota((1, WIDE), 1)
    token = lane
    for k in range(1, CAP):
        token = token - jnp.where(lane >= k * PLEN, PLEN, 0)
    limit_ref[...] = jnp.where(token.astype(F32) < length, 1.0, 0.0)
    outs += start_copies(((second_ref, second_hbm),), out_sems.at[pl.ds(1, 1)])
    copy.wait()

    def expo_copy(i):
        rows = pl.ds(i * (CHUNK * QLEN), CHUNK * QLEN)
        return pltpu.make_async_copy(expo_ref.at[rows], expo_hbm.at[rows], expo_sems.at[i])

    def chunk(i, carry):
        for u in range(CHUNK):
            s = i * CHUNK + u
            queries = recv_ref[s, 0:QROWS, :]
            sims = dot(queries, stored_rows(embed_ref, smem_ref, s), COLS_COLS)
            second = second_ref[pl.ds(s, 1), :]
            valid = limit_ref[pl.ds(s, 1), :]
            mine = jnp.where(second > 0.5, sims[QLEN:QROWS], sims[0:QLEN])
            expo = jnp.where(valid > 0.5, jnp.exp(mine * (1.0 / TAU)), 0.0)
            rows = pl.ds(pl.multiple_of(s * QLEN, QLEN), QLEN)
            expo_ref[rows, :] = expo
            round_ref[rows, :] = expo.astype(BF)
        expo_copy(i).start()
        return carry

    lax.fori_loop(0, N_DEV // CHUNK, chunk, 0)
    total = dot(round_ref[...], spread.astype(BF), COLS_COLS)
    total = jnp.where(total > 0.0, total, 1.0)
    recip_ref[...] = 1.0 / total
    outs += start_copies(((recip_ref, recip_hbm),), out_sems.at[pl.ds(2, 1)])
    scores = TAU * jnp.sum(jnp.log(total).reshape(N_DEV, QLEN, DIM), axis=1)
    lane = iota((N_DEV, DIM), 1)
    present = (pltpu.roll(meta, DIM - 6 * SLOTS, 1) > 0.5) & (lane < SLOTS)
    teach = (
        pltpu.roll(meta, DIM - 3 * SLOTS, 1)
        + pltpu.roll(meta, DIM - 4 * SLOTS, 1)
        + pltpu.roll(meta, DIM - 5 * SLOTS, 1)
    )
    teach = jnp.where(present, teach, 0.0)
    student = jnp.where(present, jnp.exp(scores), 0.0)
    which = pltpu.roll(meta, DIM - SLOTS, 1) > 0.5
    table_ref[0] = student
    table_ref[1] = teach
    table_ref[2] = jnp.where(which, 1.0, 0.0)
    outs += start_copies(((table_ref, table_hbm),), out_sems.at[pl.ds(3, 1)])
    gain = teach * scores
    columns = []
    for value in (student, gain):
        columns.append(jnp.sum(jnp.where(which, 0.0, value), axis=-1, keepdims=True))
        columns.append(jnp.sum(jnp.where(which, value, 0.0), axis=-1, keepdims=True))
    mixed = jnp.zeros((N_DEV, DIM), F32)
    for j, column in enumerate(columns):
        mixed = jnp.where(lane == j, column, mixed)
    mixed = jnp.concatenate([mixed, jnp.zeros((DIM - N_DEV, DIM), F32)], axis=0)
    part = jnp.transpose(mixed)[0:8, :]
    for s in range(N_DEV):
        sums_ref[s] = part
    wait_copies(outs)
    wait_copies([expo_copy(i) for i in range(N_DEV // CHUNK)])


def halves(one, second):
    return jnp.concatenate(
        [jnp.where(second, 0.0, one).astype(BF), jnp.where(second, one, 0.0).astype(BF)], axis=0
    )


def ahead_kernel(recv_ref, second_hbm, expo_hbm, recip_hbm, weights_ref, turned_hbm,
                 second_ref, recip_ref, expo_ref, turned_ref, small_sems, sems, out_sems):
    small = start_copies(((recip_hbm, recip_ref), (second_hbm, second_ref)), small_sems)
    steps = N_DEV // CHUNK
    span = CHUNK * QLEN
    fetch = []
    for i in range(steps):
        rows = pl.ds(i * span, span)
        fetch.append(pltpu.make_async_copy(expo_hbm.at[rows], expo_ref.at[rows], sems.at[i]))
        fetch[-1].start()
    spread = expander(2).astype(BF)
    lane = iota((span, DIM), 1)
    outs = []
    wait_copies(small)
    for i in range(steps):
        rows = pl.ds(i * span, span)
        recip = recip_ref[rows, :]
        hi = recip.astype(BF).astype(F32)
        lo = recip - hi
        factor = jnp.where(lane < SLOTS, hi, jnp.where(lane < 2 * SLOTS, pltpu.roll(lo, SLOTS, 1), 0.0))
        wide = dot(factor.astype(BF), spread)
        fetch[i].wait()
        weights = expo_ref[rows, :] * wide
        weights_ref[rows, :] = weights.astype(BF)
        for u in range(CHUNK):
            s = i * CHUNK + u
            second = second_ref[s : s + 1, :] > 0.5
            both = halves(weights[u * QLEN : (u + 1) * QLEN], second)
            turned_ref[s] = dot(both, recv_ref[s, 0:QROWS, :], ROWS_ROWS).astype(BF)
        part = pl.ds(i * CHUNK, CHUNK)
        outs.append(pltpu.make_async_copy(turned_ref.at[part], turned_hbm.at[part], out_sems.at[i]))
        outs[-1].start()
    for out in outs:
        out.wait()


def query_kernel(sums_ref, const_hbm, me_ref, table_hbm, second_hbm, weights_ref, embed_ref, place_hbm,
                 send_ref, pull_hbm, loss_hbm,
                 const_ref, table_ref, second_ref, pull_ref, loss_ref, wide_ref, smem_ref, sems, out_sems):
    small = start_copies(
        ((table_hbm, table_ref), (place_hbm, smem_ref), (const_hbm, const_ref), (second_hbm, second_ref)), sems
    )
    sums = jnp.sum(sums_ref[...], axis=0)
    log_sum = jnp.log(jnp.where(sums > 0.0, sums, 1.0))
    turned = jnp.transpose(jnp.concatenate([sums, jnp.zeros((DIM - 8, DIM), F32)], axis=0))[0:N_DEV, :]
    wait_copies(small)
    loss = const_ref[0:2, :] + log_sum[0:2, :] - sums[2:4, :]
    picked = jnp.where(iota((2, DIM), 1) == me_ref[0], loss, 0.0)
    loss_ref[...] = jnp.broadcast_to(jnp.sum(picked, axis=-1, keepdims=True), (2, DIM))
    normal = jnp.where(table_ref[2] > 0.5, turned[:, 1:2], turned[:, 0:1])
    pull = LOSS_SCALE * (table_ref[0] / normal - table_ref[1])
    pull_ref[...] = pull
    outs = start_copies(((pull_ref, pull_hbm), (loss_ref, loss_hbm)), out_sems)
    hi = pull.astype(BF).astype(F32)
    lo = pull - hi
    lane = iota((N_DEV, DIM), 1)
    factor = jnp.where(lane < SLOTS, hi, jnp.where(lane < 2 * SLOTS, pltpu.roll(lo, SLOTS, 1), 0.0))
    wide_ref[...] = dot(factor.astype(BF), expander(2).astype(BF))

    def chunk(i, carry):
        for u in range(CHUNK):
            s = i * CHUNK + u
            rows = pl.ds(pl.multiple_of(s * QLEN, QLEN), QLEN)
            mixed = weights_ref[rows, :].astype(F32) * wide_ref[pl.ds(s, 1), :]
            both = halves(mixed, second_ref[pl.ds(s, 1), :] > 0.5)
            send_ref[s] = dot(both, stored_rows(embed_ref, smem_ref, s)).astype(BF)
        return carry

    lax.fori_loop(0, N_DEV // CHUNK, chunk, 0)
    wait_copies(outs)


def stored_kernel(place_hbm, pull_hbm, hidden_hbm, proj_hbm, turned_hbm, preact_ref, head_ref,
                  hidden_ref, proj_ref, turned_ref, delta_ref, place_smem, pull_smem, smem_sems,
                  sems, turned_sems, proj_sem):
    steps = N_DEV // CHUNK
    scalars = start_copies(((place_hbm, place_smem), (pull_hbm, pull_smem)), smem_sems)
    fetch = []
    for i in range(steps):
        part = pl.ds(i * CHUNK, CHUNK)
        fetch.append(pltpu.make_async_copy(turned_hbm.at[part], turned_ref.at[part], turned_sems.at[i]))
        fetch[-1].start()
    proj_copy = pltpu.make_async_copy(proj_hbm, proj_ref, proj_sem)
    proj_copy.start()
    copies = token_copies(hidden_hbm, hidden_ref, sems)
    for copy in copies:
        copy.start()
    delta_ref[...] = jnp.zeros_like(delta_ref)
    wait_copies(scalars)

    def add(s, carry):
        for k in range(CAP):
            at = pl.ds(pl.multiple_of(place_smem[s, k], 16), PLEN)
            part = turned_ref[s, k * PLEN : (k + 1) * PLEN, :].astype(F32)
            delta_ref[k % LANES, at, :] += part * pull_smem[s, k]
        return carry

    for i in range(steps):
        fetch[i].wait()
        lax.fori_loop(i * CHUNK, (i + 1) * CHUNK, add, 0)
    proj_copy.wait()
    total = jnp.zeros((DIM, D), F32)
    for i in range(STEPS):
        rows = pl.ds(i * BLOCK, BLOCK)
        proj = proj_ref[rows, :]
        delta = jnp.sum(delta_ref[:, rows, :], axis=0)
        inverse = lax.rsqrt(jnp.sum(proj * proj, axis=-1, keepdims=True) + EPS)
        unit = proj * inverse
        radial = jnp.sum(unit * delta, axis=-1, keepdims=True)
        preact = ((delta - unit * radial) * inverse).astype(BF)
        preact_ref[rows, :] = preact
        for j in range(i * BLOCK // PART, (i + 1) * BLOCK // PART):
            copies[j].wait()
        total = total + dot(preact, hidden_ref[rows, :], ROWS_ROWS)
    head_ref[...] = jnp.transpose(total)


def back_kernel(preact_ref, weight_ref, grad_ref):
    grad_ref[...] = dot(preact_ref[...], weight_ref[...], COLS_COLS).astype(BF)


def finish_kernel(recv_ref, hidden_hbm, weight_hbm, proj_hbm, head_ref, grad_ref, send_ref,
                  hidden_ref, weight_ref, proj_ref, sems):
    copies = start_copies(((proj_hbm, proj_ref), (hidden_hbm, hidden_ref), (weight_hbm, weight_ref)), sems)
    delta = jnp.sum(recv_ref[...].astype(F32), axis=0)
    copies[0].wait()
    proj = proj_ref[...]
    inverse = lax.rsqrt(jnp.sum(proj * proj, axis=-1, keepdims=True) + EPS)
    unit = proj * inverse
    radial = jnp.sum(unit * delta, axis=-1, keepdims=True)
    preact = ((delta - unit * radial) * inverse).astype(BF)
    wait_copies(copies[1:])
    grad_ref[...] = dot(preact, weight_ref[...], COLS_COLS).astype(BF)
    head = head_ref[...] + dot(hidden_ref[...], preact, ROWS_ROWS)
    send_ref[0:HEAD_TILES] = head.reshape(HEAD_TILES, 8, DIM).astype(BF)
    send_ref[HEAD_TILES:N_ALL] = jnp.zeros((N_ALL - HEAD_TILES, 8, DIM), BF)


def reduce_kernel(recv_ref, send_ref):
    total = jnp.sum(recv_ref[...].astype(F32), axis=0).astype(BF)
    send_ref[...] = jnp.broadcast_to(total[None], (N_ALL, 8, DIM))


def shape(dims, kind):
    return jax.ShapeDtypeStruct(dims, kind)


def in_hbm(x):
    return pltpu.with_memory_space_constraint(x, pltpu.HBM)


def in_vmem(x):
    return pltpu.with_memory_space_constraint(x, pltpu.VMEM)


def exchange(x, axes):
    return lax.all_to_all(x, axes, split_axis=0, concat_axis=0, tiled=True)


def estimate(flops, size):
    return pl.CostEstimate(flops=flops, bytes_accessed=size, transcendentals=0)


def on_device(query_hidden, passage_hidden, head_weight, teacher, candidates, storage, lengths):
    query_flat = in_hbm(query_hidden.reshape(QROWS, D))
    flat_hidden = in_hbm(passage_hidden.reshape(TOKENS, D))
    head_weight = in_hbm(head_weight)
    send, query_proj, const = pl.pallas_call(
        request_kernel,
        out_shape=(
            shape((N_DEV, QROWS + META, DIM), BF),
            pltpu.HBM((QROWS, DIM), F32),
            pltpu.HBM((8, DIM), F32),
        ),
        in_specs=[HBM] * 6,
        out_specs=(VMEM, HBM, HBM),
        scratch_shapes=[
            pltpu.VMEM((QROWS, D), BF),
            pltpu.VMEM((D, DIM), BF),
            pltpu.VMEM((2, PER_QUERY), F32),
            pltpu.VMEM((2, PER_QUERY), jnp.int32),
            pltpu.VMEM((1, N_DEV * STORED), jnp.int32),
            pltpu.VMEM((1, N_DEV * STORED), jnp.int32),
            pltpu.VMEM((N_DEV, DIM), jnp.int32),
            pltpu.VMEM((N_DEV, DIM), jnp.int32),
            pltpu.VMEM((QROWS, DIM), F32),
            pltpu.VMEM((8, DIM), F32),
            pltpu.SemaphoreType.DMA((6,)),
            pltpu.SemaphoreType.DMA((2,)),
        ],
        compiler_params=params(4),
        name="request",
    )(query_flat, head_weight, in_hbm(teacher), in_hbm(candidates), in_hbm(storage), in_hbm(lengths))
    recv = exchange(send, "dev")

    proj, embed = pl.pallas_call(
        encode_kernel,
        out_shape=(pltpu.HBM((TOKENS, DIM), F32), pltpu.VMEM((TOKENS, DIM), BF)),
        in_specs=[HBM, HBM],
        out_specs=(HBM, VMEM),
        scratch_shapes=[
            pltpu.VMEM((TOKENS, D), BF),
            pltpu.VMEM((D, DIM), BF),
            pltpu.VMEM((TOKENS, DIM), F32),
            pltpu.SemaphoreType.DMA((PARTS + 1,)),
            pltpu.SemaphoreType.DMA((PARTS,)),
        ],
        cost_estimate=estimate(2 * TOKENS * D * DIM, 15_000_000),
        compiler_params=params(20),
        name="encode",
    )(flat_hidden, head_weight)

    expo, recip, sums, table, second, place = pl.pallas_call(
        score_kernel,
        out_shape=(
            pltpu.HBM((N_DEV * QLEN, WIDE), F32),
            pltpu.HBM((N_DEV * QLEN, DIM), F32),
            shape((N_DEV, 8, DIM), F32),
            pltpu.HBM((3, N_DEV, DIM), F32),
            pltpu.HBM((N_DEV, WIDE), F32),
            pltpu.HBM((N_DEV, DIM), jnp.int32),
        ),
        in_specs=[VMEM] * 2,
        out_specs=(HBM, HBM, VMEM, HBM, HBM, HBM),
        scratch_shapes=[
            pltpu.VMEM((N_DEV * QLEN, DIM), F32),
            pltpu.VMEM((3, N_DEV, DIM), F32),
            pltpu.VMEM((N_DEV, WIDE), F32),
            pltpu.VMEM((N_DEV, DIM), jnp.int32),
            pltpu.VMEM((N_DEV, DIM), F32),
            pltpu.VMEM((N_DEV, WIDE), F32),
            pltpu.VMEM((N_DEV * QLEN, WIDE), F32),
            pltpu.VMEM((N_DEV * QLEN, WIDE), BF),
            pltpu.SMEM((N_DEV, DIM), jnp.int32),
            pltpu.SemaphoreType.DMA,
            pltpu.SemaphoreType.DMA((N_DEV // CHUNK,)),
            pltpu.SemaphoreType.DMA((4,)),
        ],
        compiler_params=params(14),
        name="score",
    )(recv, in_vmem(embed))
    all_sums = exchange(sums, "dev")

    weights, turned = pl.pallas_call(
        ahead_kernel,
        out_shape=(pltpu.VMEM((N_DEV * QLEN, WIDE), BF), pltpu.HBM((N_DEV, WIDE, DIM), BF)),
        in_specs=[VMEM, HBM, HBM, HBM],
        out_specs=(VMEM, HBM),
        scratch_shapes=[
            pltpu.VMEM((N_DEV, WIDE), F32),
            pltpu.VMEM((N_DEV * QLEN, DIM), F32),
            pltpu.VMEM((N_DEV * QLEN, WIDE), F32),
            pltpu.VMEM((N_DEV, WIDE, DIM), BF),
            pltpu.SemaphoreType.DMA((2,)),
            pltpu.SemaphoreType.DMA((N_DEV // CHUNK,)),
            pltpu.SemaphoreType.DMA((N_DEV // CHUNK,)),
        ],
        cost_estimate=estimate(2 * TOKENS * D * DIM, 15_000_000),
        compiler_params=params(22),
        name="ahead",
    )(recv, in_hbm(second), in_hbm(expo), in_hbm(recip))

    me = lax.axis_index("dev").astype(jnp.int32).reshape(1)
    send_delta, pull, loss = pl.pallas_call(
        query_kernel,
        out_shape=(
            shape((N_DEV, QROWS, DIM), BF),
            pltpu.HBM((N_DEV, DIM), F32),
            pltpu.HBM((2, DIM), F32),
        ),
        in_specs=[VMEM, HBM, SMEM, HBM, HBM, VMEM, VMEM, HBM],
        out_specs=(VMEM, HBM, HBM),
        scratch_shapes=[
            pltpu.VMEM((8, DIM), F32),
            pltpu.VMEM((3, N_DEV, DIM), F32),
            pltpu.VMEM((N_DEV, WIDE), F32),
            pltpu.VMEM((N_DEV, DIM), F32),
            pltpu.VMEM((2, DIM), F32),
            pltpu.VMEM((N_DEV, WIDE), F32),
            pltpu.SMEM((N_DEV, DIM), jnp.int32),
            pltpu.SemaphoreType.DMA((4,)),
            pltpu.SemaphoreType.DMA((2,)),
        ],
        compiler_params=params(12),
        name="query",
    )(all_sums, in_hbm(const), me, in_hbm(table), in_hbm(second), in_vmem(weights), in_vmem(embed), in_hbm(place))
    recv_delta = exchange(send_delta, "dev")

    preact, head = pl.pallas_call(
        stored_kernel,
        out_shape=(pltpu.VMEM((TOKENS, DIM), BF), pltpu.VMEM((D, DIM), F32)),
        in_specs=[HBM] * 5,
        out_specs=(VMEM, VMEM),
        scratch_shapes=[
            pltpu.VMEM((TOKENS, D), BF),
            pltpu.VMEM((TOKENS, DIM), F32),
            pltpu.VMEM((N_DEV, WIDE, DIM), BF),
            pltpu.VMEM((LANES, TOKENS, DIM), F32),
            pltpu.SMEM((N_DEV, DIM), jnp.int32),
            pltpu.SMEM((N_DEV, DIM), F32),
            pltpu.SemaphoreType.DMA((2,)),
            pltpu.SemaphoreType.DMA((PARTS,)),
            pltpu.SemaphoreType.DMA((N_DEV // CHUNK,)),
            pltpu.SemaphoreType.DMA,
        ],
        cost_estimate=estimate(4 * TOKENS * D * DIM, 20_000_000),
        compiler_params=params(40),
        name="stored",
    )(in_hbm(place), in_hbm(pull), flat_hidden, in_hbm(proj), in_hbm(turned))

    query_grad, send_head = pl.pallas_call(
        finish_kernel,
        out_shape=(shape((QROWS, D), BF), shape((N_ALL, 8, DIM), BF)),
        in_specs=[VMEM, HBM, HBM, HBM, VMEM],
        out_specs=(VMEM,) * 2,
        scratch_shapes=[
            pltpu.VMEM((QROWS, D), BF),
            pltpu.VMEM((D, DIM), BF),
            pltpu.VMEM((QROWS, DIM), F32),
            pltpu.SemaphoreType.DMA((3,)),
        ],
        compiler_params=params(8),
        name="finish",
    )(recv_delta, query_flat, head_weight, in_hbm(query_proj), in_vmem(head))
    recv_head = exchange(send_head, ("group", "dev"))

    passage_grad = pl.pallas_call(
        back_kernel,
        grid=(STEPS,),
        out_shape=shape((TOKENS, D), BF),
        in_specs=[
            pl.BlockSpec((BLOCK, DIM), lambda i: (i, 0)),
            pl.BlockSpec((D, DIM), lambda i: (0, 0)),
        ],
        out_specs=pl.BlockSpec((BLOCK, D), lambda i: (i, 0)),
        cost_estimate=estimate(2 * TOKENS * D * DIM, 15_000_000),
        compiler_params=params(20),
        name="back",
    )(in_vmem(preact), head_weight)

    send_total = pl.pallas_call(
        reduce_kernel,
        out_shape=shape((N_ALL, 8, DIM), BF),
        in_specs=[VMEM],
        out_specs=VMEM,
        compiler_params=params(4),
        name="reduce",
    )(recv_head)
    head_all = exchange(send_total, ("group", "dev"))
    head_grad = head_all[:HEAD_TILES].reshape(D, DIM).astype(F32)
    return (
        loss[:, 0],
        head_grad,
        query_grad.reshape(2, QLEN, D),
        passage_grad.reshape(STORED, PLEN, D),
    )


def solution(mesh):
    return jax.shard_map(
        on_device,
        mesh=mesh,
        in_specs=(
            P(("group", "dev"), None, None),
            P(("group", "dev"), None, None),
            P(),
            P(("group", "dev"), None),
            P(("group", "dev"), None),
            P("group", None),
            P("group", None),
        ),
        out_specs=(
            P(("group", "dev")),
            P(),
            P(("group", "dev"), None, None),
            P(("group", "dev"), None, None),
        ),
        check_vma=False,
    )
```

time: 125 us -> 105 us (0.84)
  local copies, waits for them, and re-layouts: 17.4 us -> 0.63 us
  waiting for transfers between devices: 19.9 us -> 11.8 us
  Pallas kernels: 40.9 us -> 47.4 us
  blocking collectives: 21.4 us -> 19.5 us
    unnamed x52 -> x2, local copies, waits for them, and re-layouts: 16.7 us -> 0.01 us
    all_to_all x4, waiting for transfers between devices: 19.9 us -> 11.8 us  [exchange(): return lax.all_to_all(x, axes, split_axis=0, concat_axis=0, tiled=True)]
    pallas_call x4 -> x6, Pallas kernels: 37.6 us -> 41.8 us  [the longest x1 9.64 us: on_device(): pl.pallas_call(stored_kernel, out_shape=(pltpu.VMEM((TOKENS, DIM), BF), p...]
    all_to_all x1, blocking collectives: 21.4 us -> 19.5 us  [exchange(): return lax.all_to_all(x, axes, split_axis=0, concat_axis=0, tiled=True)]
    pallas_call x1, Pallas kernels: 1.37 us -> 2.84 us  [on_device(): pl.pallas_call(request_kernel, out_shape=(shape((N_DEV, QROWS + META, DIM...]
  transfers between devices with their start and end apart: 4 -> 4, of which waited for: 3 -> 4; matrix products, arithmetic and copies ran while one was open for 1% -> 1% of each run, Pallas kernels for 21% -> 30%
where the time goes in v2:
time: 105 us; the launch traced here: 104 us
  Pallas kernels  47.4 us (45%)
  starting transfers between devices  23.6 us (22%)
  blocking collectives  19.5 us (19%)
  waiting for transfers between devices  11.8 us (11%)
    all_to_all x4, starting transfers between devices, exchange(): return lax.all_to_all(x, axes, split_axis=0, concat_axis=0, tiled=True)  23.6 us
    all_to_all x1, blocking collectives, exchange(): return lax.all_to_all(x, axes, split_axis=0, concat_axis=0, tiled=True)  19.5 us
    all_to_all x4, waiting for transfers between devices, exchange(): return lax.all_to_all(x, axes, split_axis=0, concat_axis=0, tiled=True)  11.8 us
    pallas_call x1, Pallas kernels, on_device(): pl.pallas_call(stored_kernel, out_shape=(pltpu.VMEM((TOKENS, DIM), BF), p...  9.64 us
    pallas_call x1, Pallas kernels, on_device(): pl.pallas_call(encode_kernel, out_shape=(pltpu.HBM((TOKENS, DIM), F32), p...  8.95 us
    pallas_call x1, Pallas kernels, on_device(): pl.pallas_call(ahead_kernel, out_shape=(pltpu.VMEM((N_DEV * QLEN, WIDE),...  6.24 us
    pallas_call x1, Pallas kernels, on_device(): pl.pallas_call(back_kernel, grid=(STEPS,), out_shape=shape((TOKENS, D), B...  6.07 us
    pallas_call x1, Pallas kernels, on_device(): pl.pallas_call(score_kernel, out_shape=(pltpu.HBM((N_DEV * QLEN, WIDE), F...  5.68 us
  transfers between devices with their start and end apart: 4, of which 4 were waited for; matrix products, arithmetic and copies ran while one was open for 1% of the time, Pallas kernels for 30%

profile of v2, /device:TPU:1, one launch (start us, length us, event | category | flops | bytes accessed | tf_op | source)
XLA Modules:
  0.0 104.3 jit_solution(2487149378132827339)
XLA Ops:
  0.6 2.8 %request.1 = (bf16[32,80,128]{2,1,0:T(8,128)(2,1)}, f32[64,128]{1,0:T(8,128)}, f32[8,128]{1,0:T(8,128)}) custom-call(bf16[64,768]{1,0:T(8,128)(2,1)} %bitcast.13, bf16[768,128]{1,0:T(8,128)(2,1)} %weight_ref.1, f32[2,64]{1,0:T(2,128)} %teacher_hbm.1, s32[2,64]{1,0:T(2,128)} %cand_hbm.1, s32[1,4096]{1,0:T(1,128)} %storage_hbm.1, s32[1,4096]{1,0:T(1,128)} %lengths_hbm.1), custom_call_target="tpu_custom_call" | custom-call | tf_op jit(solution)/shard_map/request/pallas_call | solution.py:442
  3.5 8.6 %all-to-all-start = ((bf16[32,80,128]{2,1,0:T(8,128)(2,1)}), bf16[32,80,128]{2,1,0:T(8,128)(2,1)S(1)}, u32[]{:S(2)}, u32[]{:S(2)}) async-start(bf16[32,80,128]{2,1,0:T(8,128)(2,1)} %get-tuple-element.24), calls=%async_computation | async-start | bytes 1310720 | tf_op jit(solution)/shard_map/all_to_all | solution.py:431
  12.1 8.9 %encode.1 = (f32[6144,128]{1,0:T(8,128)}, bf16[6144,128]{1,0:T(8,128)(2,1)S(1)}) custom-call(bf16[6144,768]{1,0:T(8,128)(2,1)} %bitcast.10, bf16[768,128]{1,0:T(8,128)(2,1)} %weight_ref.1), custom_call_target="tpu_custom_call" | custom-call | flops 1207959552 | bytes 15000000 | tf_op jit(solution)/shard_map/encode/pallas_call | solution.py:470
  21.0 4.0 %all-to-all-done.recv_ref = bf16[32,80,128]{2,1,0:T(8,128)(2,1)S(1)} async-done(((bf16[32,80,128]{2,1,0:T(8,128)(2,1)}), bf16[32,80,128]{2,1,0:T(8,128)(2,1)S(1)}, u32[]{:S(2)}, u32[]{:S(2)}) %all-to-all-start) | async-done | bytes 655392 | tf_op jit(solution)/shard_map/all_to_all | solution.py:431
  25.0 5.7 %score.1 = (f32[1024,576]{1,0:T(8,128)}, f32[1024,128]{1,0:T(8,128)}, f32[32,8,128]{2,1,0:T(8,128)}, f32[3,32,128]{2,1,0:T(8,128)}, f32[32,576]{1,0:T(8,128)}, /*index=5*/s32[32,128]{1,0:T(8,128)}) custom-call(bf16[32,80,128]{2,1,0:T(8,128)(2,1)S(1)} %all-to-all-done.recv_ref, bf16[6144,128]{1,0:T(8,128)(2,1)S(1)} %get-tuple-element.25.embed_ref), custom_call_target="tpu_custom_call" | custom-call | tf_op jit(solution)/shard_map/score/pallas_call | solution.py:487
  30.7 4.7 %all-to-all-start.1 = ((f32[32,8,128]{2,1,0:T(8,128)}), f32[32,8,128]{2,1,0:T(8,128)}, u32[]{:S(2)}, u32[]{:S(2)}) async-start(f32[32,8,128]{2,1,0:T(8,128)} %get-tuple-element.26), calls=%async_computation.1 | async-start | bytes 262144 | tf_op jit(solution)/shard_map/all_to_all | solution.py:431
  35.4 6.2 %ahead.1 = (bf16[1024,576]{1,0:T(8,128)(2,1)S(1)}, bf16[32,576,128]{2,1,0:T(8,128)(2,1)}) custom-call(bf16[32,80,128]{2,1,0:T(8,128)(2,1)S(1)} %all-to-all-done.recv_ref, f32[32,576]{1,0:T(8,128)} %get-tuple-element.29.second_hbm, f32[1024,576]{1,0:T(8,128)} %get-tuple-element.30.expo_hbm, f32[1024,128]{1,0:T(8,128)} %get-tuple-element.31.recip_hbm), custom_call_target="tpu_custom_call" | custom-call | flops 1207959552 | bytes 15000000 | tf_op jit(solution)/shard_map/ahead/pallas_call | solution.py:518
  41.6 1.5 %all-to-all-done.1.sums_ref = f32[32,8,128]{2,1,0:T(8,128)} async-done(((f32[32,8,128]{2,1,0:T(8,128)}), f32[32,8,128]{2,1,0:T(8,128)}, u32[]{:S(2)}, u32[]{:S(2)}) %all-to-all-start.1) | async-done | bytes 131104 | tf_op jit(solution)/shard_map/all_to_all | solution.py:431
  43.2 5.2 %query.1 = (bf16[32,64,128]{2,1,0:T(8,128)(2,1)}, f32[32,128]{1,0:T(8,128)}, f32[2,128]{1,0:T(2,128)}) custom-call(f32[32,8,128]{2,1,0:T(8,128)} %all-to-all-done.1.sums_ref, f32[8,128]{1,0:T(8,128)} %get-tuple-element.27.const_hbm, s32[1]{0:T(128)} %bitcast.2.me_ref, f32[3,32,128]{2,1,0:T(8,128)} %get-tuple-element.28.table_hbm, ...), custom_call_target="tpu_custom_call" | custom-call | tf_op jit(solution)/shard_map/query/pallas_call | solution.py:538
  48.4 6.0 %all-to-all-start.2 = ((bf16[32,64,128]{2,1,0:T(8,128)(2,1)}), bf16[32,64,128]{2,1,0:T(8,128)(2,1)S(1)}, u32[]{:S(2)}, u32[]{:S(2)}) async-start(bf16[32,64,128]{2,1,0:T(8,128)(2,1)} %get-tuple-element.35), calls=%async_computation.2 | async-start | bytes 1048576 | tf_op jit(solution)/shard_map/all_to_all | solution.py:431
  54.4 0.0 copy-start
  54.4 9.6 %stored.1 = (bf16[6144,128]{1,0:T(8,128)(2,1)S(1)}, f32[768,128]{1,0:T(8,128)S(1)}) custom-call(s32[32,128]{1,0:T(8,128)} %get-tuple-element.33.place_hbm, f32[32,128]{1,0:T(8,128)} %get-tuple-element.37.pull_hbm, bf16[6144,768]{1,0:T(8,128)(2,1)} %bitcast.11, f32[6144,128]{1,0:T(8,128)} %get-tuple-element.38.proj_hbm, ...), custom_call_target="tpu_custom_call" | custom-call | flops 2415919104 | bytes 20000000 | tf_op jit(solution)/shard_map/stored/pallas_call | solution.py:563
  64.0 1.9 %all-to-all-done.2.recv_ref = bf16[32,64,128]{2,1,0:T(8,128)(2,1)S(1)} async-done(((bf16[32,64,128]{2,1,0:T(8,128)(2,1)}), bf16[32,64,128]{2,1,0:T(8,128)(2,1)S(1)}, u32[]{:S(2)}, u32[]{:S(2)}) %all-to-all-start.2) | async-done | bytes 524320 | tf_op jit(solution)/shard_map/all_to_all | solution.py:431
  65.9 1.9 %finish.1 = (bf16[64,768]{1,0:T(8,128)(2,1)}, bf16[128,8,128]{2,1,0:T(8,128)(2,1)S(1)}) custom-call(bf16[32,64,128]{2,1,0:T(8,128)(2,1)S(1)} %all-to-all-done.2.recv_ref, bf16[64,768]{1,0:T(8,128)(2,1)} %bitcast.14, bf16[768,128]{1,0:T(8,128)(2,1)} %weight_ref.1, f32[64,128]{1,0:T(8,128)} %get-tuple-element.36.proj_hbm, ...), custom_call_target="tpu_custom_call" | custom-call | tf_op jit(solution)/shard_map/finish/pallas_call | solution.py:585
  67.8 19.5 %all_to_all.25.recv_ref = bf16[128,8,128]{2,1,0:T(8,128)(2,1)S(1)} all-to-all(bf16[128,8,128]{2,1,0:T(8,128)(2,1)S(1)} %get-tuple-element.41), channel_id=1, replica_groups=mesh['group'=4,'dev'=32] {'group','dev'}, dimensions={0} | all-to-all | bytes 524288 | tf_op jit(solution)/shard_map/all_to_all | solution.py:431
  87.3 0.9 reduce.3
  88.2 4.3 %all-to-all-start.4 = ((bf16[128,8,128]{2,1,0:T(8,128)(2,1)}), bf16[128,8,128]{2,1,0:T(8,128)(2,1)S(1)}, u32[]{:S(2)}, u32[]{:S(2)}) async-start(bf16[128,8,128]{2,1,0:T(8,128)(2,1)} %reduce.3), calls=%async_computation.4 | async-start | bytes 524288 | tf_op jit(solution)/shard_map/all_to_all | solution.py:431
  92.5 0.0 copy-done
  92.5 0.6 slice_reduce_fusion
  93.1 6.1 %back.1 = bf16[6144,768]{1,0:T(8,128)(2,1)} custom-call(bf16[6144,128]{1,0:T(8,128)(2,1)S(1)} %get-tuple-element.43.preact_ref, bf16[768,128]{1,0:T(8,128)(2,1)} %weight_ref.1), custom_call_target="tpu_custom_call" | custom-call | flops 1207959552 | bytes 15000000 | tf_op jit(solution)/shard_map/back/pallas_call | solution.py:601
  99.2 4.4 %all-to-all-done.4 = bf16[128,8,128]{2,1,0:T(8,128)(2,1)S(1)} async-done(((bf16[128,8,128]{2,1,0:T(8,128)(2,1)}), bf16[128,8,128]{2,1,0:T(8,128)(2,1)S(1)}, u32[]{:S(2)}, u32[]{:S(2)}) %all-to-all-start.4) | async-done | bytes 262176 | tf_op jit(solution)/shard_map/all_to_all | solution.py:431
  103.6 0.8 fusion
Async XLA Ops:
  3.5 21.5 %all-to-all-start = ((bf16[32,80,128]{2,1,0:T(8,128)(2,1)}), bf16[32,80,128]{2,1,0:T(8,128)(2,1)S(1)}, u32[]{:S(2)}, u32[]{:S(2)}) async-start(bf16[32,80,128]{2,1,0:T(8,128)(2,1)} %get-tuple-element.24), calls=%async_computation | async-start | bytes 1310720 | tf_op jit(solution)/shard_map/all_to_all | solution.py:431
  30.7 12.5 %all-to-all-start.1 = ((f32[32,8,128]{2,1,0:T(8,128)}), f32[32,8,128]{2,1,0:T(8,128)}, u32[]{:S(2)}, u32[]{:S(2)}) async-start(f32[32,8,128]{2,1,0:T(8,128)} %get-tuple-element.26), calls=%async_computation.1 | async-start | bytes 262144 | tf_op jit(solution)/shard_map/all_to_all | solution.py:431
  48.4 17.5 %all-to-all-start.2 = ((bf16[32,64,128]{2,1,0:T(8,128)(2,1)}), bf16[32,64,128]{2,1,0:T(8,128)(2,1)S(1)}, u32[]{:S(2)}, u32[]{:S(2)}) async-start(bf16[32,64,128]{2,1,0:T(8,128)(2,1)} %get-tuple-element.35), calls=%async_computation.2 | async-start | bytes 1048576 | tf_op jit(solution)/shard_map/all_to_all | solution.py:431
  54.4 38.1 %copy-start = (f32[2,128]{1,0:T(2,128)S(1)}, f32[2,128]{1,0:T(2,128)}, u32[]{:S(2)}) copy-start(f32[2,128]{1,0:T(2,128)} %get-tuple-element.34) | copy-start | bytes 3076
  88.2 15.4 %all-to-all-start.4 = ((bf16[128,8,128]{2,1,0:T(8,128)(2,1)}), bf16[128,8,128]{2,1,0:T(8,128)(2,1)S(1)}, u32[]{:S(2)}, u32[]{:S(2)}) async-start(bf16[128,8,128]{2,1,0:T(8,128)(2,1)} %reduce.3), calls=%async_computation.4 | async-start | bytes 524288 | tf_op jit(solution)/shard_map/all_to_all | solution.py:431

commit v3 on v2

--- a/solution.py
+++ b/solution.py
@@ -22,11 +22,12 @@
 WIDE = CAP * PLEN
 QROWS = 2 * QLEN
 META = 16
-CHUNK = 4
+CHUNK = 16
+GROUP = 16
 TOKENS = STORED * PLEN
 BLOCK = 1536
 STEPS = TOKENS // BLOCK
-LANES = 4
+LANES = 1
 PART = 768
 PARTS = TOKENS // PART
 AHEAD = 3
@@ -157,27 +158,29 @@
     return copies
 
 
-def encode_kernel(hidden_hbm, weight_hbm, proj_hbm, embed_ref, hidden_ref, weight_ref, proj_ref, sems, out_sems):
+def encode_kernel(hidden_hbm, weight_hbm, embed_ref, inverse_hbm, hidden_ref, weight_ref, inverse_ref, sems, out_sem):
     weight_copy = pltpu.make_async_copy(weight_hbm, weight_ref, sems.at[PARTS])
     weight_copy.start()
     copies = token_copies(hidden_hbm, hidden_ref, sems)
     for copy in copies[:AHEAD]:
         copy.start()
     weight_copy.wait()
-    outs = []
+    packed = jnp.zeros((DIM, DIM), F32)
+    lane = iota((DIM, DIM), 1)
     for i, copy in enumerate(copies):
         rows = pl.ds(i * PART, PART)
         copy.wait()
         if i + AHEAD < PARTS:
             copies[i + AHEAD].start()
         proj = dot(hidden_ref[rows, :], weight_ref[...])
-        proj_ref[rows, :] = proj
-        outs.append(pltpu.make_async_copy(proj_ref.at[rows], proj_hbm.at[rows], out_sems.at[i]))
-        outs[-1].start()
         inverse = lax.rsqrt(jnp.sum(proj * proj, axis=-1, keepdims=True) + EPS)
         embed_ref[rows, :] = (proj * inverse).astype(BF)
-    for out in outs:
-        out.wait()
+        for j in range(PART // DIM):
+            packed = jnp.where(lane == i * (PART // DIM) + j, inverse[j * DIM : (j + 1) * DIM], packed)
+    inverse_ref[...] = packed
+    out = pltpu.make_async_copy(inverse_ref, inverse_hbm, out_sem)
+    out.start()
+    out.wait()
 
 
 def stored_rows(embed_ref, place_ref, s):
@@ -188,9 +191,10 @@
     return jnp.concatenate(parts, axis=0)
 
 
-def score_kernel(recv_ref, embed_ref, expo_hbm, recip_hbm, sums_ref, table_hbm, second_hbm, place_hbm,
+def score_kernel(recv_ref, embed_ref, expo_hbm, recip_hbm, sums_ref, table_hbm, second_hbm, place_hbm, queries_hbm,
                  recip_ref, table_ref, second_ref, place_ref, meta_ref, limit_ref, expo_ref, round_ref,
                  smem_ref, sem, expo_sems, out_sems):
+    outs = start_copies(((recv_ref.at[:, pl.ds(0, QROWS)], queries_hbm),), out_sems.at[pl.ds(4, 1)])
     for s in range(N_DEV):
         rows = recv_ref[s, QROWS : QROWS + META, :].astype(F32)
         meta_ref[s : s + 1, :] = rows[0:1, :]
@@ -198,7 +202,7 @@
     place_ref[...] = meta.astype(jnp.int32) * PLEN
     copy = pltpu.make_async_copy(place_ref, smem_ref, sem)
     copy.start()
-    outs = start_copies(((place_ref, place_hbm),), out_sems)
+    outs += start_copies(((place_ref, place_hbm),), out_sems)
     meta_bf = meta.astype(BF)
     spread = expander(1)
     second_ref[...] = dot(pltpu.roll(meta, DIM - SLOTS, 1).astype(BF), spread.astype(BF))
@@ -272,45 +276,33 @@
     )
 
 
-def ahead_kernel(recv_ref, second_hbm, expo_hbm, recip_hbm, weights_ref, turned_hbm,
-                 second_ref, recip_ref, expo_ref, turned_ref, small_sems, sems, out_sems):
-    small = start_copies(((recip_hbm, recip_ref), (second_hbm, second_ref)), small_sems)
-    steps = N_DEV // CHUNK
-    span = CHUNK * QLEN
+def ahead_kernel(expo_hbm, recip_hbm, weights_ref, recip_ref, expo_ref, sems):
+    steps = N_DEV // GROUP
+    span = GROUP * QLEN
     fetch = []
     for i in range(steps):
         rows = pl.ds(i * span, span)
-        fetch.append(pltpu.make_async_copy(expo_hbm.at[rows], expo_ref.at[rows], sems.at[i]))
-        fetch[-1].start()
+        fetch.append(
+            start_copies(
+                ((recip_hbm.at[rows], recip_ref.at[rows]), (expo_hbm.at[rows], expo_ref.at[rows])), sems.at[i]
+            )
+        )
     spread = expander(2).astype(BF)
     lane = iota((span, DIM), 1)
-    outs = []
-    wait_copies(small)
     for i in range(steps):
         rows = pl.ds(i * span, span)
+        wait_copies(fetch[i])
         recip = recip_ref[rows, :]
         hi = recip.astype(BF).astype(F32)
         lo = recip - hi
         factor = jnp.where(lane < SLOTS, hi, jnp.where(lane < 2 * SLOTS, pltpu.roll(lo, SLOTS, 1), 0.0))
-        wide = dot(factor.astype(BF), spread)
-        fetch[i].wait()
-        weights = expo_ref[rows, :] * wide
-        weights_ref[rows, :] = weights.astype(BF)
-        for u in range(CHUNK):
-            s = i * CHUNK + u
-            second = second_ref[s : s + 1, :] > 0.5
-            both = halves(weights[u * QLEN : (u + 1) * QLEN], second)
-            turned_ref[s] = dot(both, recv_ref[s, 0:QROWS, :], ROWS_ROWS).astype(BF)
-        part = pl.ds(i * CHUNK, CHUNK)
-        outs.append(pltpu.make_async_copy(turned_ref.at[part], turned_hbm.at[part], out_sems.at[i]))
-        outs[-1].start()
-    for out in outs:
-        out.wait()
+        weights_ref[rows, :] = (expo_ref[rows, :] * dot(factor.astype(BF), spread)).astype(BF)
 
 
 def query_kernel(sums_ref, const_hbm, me_ref, table_hbm, second_hbm, weights_ref, embed_ref, place_hbm,
-                 send_ref, pull_hbm, loss_hbm,
-                 const_ref, table_ref, second_ref, pull_ref, loss_ref, wide_ref, smem_ref, sems, out_sems):
+                 send_hbm, mixed_hbm, loss_hbm,
+                 const_ref, table_ref, second_ref, loss_ref, wide_ref, send_ref, mixed_ref, smem_ref,
+                 sems, out_sems, part_sems):
     small = start_copies(
         ((table_hbm, table_ref), (place_hbm, smem_ref), (const_hbm, const_ref), (second_hbm, second_ref)), sems
     )
@@ -323,79 +315,102 @@
     loss_ref[...] = jnp.broadcast_to(jnp.sum(picked, axis=-1, keepdims=True), (2, DIM))
     normal = jnp.where(table_ref[2] > 0.5, turned[:, 1:2], turned[:, 0:1])
     pull = LOSS_SCALE * (table_ref[0] / normal - table_ref[1])
-    pull_ref[...] = pull
-    outs = start_copies(((pull_ref, pull_hbm), (loss_ref, loss_hbm)), out_sems)
+    outs = start_copies(((loss_ref, loss_hbm),), out_sems)
     hi = pull.astype(BF).astype(F32)
     lo = pull - hi
     lane = iota((N_DEV, DIM), 1)
     factor = jnp.where(lane < SLOTS, hi, jnp.where(lane < 2 * SLOTS, pltpu.roll(lo, SLOTS, 1), 0.0))
     wide_ref[...] = dot(factor.astype(BF), expander(2).astype(BF))
 
+    def part_copies(i):
+        some = pl.ds(i * CHUNK, CHUNK)
+        rows = pl.ds(i * (CHUNK * QLEN), CHUNK * QLEN)
+        return [
+            pltpu.make_async_copy(send_ref.at[some], send_hbm.at[some], part_sems.at[i, 0]),
+            pltpu.make_async_copy(mixed_ref.at[rows], mixed_hbm.at[rows], part_sems.at[i, 1]),
+        ]
+
     def chunk(i, carry):
         for u in range(CHUNK):
             s = i * CHUNK + u
             rows = pl.ds(pl.multiple_of(s * QLEN, QLEN), QLEN)
             mixed = weights_ref[rows, :].astype(F32) * wide_ref[pl.ds(s, 1), :]
+            mixed_ref[rows, :] = mixed.astype(BF)
             both = halves(mixed, second_ref[pl.ds(s, 1), :] > 0.5)
             send_ref[s] = dot(both, stored_rows(embed_ref, smem_ref, s)).astype(BF)
+        for copy in part_copies(i):
+            copy.start()
         return carry
 
     lax.fori_loop(0, N_DEV // CHUNK, chunk, 0)
     wait_copies(outs)
-
-
-def stored_kernel(place_hbm, pull_hbm, hidden_hbm, proj_hbm, turned_hbm, preact_ref, head_ref,
-                  hidden_ref, proj_ref, turned_ref, delta_ref, place_smem, pull_smem, smem_sems,
-                  sems, turned_sems, proj_sem):
-    steps = N_DEV // CHUNK
-    scalars = start_copies(((place_hbm, place_smem), (pull_hbm, pull_smem)), smem_sems)
+    for i in range(N_DEV // CHUNK):
+        wait_copies(part_copies(i))
+
+
+def stored_kernel(place_hbm, queries_hbm, second_hbm, mixed_hbm, inverse_hbm, hidden_hbm, embed_ref,
+                  preact_hbm, head_ref,
+                  preact_ref, hidden_ref, queries_ref, second_ref, mixed_ref, inverse_ref, delta_ref, place_smem,
+                  sems, small_sems, mixed_sems, out_sems):
+    steps = N_DEV // GROUP
+    small = start_copies(
+        ((place_hbm, place_smem), (second_hbm, second_ref), (queries_hbm, queries_ref), (inverse_hbm, inverse_ref)),
+        small_sems,
+    )
     fetch = []
     for i in range(steps):
-        part = pl.ds(i * CHUNK, CHUNK)
-        fetch.append(pltpu.make_async_copy(turned_hbm.at[part], turned_ref.at[part], turned_sems.at[i]))
-        fetch[-1].start()
-    proj_copy = pltpu.make_async_copy(proj_hbm, proj_ref, proj_sem)
-    proj_copy.start()
+        rows = pl.ds(i * GROUP * QLEN, GROUP * QLEN)
+        fetch += start_copies(((mixed_hbm.at[rows], mixed_ref.at[rows]),), mixed_sems.at[pl.ds(i, 1)])
     copies = token_copies(hidden_hbm, hidden_ref, sems)
-    for copy in copies:
-        copy.start()
     delta_ref[...] = jnp.zeros_like(delta_ref)
-    wait_copies(scalars)
-
-    def add(s, carry):
-        for k in range(CAP):
-            at = pl.ds(pl.multiple_of(place_smem[s, k], 16), PLEN)
-            part = turned_ref[s, k * PLEN : (k + 1) * PLEN, :].astype(F32)
-            delta_ref[k % LANES, at, :] += part * pull_smem[s, k]
-        return carry
+    wait_copies(small)
 
     for i in range(steps):
         fetch[i].wait()
-        lax.fori_loop(i * CHUNK, (i + 1) * CHUNK, add, 0)
-    proj_copy.wait()
+        for copy in copies[i * PARTS // steps : (i + 1) * PARTS // steps]:
+            copy.start()
+        for s in range(i * GROUP, (i + 1) * GROUP):
+            both = halves(mixed_ref[s * QLEN : (s + 1) * QLEN, :].astype(F32), second_ref[s : s + 1, :] > 0.5)
+            part = dot(both, queries_ref[s], ROWS_ROWS)
+            for k in range(CAP):
+                at = pl.ds(pl.multiple_of(place_smem[s, k], 16), PLEN)
+                delta_ref[k % LANES, at, :] += part[k * PLEN : (k + 1) * PLEN]
     total = jnp.zeros((DIM, D), F32)
+    outs = []
     for i in range(STEPS):
         rows = pl.ds(i * BLOCK, BLOCK)
-        proj = proj_ref[rows, :]
+        unit = embed_ref[rows, :].astype(F32)
         delta = jnp.sum(delta_ref[:, rows, :], axis=0)
-        inverse = lax.rsqrt(jnp.sum(proj * proj, axis=-1, keepdims=True) + EPS)
-        unit = proj * inverse
         radial = jnp.sum(unit * delta, axis=-1, keepdims=True)
-        preact = ((delta - unit * radial) * inverse).astype(BF)
+        tangent = delta - unit * radial
+        scaled = []
+        for j in range(BLOCK // DIM):
+            b = i * (BLOCK // DIM) + j
+            scaled.append(tangent[j * DIM : (j + 1) * DIM] * inverse_ref[:, b : b + 1])
+        preact = jnp.concatenate(scaled, axis=0).astype(BF)
         preact_ref[rows, :] = preact
+        outs += start_copies(((preact_ref.at[rows], preact_hbm.at[rows]),), out_sems.at[pl.ds(i, 1)])
         for j in range(i * BLOCK // PART, (i + 1) * BLOCK // PART):
             copies[j].wait()
         total = total + dot(preact, hidden_ref[rows, :], ROWS_ROWS)
     head_ref[...] = jnp.transpose(total)
-
-
-def back_kernel(preact_ref, weight_ref, grad_ref):
+    wait_copies(outs)
+
+
+def back_kernel(preact_ref, weight_ref, after_ref, grad_ref):
     grad_ref[...] = dot(preact_ref[...], weight_ref[...], COLS_COLS).astype(BF)
 
 
-def finish_kernel(recv_ref, hidden_hbm, weight_hbm, proj_hbm, head_ref, grad_ref, send_ref,
-                  hidden_ref, weight_ref, proj_ref, sems):
-    copies = start_copies(((proj_hbm, proj_ref), (hidden_hbm, hidden_ref), (weight_hbm, weight_ref)), sems)
+def query_back_kernel(preact_ref, weight_hbm, after_ref, grad_ref, weight_ref, sem):
+    copy = pltpu.make_async_copy(weight_hbm, weight_ref, sem)
+    copy.start()
+    copy.wait()
+    grad_ref[...] = dot(preact_ref[...], weight_ref[...], COLS_COLS).astype(BF)
+
+
+def finish_kernel(recv_ref, hidden_hbm, proj_hbm, head_ref, preact_ref, send_ref,
+                  hidden_ref, proj_ref, sems):
+    copies = start_copies(((proj_hbm, proj_ref), (hidden_hbm, hidden_ref)), sems)
     delta = jnp.sum(recv_ref[...].astype(F32), axis=0)
     copies[0].wait()
     proj = proj_ref[...]
@@ -403,14 +418,14 @@
     unit = proj * inverse
     radial = jnp.sum(unit * delta, axis=-1, keepdims=True)
     preact = ((delta - unit * radial) * inverse).astype(BF)
+    preact_ref[...] = preact
     wait_copies(copies[1:])
-    grad_ref[...] = dot(preact, weight_ref[...], COLS_COLS).astype(BF)
     head = head_ref[...] + dot(hidden_ref[...], preact, ROWS_ROWS)
     send_ref[0:HEAD_TILES] = head.reshape(HEAD_TILES, 8, DIM).astype(BF)
     send_ref[HEAD_TILES:N_ALL] = jnp.zeros((N_ALL - HEAD_TILES, 8, DIM), BF)
 
 
-def reduce_kernel(recv_ref, send_ref):
+def reduce_kernel(recv_ref, after_ref, send_ref):
     total = jnp.sum(recv_ref[...].astype(F32), axis=0).astype(BF)
     send_ref[...] = jnp.broadcast_to(total[None], (N_ALL, 8, DIM))
 
@@ -467,24 +482,24 @@
     )(query_flat, head_weight, in_hbm(teacher), in_hbm(candidates), in_hbm(storage), in_hbm(lengths))
     recv = exchange(send, "dev")
 
-    proj, embed = pl.pallas_call(
+    embed, inverse = pl.pallas_call(
         encode_kernel,
-        out_shape=(pltpu.HBM((TOKENS, DIM), F32), pltpu.VMEM((TOKENS, DIM), BF)),
+        out_shape=(pltpu.VMEM((TOKENS, DIM), BF), pltpu.HBM((DIM, DIM), F32)),
         in_specs=[HBM, HBM],
-        out_specs=(HBM, VMEM),
+        out_specs=(VMEM, HBM),
         scratch_shapes=[
             pltpu.VMEM((TOKENS, D), BF),
             pltpu.VMEM((D, DIM), BF),
-            pltpu.VMEM((TOKENS, DIM), F32),
+            pltpu.VMEM((DIM, DIM), F32),
             pltpu.SemaphoreType.DMA((PARTS + 1,)),
-            pltpu.SemaphoreType.DMA((PARTS,)),
+            pltpu.SemaphoreType.DMA,
         ],
         cost_estimate=estimate(2 * TOKENS * D * DIM, 15_000_000),
         compiler_params=params(20),
         name="encode",
     )(flat_hidden, head_weight)
 
-    expo, recip, sums, table, second, place = pl.pallas_call(
+    expo, recip, sums, table, second, place, queries = pl.pallas_call(
         score_kernel,
         out_shape=(
             pltpu.HBM((N_DEV * QLEN, WIDE), F32),
@@ -493,9 +508,10 @@
             pltpu.HBM((3, N_DEV, DIM), F32),
             pltpu.HBM((N_DEV, WIDE), F32),
             pltpu.HBM((N_DEV, DIM), jnp.int32),
+            pltpu.HBM((N_DEV, QROWS, DIM), BF),
         ),
         in_specs=[VMEM] * 2,
-        out_specs=(HBM, HBM, VMEM, HBM, HBM, HBM),
+        out_specs=(HBM, HBM, VMEM, HBM, HBM, HBM, HBM),
         scratch_shapes=[
             pltpu.VMEM((N_DEV * QLEN, DIM), F32),
             pltpu.VMEM((3, N_DEV, DIM), F32),
@@ -508,52 +524,50 @@
             pltpu.SMEM((N_DEV, DIM), jnp.int32),
             pltpu.SemaphoreType.DMA,
             pltpu.SemaphoreType.DMA((N_DEV // CHUNK,)),
-            pltpu.SemaphoreType.DMA((4,)),
+            pltpu.SemaphoreType.DMA((5,)),
         ],
         compiler_params=params(14),
         name="score",
     )(recv, in_vmem(embed))
     all_sums = exchange(sums, "dev")
 
-    weights, turned = pl.pallas_call(
+    weights = pl.pallas_call(
         ahead_kernel,
-        out_shape=(pltpu.VMEM((N_DEV * QLEN, WIDE), BF), pltpu.HBM((N_DEV, WIDE, DIM), BF)),
-        in_specs=[VMEM, HBM, HBM, HBM],
-        out_specs=(VMEM, HBM),
+        out_shape=pltpu.VMEM((N_DEV * QLEN, WIDE), BF),
+        in_specs=[HBM, HBM],
+        out_specs=VMEM,
         scratch_shapes=[
-            pltpu.VMEM((N_DEV, WIDE), F32),
             pltpu.VMEM((N_DEV * QLEN, DIM), F32),
             pltpu.VMEM((N_DEV * QLEN, WIDE), F32),
-            pltpu.VMEM((N_DEV, WIDE, DIM), BF),
-            pltpu.SemaphoreType.DMA((2,)),
-            pltpu.SemaphoreType.DMA((N_DEV // CHUNK,)),
-            pltpu.SemaphoreType.DMA((N_DEV // CHUNK,)),
+            pltpu.SemaphoreType.DMA((N_DEV // GROUP, 2)),
         ],
         cost_estimate=estimate(2 * TOKENS * D * DIM, 15_000_000),
-        compiler_params=params(22),
+        compiler_params=params(12),
         name="ahead",
-    )(recv, in_hbm(second), in_hbm(expo), in_hbm(recip))
+    )(in_hbm(expo), in_hbm(recip))
 
     me = lax.axis_index("dev").astype(jnp.int32).reshape(1)
-    send_delta, pull, loss = pl.pallas_call(
+    send_delta, mixed, loss = pl.pallas_call(
         query_kernel,
         out_shape=(
-            shape((N_DEV, QROWS, DIM), BF),
-            pltpu.HBM((N_DEV, DIM), F32),
+            pltpu.HBM((N_DEV, QROWS, DIM), BF),
+            pltpu.HBM((N_DEV * QLEN, WIDE), BF),
             pltpu.HBM((2, DIM), F32),
         ),
         in_specs=[VMEM, HBM, SMEM, HBM, HBM, VMEM, VMEM, HBM],
-        out_specs=(VMEM, HBM, HBM),
+        out_specs=(HBM, HBM, HBM),
         scratch_shapes=[
             pltpu.VMEM((8, DIM), F32),
             pltpu.VMEM((3, N_DEV, DIM), F32),
             pltpu.VMEM((N_DEV, WIDE), F32),
-            pltpu.VMEM((N_DEV, DIM), F32),
             pltpu.VMEM((2, DIM), F32),
             pltpu.VMEM((N_DEV, WIDE), F32),
+            pltpu.VMEM((N_DEV, QROWS, DIM), BF),
+            pltpu.VMEM((N_DEV * QLEN, WIDE), BF),
             pltpu.SMEM((N_DEV, DIM), jnp.int32),
             pltpu.SemaphoreType.DMA((4,)),
-            pltpu.SemaphoreType.DMA((2,)),
+            pltpu.SemaphoreType.DMA((1,)),
+            pltpu.SemaphoreType.DMA((N_DEV // CHUNK, 2)),
         ],
         compiler_params=params(12),
         name="query",
@@ -562,64 +576,78 @@
 
     preact, head = pl.pallas_call(
         stored_kernel,
-        out_shape=(pltpu.VMEM((TOKENS, DIM), BF), pltpu.VMEM((D, DIM), F32)),
-        in_specs=[HBM] * 5,
-        out_specs=(VMEM, VMEM),
+        out_shape=(pltpu.HBM((TOKENS, DIM), BF), pltpu.VMEM((D, DIM), F32)),
+        in_specs=[HBM] * 6 + [VMEM],
+        out_specs=(HBM, VMEM),
         scratch_shapes=[
+            pltpu.VMEM((TOKENS, DIM), BF),
             pltpu.VMEM((TOKENS, D), BF),
-            pltpu.VMEM((TOKENS, DIM), F32),
-            pltpu.VMEM((N_DEV, WIDE, DIM), BF),
+            pltpu.VMEM((N_DEV, QROWS, DIM), BF),
+            pltpu.VMEM((N_DEV, WIDE), F32),
+            pltpu.VMEM((N_DEV * QLEN, WIDE), BF),
+            pltpu.VMEM((DIM, DIM), F32),
             pltpu.VMEM((LANES, TOKENS, DIM), F32),
             pltpu.SMEM((N_DEV, DIM), jnp.int32),
-            pltpu.SMEM((N_DEV, DIM), F32),
-            pltpu.SemaphoreType.DMA((2,)),
             pltpu.SemaphoreType.DMA((PARTS,)),
-            pltpu.SemaphoreType.DMA((N_DEV // CHUNK,)),
-            pltpu.SemaphoreType.DMA,
+            pltpu.SemaphoreType.DMA((4,)),
+            pltpu.SemaphoreType.DMA((N_DEV // GROUP,)),
+            pltpu.SemaphoreType.DMA((STEPS,)),
         ],
         cost_estimate=estimate(4 * TOKENS * D * DIM, 20_000_000),
         compiler_params=params(40),
         name="stored",
-    )(in_hbm(place), in_hbm(pull), flat_hidden, in_hbm(proj), in_hbm(turned))
-
-    query_grad, send_head = pl.pallas_call(
+    )(
+        in_hbm(place), in_hbm(queries), in_hbm(second), in_hbm(mixed), in_hbm(inverse), flat_hidden, in_vmem(embed)
+    )
+
+    query_preact, send_head = pl.pallas_call(
         finish_kernel,
-        out_shape=(shape((QROWS, D), BF), shape((N_ALL, 8, DIM), BF)),
-        in_specs=[VMEM, HBM, HBM, HBM, VMEM],
+        out_shape=(pltpu.VMEM((QROWS, DIM), BF), shape((N_ALL, 8, DIM), BF)),
+        in_specs=[VMEM, HBM, HBM, VMEM],
         out_specs=(VMEM,) * 2,
         scratch_shapes=[
             pltpu.VMEM((QROWS, D), BF),
-            pltpu.VMEM((D, DIM), BF),
             pltpu.VMEM((QROWS, DIM), F32),
-            pltpu.SemaphoreType.DMA((3,)),
+            pltpu.SemaphoreType.DMA((2,)),
         ],
         compiler_params=params(8),
         name="finish",
-    )(recv_delta, query_flat, head_weight, in_hbm(query_proj), in_vmem(head))
+    )(recv_delta, query_flat, in_hbm(query_proj), in_vmem(head))
     recv_head = exchange(send_head, ("group", "dev"))
 
     passage_grad = pl.pallas_call(
         back_kernel,
         grid=(STEPS,),
-        out_shape=shape((TOKENS, D), BF),
+        out_shape=pltpu.HBM((TOKENS, D), BF),
         in_specs=[
             pl.BlockSpec((BLOCK, DIM), lambda i: (i, 0)),
             pl.BlockSpec((D, DIM), lambda i: (0, 0)),
+            pl.BlockSpec(memory_space=pl.ANY),
         ],
         out_specs=pl.BlockSpec((BLOCK, D), lambda i: (i, 0)),
         cost_estimate=estimate(2 * TOKENS * D * DIM, 15_000_000),
         compiler_params=params(20),
         name="back",
-    )(in_vmem(preact), head_weight)
+    )(in_hbm(preact), head_weight, query_preact)
 
     send_total = pl.pallas_call(
         reduce_kernel,
         out_shape=shape((N_ALL, 8, DIM), BF),
-        in_specs=[VMEM],
+        in_specs=[VMEM, pl.BlockSpec(memory_space=pl.ANY)],
         out_specs=VMEM,
         compiler_params=params(4),
         name="reduce",
-    )(recv_head)
+    )(recv_head, in_hbm(passage_grad))
+    query_grad = pl.pallas_call(
+        query_back_kernel,
+        out_shape=shape((QROWS, D), BF),
+        in_specs=[VMEM, HBM, pl.BlockSpec(memory_space=pl.ANY)],
+        out_specs=VMEM,
+        scratch_shapes=[pltpu.VMEM((D, DIM), BF), pltpu.SemaphoreType.DMA],
+        cost_estimate=estimate(2 * QROWS * D * DIM, 400_000),
+        compiler_params=params(4),
+        name="query_back",
+    )(query_preact, head_weight, send_total)
     head_all = exchange(send_total, ("group", "dev"))
     head_grad = head_all[:HEAD_TILES].reshape(D, DIM).astype(F32)
     return (

time: 105 us -> 99.4 us (0.947)
  blocking collectives: 19.5 us -> 0 us
  waiting for transfers between devices: 11.8 us -> 26.3 us
  Pallas kernels: 47.4 us -> 41.5 us
  starting transfers between devices: 23.6 us -> 28.8 us
    all_to_all x1 -> x0, blocking collectives: 19.5 us -> none  [exchange(): return lax.all_to_all(x, axes, split_axis=0, concat_axis=0, tiled=True)]
    all_to_all x4 -> x5, waiting for transfers between devices: 11.8 us -> 26.3 us  [exchange(): return lax.all_to_all(x, axes, split_axis=0, concat_axis=0, tiled=True)]
    all_to_all x4 -> x5, starting transfers between devices: 23.6 us -> 28.8 us  [exchange(): return lax.all_to_all(x, axes, split_axis=0, concat_axis=0, tiled=True)]
    pallas_call x6 -> x7, Pallas kernels: 38 us -> 33 us  [the longest x1 8.82 us: on_device(): pl.pallas_call(encode_kernel, out_shape=(pltpu.VMEM((TOKENS, DIM), BF), p...]
  transfers between devices with their start and end apart: 4 -> 5, of which waited for: 4 -> 5; matrix products, arithmetic and copies ran while one was open for 1% -> 1% of each run, Pallas kernels for 30% -> 28%
where the time goes in v3:
time: 99.4 us; the launch traced here: 98.7 us
  Pallas kernels  41.5 us (42%)
  starting transfers between devices  28.8 us (29%)
  waiting for transfers between devices  26.3 us (26%)
    all_to_all x5, starting transfers between devices, exchange(): return lax.all_to_all(x, axes, split_axis=0, concat_axis=0, tiled=True)  28.8 us
    all_to_all x5, waiting for transfers between devices, exchange(): return lax.all_to_all(x, axes, split_axis=0, concat_axis=0, tiled=True)  26.3 us
    pallas_call x1, Pallas kernels, on_device(): pl.pallas_call(encode_kernel, out_shape=(pltpu.VMEM((TOKENS, DIM), BF), p...  8.82 us
    pallas_call x1, Pallas kernels, on_device(): pl.pallas_call(stored_kernel, out_shape=(pltpu.HBM((TOKENS, DIM), BF), pl...  7.93 us
    pallas_call x1, Pallas kernels, on_device(): pl.pallas_call(back_kernel, grid=(STEPS,), out_shape=pltpu.HBM((TOKENS, D...  6.7 us
    pallas_call x1, Pallas kernels, on_device(): pl.pallas_call(score_kernel, out_shape=(pltpu.HBM((N_DEV * QLEN, WIDE), F...  4.79 us
    pallas_call x1, Pallas kernels, on_device(): pl.pallas_call(query_kernel, out_shape=(pltpu.HBM((N_DEV, QROWS, DIM), BF...  3.59 us
    pallas_call x1, Pallas kernels, on_device(): pl.pallas_call(request_kernel, out_shape=(shape((N_DEV, QROWS + META, DIM...  2.84 us
  transfers between devices with their start and end apart: 5, of which 5 were waited for; matrix products, arithmetic and copies ran while one was open for 1% of the time, Pallas kernels for 28%

profile of v3, /device:TPU:1, one launch (start us, length us, event | category | flops | bytes accessed | tf_op | source)
XLA Modules:
  0.0 98.7 jit_solution(8995043590467916400)
XLA Ops:
  0.6 2.8 %request.1 = (bf16[32,80,128]{2,1,0:T(8,128)(2,1)}, f32[64,128]{1,0:T(8,128)}, f32[8,128]{1,0:T(8,128)}) custom-call(bf16[64,768]{1,0:T(8,128)(2,1)} %bitcast.13, bf16[768,128]{1,0:T(8,128)(2,1)} %weight_hbm.5, f32[2,64]{1,0:T(2,128)} %teacher_hbm.1, s32[2,64]{1,0:T(2,128)} %cand_hbm.1, s32[1,4096]{1,0:T(1,128)} %storage_hbm.1, s32[1,4096]{1,0:T(1,128)} %lengths_hbm.1), custom_call_target="tpu_custom_call" | custom-call | tf_op jit(solution)/shard_map/request/pallas_call | solution.py:457
  3.5 8.6 %all-to-all-start = ((bf16[32,80,128]{2,1,0:T(8,128)(2,1)}), bf16[32,80,128]{2,1,0:T(8,128)(2,1)S(1)}, u32[]{:S(2)}, u32[]{:S(2)}) async-start(bf16[32,80,128]{2,1,0:T(8,128)(2,1)} %get-tuple-element.23), calls=%async_computation | async-start | bytes 1310720 | tf_op jit(solution)/shard_map/all_to_all | solution.py:446
  12.1 8.8 %encode.1 = (bf16[6144,128]{1,0:T(8,128)(2,1)S(1)}, f32[128,128]{1,0:T(8,128)}) custom-call(bf16[6144,768]{1,0:T(8,128)(2,1)} %bitcast.10, bf16[768,128]{1,0:T(8,128)(2,1)} %weight_hbm.5), custom_call_target="tpu_custom_call" | custom-call | flops 1207959552 | bytes 15000000 | tf_op jit(solution)/shard_map/encode/pallas_call | solution.py:485
  20.9 4.1 %all-to-all-done.recv_ref = bf16[32,80,128]{2,1,0:T(8,128)(2,1)S(1)} async-done(((bf16[32,80,128]{2,1,0:T(8,128)(2,1)}), bf16[32,80,128]{2,1,0:T(8,128)(2,1)S(1)}, u32[]{:S(2)}, u32[]{:S(2)}) %all-to-all-start) | async-done | bytes 655392 | tf_op jit(solution)/shard_map/all_to_all | solution.py:446
  25.0 4.8 %score.1 = (f32[1024,576]{1,0:T(8,128)}, f32[1024,128]{1,0:T(8,128)}, f32[32,8,128]{2,1,0:T(8,128)}, f32[3,32,128]{2,1,0:T(8,128)}, f32[32,576]{1,0:T(8,128)}, /...) custom-call(bf16[32,80,128]{2,1,0:T(8,128)(2,1)S(1)} %all-to-all-done.recv_ref, ...), custom_call_target="tpu_custom_call" | custom-call | tf_op jit(solution)/shard_map/score/pallas_call | solution.py:502
  29.8 4.1 %all-to-all-start.1 = ((f32[32,8,128]{2,1,0:T(8,128)}), f32[32,8,128]{2,1,0:T(8,128)S(1)}, u32[]{:S(2)}, u32[]{:S(2)}) async-start(f32[32,8,128]{2,1,0:T(8,128)} %get-tuple-element.25), calls=%async_computation.1 | async-start | bytes 262144 | tf_op jit(solution)/shard_map/all_to_all | solution.py:446
  33.9 2.3 %ahead.1.weights_ref = bf16[1024,576]{1,0:T(8,128)(2,1)S(1)} custom-call(f32[1024,576]{1,0:T(8,128)} %get-tuple-element.29.expo_hbm, f32[1024,128]{1,0:T(8,128)} %get-tuple-element.30.recip_hbm), custom_call_target="tpu_custom_call" | custom-call | flops 1207959552 | bytes 15000000 | tf_op jit(solution)/shard_map/ahead/pallas_call | solution.py:534
  36.2 5.4 %all-to-all-done.1.sums_ref = f32[32,8,128]{2,1,0:T(8,128)S(1)} async-done(((f32[32,8,128]{2,1,0:T(8,128)}), f32[32,8,128]{2,1,0:T(8,128)S(1)}, u32[]{:S(2)}, u32[]{:S(2)}) %all-to-all-start.1) | async-done | bytes 131104 | tf_op jit(solution)/shard_map/all_to_all | solution.py:446
  41.6 3.6 %query.1 = (bf16[32,64,128]{2,1,0:T(8,128)(2,1)}, bf16[1024,576]{1,0:T(8,128)(2,1)}, f32[2,128]{1,0:T(2,128)}) custom-call(f32[32,8,128]{2,1,0:T(8,128)S(1)} %all-to-all-done.1.sums_ref, f32[8,128]{1,0:T(8,128)} %get-tuple-element.26.const_hbm, s32[1]{0:T(128)} %bitcast.2.me_ref, f32[3,32,128]{2,1,0:T(8,128)} %get-tuple-element.27.table_hbm, ...), custom_call_target="tpu_custom_call" | custom-call | tf_op jit(solution)/shard_map/query/pallas_call | solution.py:550
  45.2 4.0 %all-to-all-start.2 = ((bf16[32,64,128]{2,1,0:T(8,128)(2,1)}), bf16[32,64,128]{2,1,0:T(8,128)(2,1)S(1)}, u32[]{:S(2)}, u32[]{:S(2)}) async-start(bf16[32,64,128]{2,1,0:T(8,128)(2,1)} %get-tuple-element.33), calls=%async_computation.2 | async-start | bytes 1048576 | tf_op jit(solution)/shard_map/all_to_all | solution.py:446
  49.2 7.9 %stored.1 = (bf16[6144,128]{1,0:T(8,128)(2,1)}, f32[768,128]{1,0:T(8,128)S(1)}) custom-call(s32[32,128]{1,0:T(8,128)} %get-tuple-element.31.place_hbm, bf16[32,64,128]{2,1,0:T(8,128)(2,1)} %get-tuple-element.35.queries_hbm, f32[32,576]{1,0:T(8,128)} %get-tuple-element.28.second_hbm, bf16[1024,576]{1,0:T(8,128)(2,1)} %get-tuple-element.36.mixed_hbm, ...), custom_call_target="tpu_custom_call" | custom-call | flops 2415919104 | bytes 20000000 | tf_op jit(solution)/shard_map/stored/pallas_call | solution.py:577
  57.1 3.7 %all-to-all-done.2.recv_ref = bf16[32,64,128]{2,1,0:T(8,128)(2,1)S(1)} async-done(((bf16[32,64,128]{2,1,0:T(8,128)(2,1)}), bf16[32,64,128]{2,1,0:T(8,128)(2,1)S(1)}, u32[]{:S(2)}, u32[]{:S(2)}) %all-to-all-start.2) | async-done | bytes 524320 | tf_op jit(solution)/shard_map/all_to_all | solution.py:446
  60.8 1.9 %finish.1 = (bf16[64,128]{1,0:T(8,128)(2,1)S(1)}, bf16[128,8,128]{2,1,0:T(8,128)(2,1)}) custom-call(bf16[32,64,128]{2,1,0:T(8,128)(2,1)S(1)} %all-to-all-done.2.recv_ref, bf16[64,768]{1,0:T(8,128)(2,1)} %bitcast.14, f32[64,128]{1,0:T(8,128)} %get-tuple-element.34.proj_hbm, f32[768,128]{1,0:T(8,128)S(1)} %get-tuple-element.38.head_ref), custom_call_target="tpu_custom_call" | custom-call | tf_op jit(solution)/shard_map/finish/pallas_call | solution.py:603
  62.7 6.8 %all-to-all-start.3 = ((bf16[128,8,128]{2,1,0:T(8,128)(2,1)}), bf16[128,8,128]{2,1,0:T(8,128)(2,1)S(1)}, u32[]{:S(2)}, u32[]{:S(2)}) async-start(bf16[128,8,128]{2,1,0:T(8,128)(2,1)} %get-tuple-element.39), calls=%async_computation.3 | async-start | bytes 524288 | tf_op jit(solution)/shard_map/all_to_all | solution.py:446
  69.5 6.7 %back.1.after_ref = bf16[6144,768]{1,0:T(8,128)(2,1)} custom-call(bf16[6144,128]{1,0:T(8,128)(2,1)} %get-tuple-element.40.preact_ref, bf16[768,128]{1,0:T(8,128)(2,1)} %weight_hbm.5, bf16[64,128]{1,0:T(8,128)(2,1)S(1)} %get-tuple-element.41.after_ref.preact_ref), custom_call_target="tpu_custom_call" | custom-call | flops 1207959552 | bytes 15000000 | tf_op jit(solution)/shard_map/back/pallas_call | solution.py:618
  76.2 0.0 copy-start
  76.2 4.4 %all-to-all-done.3.recv_ref = bf16[128,8,128]{2,1,0:T(8,128)(2,1)S(1)} async-done(((bf16[128,8,128]{2,1,0:T(8,128)(2,1)}), bf16[128,8,128]{2,1,0:T(8,128)(2,1)S(1)}, u32[]{:S(2)}, u32[]{:S(2)}) %all-to-all-start.3) | async-done | bytes 262176 | tf_op jit(solution)/shard_map/all_to_all | solution.py:446
  80.6 0.9 reduce.3.after_ref
  81.5 5.4 %all-to-all-start.4 = ((bf16[128,8,128]{2,1,0:T(8,128)(2,1)}), bf16[128,8,128]{2,1,0:T(8,128)(2,1)S(1)}, u32[]{:S(2)}, u32[]{:S(2)}) async-start(bf16[128,8,128]{2,1,0:T(8,128)(2,1)} %reduce.3.after_ref), calls=%async_computation.4 | async-start | bytes 524288 | tf_op jit(solution)/shard_map/all_to_all | solution.py:446
  86.9 0.0 copy-done
  86.9 0.6 slice_reduce_fusion
  87.5 1.8 %query_back.1 = bf16[64,768]{1,0:T(8,128)(2,1)} custom-call(bf16[64,128]{1,0:T(8,128)(2,1)S(1)} %get-tuple-element.41.after_ref.preact_ref, bf16[768,128]{1,0:T(8,128)(2,1)} %weight_hbm.5, bf16[128,8,128]{2,1,0:T(8,128)(2,1)} %reduce.3.after_ref), custom_call_target="tpu_custom_call" | custom-call | flops 12582912 | bytes 400000 | tf_op jit(solution)/shard_map/query_back/pallas_call | solution.py:641
  89.3 8.7 %all-to-all-done.4 = bf16[128,8,128]{2,1,0:T(8,128)(2,1)S(1)} async-done(((bf16[128,8,128]{2,1,0:T(8,128)(2,1)}), bf16[128,8,128]{2,1,0:T(8,128)(2,1)S(1)}, u32[]{:S(2)}, u32[]{:S(2)}) %all-to-all-start.4) | async-done | bytes 262176 | tf_op jit(solution)/shard_map/all_to_all | solution.py:446
  98.0 0.8 fusion
Async XLA Ops:
  3.5 21.5 %all-to-all-start = ((bf16[32,80,128]{2,1,0:T(8,128)(2,1)}), bf16[32,80,128]{2,1,0:T(8,128)(2,1)S(1)}, u32[]{:S(2)}, u32[]{:S(2)}) async-start(bf16[32,80,128]{2,1,0:T(8,128)(2,1)} %get-tuple-element.23), calls=%async_computation | async-start | bytes 1310720 | tf_op jit(solution)/shard_map/all_to_all | solution.py:446
  29.8 11.8 %all-to-all-start.1 = ((f32[32,8,128]{2,1,0:T(8,128)}), f32[32,8,128]{2,1,0:T(8,128)S(1)}, u32[]{:S(2)}, u32[]{:S(2)}) async-start(f32[32,8,128]{2,1,0:T(8,128)} %get-tuple-element.25), calls=%async_computation.1 | async-start | bytes 262144 | tf_op jit(solution)/shard_map/all_to_all | solution.py:446
  45.2 15.6 %all-to-all-start.2 = ((bf16[32,64,128]{2,1,0:T(8,128)(2,1)}), bf16[32,64,128]{2,1,0:T(8,128)(2,1)S(1)}, u32[]{:S(2)}, u32[]{:S(2)}) async-start(bf16[32,64,128]{2,1,0:T(8,128)(2,1)} %get-tuple-element.33), calls=%async_computation.2 | async-start | bytes 1048576 | tf_op jit(solution)/shard_map/all_to_all | solution.py:446
  62.7 17.9 %all-to-all-start.3 = ((bf16[128,8,128]{2,1,0:T(8,128)(2,1)}), bf16[128,8,128]{2,1,0:T(8,128)(2,1)S(1)}, u32[]{:S(2)}, u32[]{:S(2)}) async-start(bf16[128,8,128]{2,1,0:T(8,128)(2,1)} %get-tuple-element.39), calls=%async_computation.3 | async-start | bytes 524288 | tf_op jit(solution)/shard_map/all_to_all | solution.py:446
  76.2 10.6 %copy-start = (f32[2,128]{1,0:T(2,128)S(1)}, f32[2,128]{1,0:T(2,128)}, u32[]{:S(2)}) copy-start(f32[2,128]{1,0:T(2,128)} %get-tuple-element.32) | copy-start | bytes 3076
  81.5 16.5 %all-to-all-start.4 = ((bf16[128,8,128]{2,1,0:T(8,128)(2,1)}), bf16[128,8,128]{2,1,0:T(8,128)(2,1)S(1)}, u32[]{:S(2)}, u32[]{:S(2)}) async-start(bf16[128,8,128]{2,1,0:T(8,128)(2,1)} %reduce.3.after_ref), calls=%async_computation.4 | async-start | bytes 524288 | tf_op jit(solution)/shard_map/all_to_all | solution.py:446

commit v4 on v3

--- a/solution.py
+++ b/solution.py
@@ -30,7 +30,8 @@
 LANES = 1
 PART = 768
 PARTS = TOKENS // PART
-AHEAD = 3
+AHEAD = 4
+TILE = 256
 HEAD_TILES = D // 8
 
 BF = jnp.bfloat16
@@ -81,9 +82,9 @@
 
 
 def request_kernel(hidden_hbm, weight_hbm, teacher_hbm, cand_hbm, storage_hbm, lengths_hbm,
-                   send_ref, proj_hbm, const_hbm,
+                   send_hbm, proj_hbm, const_hbm,
                    hidden_ref, weight_ref, teacher_ref, cand_ref, storage_ref, lengths_ref,
-                   place_ref, length_ref, proj_ref, const_ref, sems, out_sems):
+                   place_ref, length_ref, proj_ref, const_ref, embed_ref, meta_ref, sems, out_sems, send_sems):
     small = start_copies(
         (
             (cand_hbm, cand_ref),
@@ -95,15 +96,18 @@
         ),
         sems,
     )
-    wait_copies(small)
+    wait_copies(small[4:])
+    proj = dot(hidden_ref[...], weight_ref[...])
+    proj_ref[...] = proj
+    inverse = lax.rsqrt(jnp.sum(proj * proj, axis=-1, keepdims=True) + EPS)
+    embed_ref[...] = (proj * inverse).astype(BF)
+    sends = start_copies(
+        [(embed_ref, send_hbm.at[s, pl.ds(0, QROWS)]) for s in range(N_DEV)], send_sems
+    )
+    wait_copies(small[:4])
     for i in range(N_DEV):
         place_ref[i : i + 1, :] = storage_ref[0:1, i * STORED : (i + 1) * STORED]
         length_ref[i : i + 1, :] = lengths_ref[0:1, i * STORED : (i + 1) * STORED]
-    proj = dot(hidden_ref[...], weight_ref[...])
-    proj_ref[...] = proj
-    inverse = lax.rsqrt(jnp.sum(proj * proj, axis=-1, keepdims=True) + EPS)
-    embed = (proj * inverse).astype(BF)
-
     teacher = teacher_ref[...]
     log_t = teacher - jnp.log(jnp.sum(jnp.exp(teacher), axis=-1, keepdims=True))
     prob = jnp.exp(log_t)
@@ -145,8 +149,9 @@
     values = jnp.where((sub128 & (SLOTS - 1)) == rank, values, 0.0).astype(BF)
     meta = dot(match_bf, values, COLS_COLS)
     for s in range(N_DEV):
-        send_ref[s, 0:QROWS, :] = embed
-        send_ref[s, QROWS : QROWS + META, :] = jnp.broadcast_to(meta[s : s + 1], (META, DIM)).astype(BF)
+        meta_ref[s] = jnp.broadcast_to(meta[s : s + 1], (META, DIM)).astype(BF)
+    outs += start_copies(((meta_ref, send_hbm.at[:, pl.ds(QROWS, META)]),), out_sems.at[pl.ds(2, 1)])
+    wait_copies(sends)
     wait_copies(outs)
 
 
@@ -167,16 +172,25 @@
     weight_copy.wait()
     packed = jnp.zeros((DIM, DIM), F32)
     lane = iota((DIM, DIM), 1)
-    for i, copy in enumerate(copies):
-        rows = pl.ds(i * PART, PART)
-        copy.wait()
-        if i + AHEAD < PARTS:
-            copies[i + AHEAD].start()
-        proj = dot(hidden_ref[rows, :], weight_ref[...])
-        inverse = lax.rsqrt(jnp.sum(proj * proj, axis=-1, keepdims=True) + EPS)
-        embed_ref[rows, :] = (proj * inverse).astype(BF)
-        for j in range(PART // DIM):
-            packed = jnp.where(lane == i * (PART // DIM) + j, inverse[j * DIM : (j + 1) * DIM], packed)
+    begun = AHEAD
+    for i in range(STEPS):
+        for copy in copies[i * BLOCK // PART : (i + 1) * BLOCK // PART]:
+            copy.wait()
+            if begun < PARTS:
+                copies[begun].start()
+                begun += 1
+
+        def tile(t, carry):
+            start = i * BLOCK + t * TILE
+            rows = pl.ds(pl.multiple_of(start, TILE), TILE)
+            proj = dot(hidden_ref[rows, :], weight_ref[...])
+            inverse = lax.rsqrt(jnp.sum(proj * proj, axis=-1, keepdims=True) + EPS)
+            embed_ref[rows, :] = (proj * inverse).astype(BF)
+            for j in range(TILE // DIM):
+                carry = jnp.where(lane == start // DIM + j, inverse[j * DIM : (j + 1) * DIM], carry)
+            return carry
+
+        packed = lax.fori_loop(0, BLOCK // TILE, tile, packed, unroll=2)
     inverse_ref[...] = packed
     out = pltpu.make_async_copy(inverse_ref, inverse_hbm, out_sem)
     out.start()
@@ -397,15 +411,12 @@
     wait_copies(outs)
 
 
-def back_kernel(preact_ref, weight_ref, after_ref, grad_ref):
+def back_kernel(preact_ref, weight_ref, query_ref, grad_ref, query_grad_ref):
     grad_ref[...] = dot(preact_ref[...], weight_ref[...], COLS_COLS).astype(BF)
 
-
-def query_back_kernel(preact_ref, weight_hbm, after_ref, grad_ref, weight_ref, sem):
-    copy = pltpu.make_async_copy(weight_hbm, weight_ref, sem)
-    copy.start()
-    copy.wait()
-    grad_ref[...] = dot(preact_ref[...], weight_ref[...], COLS_COLS).astype(BF)
+    @pl.when(pl.program_id(0) == 0)
+    def _():
+        query_grad_ref[...] = dot(query_ref[...], weight_ref[...], COLS_COLS).astype(BF)
 
 
 def finish_kernel(recv_ref, hidden_hbm, proj_hbm, head_ref, preact_ref, send_ref,
@@ -425,7 +436,7 @@
     send_ref[HEAD_TILES:N_ALL] = jnp.zeros((N_ALL - HEAD_TILES, 8, DIM), BF)
 
 
-def reduce_kernel(recv_ref, after_ref, send_ref):
+def reduce_kernel(recv_ref, send_ref):
     total = jnp.sum(recv_ref[...].astype(F32), axis=0).astype(BF)
     send_ref[...] = jnp.broadcast_to(total[None], (N_ALL, 8, DIM))
 
@@ -457,12 +468,12 @@
     send, query_proj, const = pl.pallas_call(
         request_kernel,
         out_shape=(
-            shape((N_DEV, QROWS + META, DIM), BF),
+            pltpu.HBM((N_DEV, QROWS + META, DIM), BF),
             pltpu.HBM((QROWS, DIM), F32),
             pltpu.HBM((8, DIM), F32),
         ),
         in_specs=[HBM] * 6,
-        out_specs=(VMEM, HBM, HBM),
+        out_specs=(HBM, HBM, HBM),
         scratch_shapes=[
             pltpu.VMEM((QROWS, D), BF),
             pltpu.VMEM((D, DIM), BF),
@@ -474,8 +485,11 @@
             pltpu.VMEM((N_DEV, DIM), jnp.int32),
             pltpu.VMEM((QROWS, DIM), F32),
             pltpu.VMEM((8, DIM), F32),
+            pltpu.VMEM((QROWS, DIM), BF),
+            pltpu.VMEM((N_DEV, META, DIM), BF),
             pltpu.SemaphoreType.DMA((6,)),
-            pltpu.SemaphoreType.DMA((2,)),
+            pltpu.SemaphoreType.DMA((3,)),
+            pltpu.SemaphoreType.DMA((N_DEV,)),
         ],
         compiler_params=params(4),
         name="request",
@@ -615,16 +629,16 @@
     )(recv_delta, query_flat, in_hbm(query_proj), in_vmem(head))
     recv_head = exchange(send_head, ("group", "dev"))
 
-    passage_grad = pl.pallas_call(
+    passage_grad, query_grad = pl.pallas_call(
         back_kernel,
         grid=(STEPS,),
-        out_shape=pltpu.HBM((TOKENS, D), BF),
+        out_shape=(pltpu.HBM((TOKENS, D), BF), pltpu.HBM((QROWS, D), BF)),
         in_specs=[
             pl.BlockSpec((BLOCK, DIM), lambda i: (i, 0)),
             pl.BlockSpec((D, DIM), lambda i: (0, 0)),
-            pl.BlockSpec(memory_space=pl.ANY),
-        ],
-        out_specs=pl.BlockSpec((BLOCK, D), lambda i: (i, 0)),
+            pl.BlockSpec((QROWS, DIM), lambda i: (0, 0)),
+        ],
+        out_specs=(pl.BlockSpec((BLOCK, D), lambda i: (i, 0)), pl.BlockSpec((QROWS, D), lambda i: (0, 0))),
         cost_estimate=estimate(2 * TOKENS * D * DIM, 15_000_000),
         compiler_params=params(20),
         name="back",
@@ -633,21 +647,11 @@
     send_total = pl.pallas_call(
         reduce_kernel,
         out_shape=shape((N_ALL, 8, DIM), BF),
-        in_specs=[VMEM, pl.BlockSpec(memory_space=pl.ANY)],
+        in_specs=[VMEM],
         out_specs=VMEM,
         compiler_params=params(4),
         name="reduce",
-    )(recv_head, in_hbm(passage_grad))
-    query_grad = pl.pallas_call(
-        query_back_kernel,
-        out_shape=shape((QROWS, D), BF),
-        in_specs=[VMEM, HBM, pl.BlockSpec(memory_space=pl.ANY)],
-        out_specs=VMEM,
-        scratch_shapes=[pltpu.VMEM((D, DIM), BF), pltpu.SemaphoreType.DMA],
-        cost_estimate=estimate(2 * QROWS * D * DIM, 400_000),
-        compiler_params=params(4),
-        name="query_back",
-    )(query_preact, head_weight, send_total)
+    )(recv_head)
     head_all = exchange(send_total, ("group", "dev"))
     head_grad = head_all[:HEAD_TILES].reshape(D, DIM).astype(F32)
     return (

time: 99.4 us -> 97.5 us (0.981)
  blocking collectives: 0 us -> 17.8 us
  waiting for transfers between devices: 26.3 us -> 17.8 us
  starting transfers between devices: 28.8 us -> 20.9 us
  Pallas kernels: 41.5 us -> 38.2 us
    all_to_all x0 -> x1, blocking collectives: none -> 17.8 us  [exchange(): return lax.all_to_all(x, axes, split_axis=0, concat_axis=0, tiled=True)]
    all_to_all x5 -> x4, waiting for transfers between devices: 26.3 us -> 17.8 us  [exchange(): return lax.all_to_all(x, axes, split_axis=0, concat_axis=0, tiled=True)]
    all_to_all x5 -> x4, starting transfers between devices: 28.8 us -> 20.9 us  [exchange(): return lax.all_to_all(x, axes, split_axis=0, concat_axis=0, tiled=True)]
    pallas_call x3 -> x2, Pallas kernels: 11.3 us -> 9.78 us  [the longest x1 6.88 us: on_device(): pl.pallas_call(back_kernel, grid=(STEPS,), out_shape=(pltpu.HBM((TOKENS,...]
    pallas_call x1, Pallas kernels: 8.82 us -> 7.74 us  [on_device(): pl.pallas_call(encode_kernel, out_shape=(pltpu.VMEM((TOKENS, DIM), BF), p...]
  transfers between devices with their start and end apart: 5 -> 4, of which waited for: 5 -> 4; matrix products, arithmetic and copies ran while one was open for 1% -> 1% of each run, Pallas kernels for 28% -> 26%
where the time goes in v4:
time: 97.5 us; the launch traced here: 96.9 us
  Pallas kernels  38.2 us (39%)
  starting transfers between devices  20.9 us (21%)
  waiting for transfers between devices  17.8 us (18%)
  blocking collectives  17.8 us (18%)
    all_to_all x4, starting transfers between devices, exchange(): return lax.all_to_all(x, axes, split_axis=0, concat_axis=0, tiled=True)  20.9 us
    all_to_all x4, waiting for transfers between devices, exchange(): return lax.all_to_all(x, axes, split_axis=0, concat_axis=0, tiled=True)  17.8 us
    all_to_all x1, blocking collectives, exchange(): return lax.all_to_all(x, axes, split_axis=0, concat_axis=0, tiled=True)  17.8 us
    pallas_call x1, Pallas kernels, on_device(): pl.pallas_call(stored_kernel, out_shape=(pltpu.HBM((TOKENS, DIM), BF), pl...  7.94 us
    pallas_call x1, Pallas kernels, on_device(): pl.pallas_call(encode_kernel, out_shape=(pltpu.VMEM((TOKENS, DIM), BF), p...  7.74 us
    pallas_call x1, Pallas kernels, on_device(): pl.pallas_call(back_kernel, grid=(STEPS,), out_shape=(pltpu.HBM((TOKENS,...  6.88 us
    pallas_call x1, Pallas kernels, on_device(): pl.pallas_call(score_kernel, out_shape=(pltpu.HBM((N_DEV * QLEN, WIDE), F...  4.79 us
    pallas_call x1, Pallas kernels, on_device(): pl.pallas_call(query_kernel, out_shape=(pltpu.HBM((N_DEV, QROWS, DIM), BF...  3.6 us
  transfers between devices with their start and end apart: 4, of which 4 were waited for; matrix products, arithmetic and copies ran while one was open for 1% of the time, Pallas kernels for 26%

profile of v4, /device:TPU:1, one launch (start us, length us, event | category | flops | bytes accessed | tf_op | source)
XLA Modules:
  0.0 96.9 jit_solution(7961464798874945855)
XLA Ops:
  0.6 2.9 %request.1 = (bf16[32,80,128]{2,1,0:T(8,128)(2,1)}, f32[64,128]{1,0:T(8,128)}, f32[8,128]{1,0:T(8,128)}) custom-call(bf16[64,768]{1,0:T(8,128)(2,1)} %bitcast.12, bf16[768,128]{1,0:T(8,128)(2,1)} %weight_ref.1, f32[2,64]{1,0:T(2,128)} %teacher_hbm.1, s32[2,64]{1,0:T(2,128)} %cand_hbm.1, s32[1,4096]{1,0:T(1,128)} %storage_hbm.1, s32[1,4096]{1,0:T(1,128)} %lengths_hbm.1), custom_call_target="tpu_custom_call" | custom-call | tf_op jit(solution)/shard_map/request/pallas_call | solution.py:468
  3.5 8.6 %all-to-all-start = ((bf16[32,80,128]{2,1,0:T(8,128)(2,1)}), bf16[32,80,128]{2,1,0:T(8,128)(2,1)S(1)}, u32[]{:S(2)}, u32[]{:S(2)}) async-start(bf16[32,80,128]{2,1,0:T(8,128)(2,1)} %get-tuple-element.25), calls=%async_computation | async-start | bytes 1310720 | tf_op jit(solution)/shard_map/all_to_all | solution.py:457
  12.1 7.7 %encode.1 = (bf16[6144,128]{1,0:T(8,128)(2,1)S(1)}, f32[128,128]{1,0:T(8,128)}) custom-call(bf16[6144,768]{1,0:T(8,128)(2,1)} %bitcast.10, bf16[768,128]{1,0:T(8,128)(2,1)} %weight_ref.1), custom_call_target="tpu_custom_call" | custom-call | flops 1207959552 | bytes 15000000 | tf_op jit(solution)/shard_map/encode/pallas_call | solution.py:499
  19.9 5.2 %all-to-all-done.recv_ref = bf16[32,80,128]{2,1,0:T(8,128)(2,1)S(1)} async-done(((bf16[32,80,128]{2,1,0:T(8,128)(2,1)}), bf16[32,80,128]{2,1,0:T(8,128)(2,1)S(1)}, u32[]{:S(2)}, u32[]{:S(2)}) %all-to-all-start) | async-done | bytes 655392 | tf_op jit(solution)/shard_map/all_to_all | solution.py:457
  25.0 4.8 %score.1 = (f32[1024,576]{1,0:T(8,128)}, f32[1024,128]{1,0:T(8,128)}, f32[32,8,128]{2,1,0:T(8,128)}, f32[3,32,128]{2,1,0:T(8,128)}, f32[32,576]{1,0:T(8,128)}, /...) custom-call(bf16[32,80,128]{2,1,0:T(8,128)(2,1)S(1)} %all-to-all-done.recv_ref, ...), custom_call_target="tpu_custom_call" | custom-call | tf_op jit(solution)/shard_map/score/pallas_call | solution.py:516
  29.8 4.1 %all-to-all-start.1 = ((f32[32,8,128]{2,1,0:T(8,128)}), f32[32,8,128]{2,1,0:T(8,128)S(1)}, u32[]{:S(2)}, u32[]{:S(2)}) async-start(f32[32,8,128]{2,1,0:T(8,128)} %get-tuple-element.27), calls=%async_computation.1 | async-start | bytes 262144 | tf_op jit(solution)/shard_map/all_to_all | solution.py:457
  33.9 2.3 %ahead.1.weights_ref = bf16[1024,576]{1,0:T(8,128)(2,1)S(1)} custom-call(f32[1024,576]{1,0:T(8,128)} %get-tuple-element.31.expo_hbm, f32[1024,128]{1,0:T(8,128)} %get-tuple-element.32.recip_hbm), custom_call_target="tpu_custom_call" | custom-call | flops 1207959552 | bytes 15000000 | tf_op jit(solution)/shard_map/ahead/pallas_call | solution.py:548
  36.3 5.4 %all-to-all-done.1.sums_ref = f32[32,8,128]{2,1,0:T(8,128)S(1)} async-done(((f32[32,8,128]{2,1,0:T(8,128)}), f32[32,8,128]{2,1,0:T(8,128)S(1)}, u32[]{:S(2)}, u32[]{:S(2)}) %all-to-all-start.1) | async-done | bytes 131104 | tf_op jit(solution)/shard_map/all_to_all | solution.py:457
  41.7 3.6 %query.1 = (bf16[32,64,128]{2,1,0:T(8,128)(2,1)}, bf16[1024,576]{1,0:T(8,128)(2,1)}, f32[2,128]{1,0:T(2,128)}) custom-call(f32[32,8,128]{2,1,0:T(8,128)S(1)} %all-to-all-done.1.sums_ref, f32[8,128]{1,0:T(8,128)} %get-tuple-element.28.const_hbm, s32[1]{0:T(128)} %bitcast.2.me_ref, f32[3,32,128]{2,1,0:T(8,128)} %get-tuple-element.29.table_hbm, ...), custom_call_target="tpu_custom_call" | custom-call | tf_op jit(solution)/shard_map/query/pallas_call | solution.py:564
  45.3 4.0 %all-to-all-start.2 = ((bf16[32,64,128]{2,1,0:T(8,128)(2,1)}), bf16[32,64,128]{2,1,0:T(8,128)(2,1)S(1)}, u32[]{:S(2)}, u32[]{:S(2)}) async-start(bf16[32,64,128]{2,1,0:T(8,128)(2,1)} %get-tuple-element.35), calls=%async_computation.2 | async-start | bytes 1048576 | tf_op jit(solution)/shard_map/all_to_all | solution.py:457
  49.2 7.9 %stored.1 = (bf16[6144,128]{1,0:T(8,128)(2,1)}, f32[768,128]{1,0:T(8,128)S(1)}) custom-call(s32[32,128]{1,0:T(8,128)} %get-tuple-element.33.place_hbm, bf16[32,64,128]{2,1,0:T(8,128)(2,1)} %get-tuple-element.37.queries_hbm, f32[32,576]{1,0:T(8,128)} %get-tuple-element.30.second_hbm, bf16[1024,576]{1,0:T(8,128)(2,1)} %get-tuple-element.38.mixed_hbm, ...), custom_call_target="tpu_custom_call" | custom-call | flops 2415919104 | bytes 20000000 | tf_op jit(solution)/shard_map/stored/pallas_call | solution.py:591
  57.2 0.0 copy-start
  57.2 3.7 %all-to-all-done.2.recv_ref = bf16[32,64,128]{2,1,0:T(8,128)(2,1)S(1)} async-done(((bf16[32,64,128]{2,1,0:T(8,128)(2,1)}), bf16[32,64,128]{2,1,0:T(8,128)(2,1)S(1)}, u32[]{:S(2)}, u32[]{:S(2)}) %all-to-all-start.2) | async-done | bytes 524320 | tf_op jit(solution)/shard_map/all_to_all | solution.py:457
  60.9 1.2 %finish.1 = (bf16[64,128]{1,0:T(8,128)(2,1)S(1)}, bf16[128,8,128]{2,1,0:T(8,128)(2,1)S(1)}) custom-call(bf16[32,64,128]{2,1,0:T(8,128)(2,1)S(1)} %all-to-all-done.2.recv_ref, bf16[64,768]{1,0:T(8,128)(2,1)} %bitcast.13, f32[64,128]{1,0:T(8,128)} %get-tuple-element.36.proj_hbm, f32[768,128]{1,0:T(8,128)S(1)} %get-tuple-element.40.head_ref), custom_call_target="tpu_custom_call" | custom-call | tf_op jit(solution)/shard_map/finish/pallas_call | solution.py:617
  62.1 17.8 %all_to_all.25.recv_ref = bf16[128,8,128]{2,1,0:T(8,128)(2,1)S(1)} all-to-all(bf16[128,8,128]{2,1,0:T(8,128)(2,1)S(1)} %get-tuple-element.41), channel_id=1, replica_groups=mesh['group'=4,'dev'=32] {'group','dev'}, dimensions={0} | all-to-all | bytes 524288 | tf_op jit(solution)/shard_map/all_to_all | solution.py:457
  79.9 0.9 reduce.3
  80.7 4.3 %all-to-all-start.4 = ((bf16[128,8,128]{2,1,0:T(8,128)(2,1)}), bf16[128,8,128]{2,1,0:T(8,128)(2,1)S(1)}, u32[]{:S(2)}, u32[]{:S(2)}) async-start(bf16[128,8,128]{2,1,0:T(8,128)(2,1)} %reduce.3), calls=%async_computation.4 | async-start | bytes 524288 | tf_op jit(solution)/shard_map/all_to_all | solution.py:457
  85.0 0.0 copy-done
  85.1 0.6 slice_reduce_fusion
  85.7 6.9 %back.1 = (bf16[6144,768]{1,0:T(8,128)(2,1)}, bf16[64,768]{1,0:T(8,128)(2,1)}) custom-call(bf16[6144,128]{1,0:T(8,128)(2,1)} %get-tuple-element.42.preact_ref, bf16[768,128]{1,0:T(8,128)(2,1)} %weight_ref.1, bf16[64,128]{1,0:T(8,128)(2,1)S(1)} %get-tuple-element.43.query_ref), custom_call_target="tpu_custom_call" | custom-call | flops 1207959552 | bytes 15000000 | tf_op jit(solution)/shard_map/back/pallas_call | solution.py:632
  92.6 3.6 %all-to-all-done.4 = bf16[128,8,128]{2,1,0:T(8,128)(2,1)S(1)} async-done(((bf16[128,8,128]{2,1,0:T(8,128)(2,1)}), bf16[128,8,128]{2,1,0:T(8,128)(2,1)S(1)}, u32[]{:S(2)}, u32[]{:S(2)}) %all-to-all-start.4) | async-done | bytes 262176 | tf_op jit(solution)/shard_map/all_to_all | solution.py:457
  96.1 0.8 fusion
Async XLA Ops:
  3.5 21.5 %all-to-all-start = ((bf16[32,80,128]{2,1,0:T(8,128)(2,1)}), bf16[32,80,128]{2,1,0:T(8,128)(2,1)S(1)}, u32[]{:S(2)}, u32[]{:S(2)}) async-start(bf16[32,80,128]{2,1,0:T(8,128)(2,1)} %get-tuple-element.25), calls=%async_computation | async-start | bytes 1310720 | tf_op jit(solution)/shard_map/all_to_all | solution.py:457
  29.8 11.8 %all-to-all-start.1 = ((f32[32,8,128]{2,1,0:T(8,128)}), f32[32,8,128]{2,1,0:T(8,128)S(1)}, u32[]{:S(2)}, u32[]{:S(2)}) async-start(f32[32,8,128]{2,1,0:T(8,128)} %get-tuple-element.27), calls=%async_computation.1 | async-start | bytes 262144 | tf_op jit(solution)/shard_map/all_to_all | solution.py:457
  45.3 15.6 %all-to-all-start.2 = ((bf16[32,64,128]{2,1,0:T(8,128)(2,1)}), bf16[32,64,128]{2,1,0:T(8,128)(2,1)S(1)}, u32[]{:S(2)}, u32[]{:S(2)}) async-start(bf16[32,64,128]{2,1,0:T(8,128)(2,1)} %get-tuple-element.35), calls=%async_computation.2 | async-start | bytes 1048576 | tf_op jit(solution)/shard_map/all_to_all | solution.py:457
  57.2 27.9 %copy-start = (f32[2,128]{1,0:T(2,128)S(1)}, f32[2,128]{1,0:T(2,128)}, u32[]{:S(2)}) copy-start(f32[2,128]{1,0:T(2,128)} %get-tuple-element.34) | copy-start | bytes 3076
  80.7 15.4 %all-to-all-start.4 = ((bf16[128,8,128]{2,1,0:T(8,128)(2,1)}), bf16[128,8,128]{2,1,0:T(8,128)(2,1)S(1)}, u32[]{:S(2)}, u32[]{:S(2)}) async-start(bf16[128,8,128]{2,1,0:T(8,128)(2,1)} %reduce.3), calls=%async_computation.4 | async-start | bytes 524288 | tf_op jit(solution)/shard_map/all_to_all | solution.py:457

commit v5 on v4

--- a/solution.py
+++ b/solution.py
@@ -22,7 +22,7 @@
 WIDE = CAP * PLEN
 QROWS = 2 * QLEN
 META = 16
-CHUNK = 16
+CHUNK = 8
 GROUP = 16
 TOKENS = STORED * PLEN
 BLOCK = 1536
@@ -248,7 +248,8 @@
         expo_copy(i).start()
         return carry
 
-    lax.fori_loop(0, N_DEV // CHUNK, chunk, 0)
+    for i in range(N_DEV // CHUNK):
+        chunk(i, 0)
     total = dot(round_ref[...], spread.astype(BF), COLS_COLS)
     total = jnp.where(total > 0.0, total, 1.0)
     recip_ref[...] = 1.0 / total
@@ -356,7 +357,8 @@
             copy.start()
         return carry
 
-    lax.fori_loop(0, N_DEV // CHUNK, chunk, 0)
+    for i in range(N_DEV // CHUNK):
+        chunk(i, 0)
     wait_copies(outs)
     for i in range(N_DEV // CHUNK):
         wait_copies(part_copies(i))
@@ -411,12 +413,24 @@
     wait_copies(outs)
 
 
-def back_kernel(preact_ref, weight_ref, query_ref, grad_ref, query_grad_ref):
-    grad_ref[...] = dot(preact_ref[...], weight_ref[...], COLS_COLS).astype(BF)
-
-    @pl.when(pl.program_id(0) == 0)
-    def _():
-        query_grad_ref[...] = dot(query_ref[...], weight_ref[...], COLS_COLS).astype(BF)
+def back_kernel(preact_hbm, weight_hbm, query_ref, grad_hbm, query_grad_hbm,
+                preact_ref, weight_ref, grad_ref, query_grad_ref, sems, out_sems):
+    copies = start_copies(((weight_hbm, weight_ref), (preact_hbm, preact_ref)), sems)
+    wait_copies(copies)
+    outs = []
+    for i in range(PARTS):
+
+        def tile(t, carry):
+            rows = pl.ds(pl.multiple_of(i * PART + t * TILE, TILE), TILE)
+            grad_ref[rows, :] = dot(preact_ref[rows, :], weight_ref[...], COLS_COLS).astype(BF)
+            return carry
+
+        lax.fori_loop(0, PART // TILE, tile, 0, unroll=2)
+        rows = pl.ds(i * PART, PART)
+        outs += start_copies(((grad_ref.at[rows], grad_hbm.at[rows]),), out_sems.at[pl.ds(i, 1)])
+    query_grad_ref[...] = dot(query_ref[...], weight_ref[...], COLS_COLS).astype(BF)
+    outs += start_copies(((query_grad_ref, query_grad_hbm),), out_sems.at[pl.ds(PARTS, 1)])
+    wait_copies(outs)
 
 
 def finish_kernel(recv_ref, hidden_hbm, proj_hbm, head_ref, preact_ref, send_ref,
@@ -631,18 +645,21 @@
 
     passage_grad, query_grad = pl.pallas_call(
         back_kernel,
-        grid=(STEPS,),
         out_shape=(pltpu.HBM((TOKENS, D), BF), pltpu.HBM((QROWS, D), BF)),
-        in_specs=[
-            pl.BlockSpec((BLOCK, DIM), lambda i: (i, 0)),
-            pl.BlockSpec((D, DIM), lambda i: (0, 0)),
-            pl.BlockSpec((QROWS, DIM), lambda i: (0, 0)),
+        in_specs=[HBM, HBM, VMEM],
+        out_specs=(HBM, HBM),
+        scratch_shapes=[
+            pltpu.VMEM((TOKENS, DIM), BF),
+            pltpu.VMEM((D, DIM), BF),
+            pltpu.VMEM((TOKENS, D), BF),
+            pltpu.VMEM((QROWS, D), BF),
+            pltpu.SemaphoreType.DMA((2,)),
+            pltpu.SemaphoreType.DMA((PARTS + 1,)),
         ],
-        out_specs=(pl.BlockSpec((BLOCK, D), lambda i: (i, 0)), pl.BlockSpec((QROWS, D), lambda i: (0, 0))),
         cost_estimate=estimate(2 * TOKENS * D * DIM, 15_000_000),
         compiler_params=params(20),
         name="back",
-    )(in_hbm(preact), head_weight, query_preact)
+    )(in_hbm(preact), head_weight, in_vmem(query_preact))
 
     send_total = pl.pallas_call(
         reduce_kernel,

time: 97.5 us -> 97 us (level)
  Pallas kernels: 38.2 us -> 36.6 us
  waiting for transfers between devices: 17.8 us -> 18.9 us
    pallas_call x1, Pallas kernels: 6.88 us -> 5.75 us  [on_device(): pl.pallas_call(back_kernel, out_shape=(pltpu.HBM((TOKENS, D), BF), pltpu....]
    all_to_all x4, waiting for transfers between devices: 17.8 us -> 18.9 us  [exchange(): return lax.all_to_all(x, axes, split_axis=0, concat_axis=0, tiled=True)]
  transfers between devices with their start and end apart: 4 -> 4, of which waited for: 4 -> 4; matrix products, arithmetic and copies ran while one was open for 1% -> 1% of each run, Pallas kernels for 26% -> 25%
where the time goes in v5:
time: 97 us; the launch traced here: 96.4 us
  Pallas kernels  36.6 us (38%)
  starting transfers between devices  20.9 us (22%)
  waiting for transfers between devices  18.9 us (19%)
  blocking collectives  17.8 us (18%)
    all_to_all x4, starting transfers between devices, exchange(): return lax.all_to_all(x, axes, split_axis=0, concat_axis=0, tiled=True)  20.9 us
    all_to_all x4, waiting for transfers between devices, exchange(): return lax.all_to_all(x, axes, split_axis=0, concat_axis=0, tiled=True)  18.9 us
    all_to_all x1, blocking collectives, exchange(): return lax.all_to_all(x, axes, split_axis=0, concat_axis=0, tiled=True)  17.8 us
    pallas_call x1, Pallas kernels, on_device(): pl.pallas_call(stored_kernel, out_shape=(pltpu.HBM((TOKENS, DIM), BF), pl...  7.94 us
    pallas_call x1, Pallas kernels, on_device(): pl.pallas_call(encode_kernel, out_shape=(pltpu.VMEM((TOKENS, DIM), BF), p...  7.74 us
    pallas_call x1, Pallas kernels, on_device(): pl.pallas_call(back_kernel, out_shape=(pltpu.HBM((TOKENS, D), BF), pltpu....  5.75 us
    pallas_call x1, Pallas kernels, on_device(): pl.pallas_call(score_kernel, out_shape=(pltpu.HBM((N_DEV * QLEN, WIDE), F...  4.54 us
    pallas_call x1, Pallas kernels, on_device(): pl.pallas_call(query_kernel, out_shape=(pltpu.HBM((N_DEV, QROWS, DIM), BF...  3.33 us
  transfers between devices with their start and end apart: 4, of which 4 were waited for; matrix products, arithmetic and copies ran while one was open for 1% of the time, Pallas kernels for 25%

profile of v5, /device:TPU:1, one launch (start us, length us, event | category | flops | bytes accessed | tf_op | source)
XLA Modules:
  0.0 96.4 jit_solution(10391535923561133828)
XLA Ops:
  0.6 2.9 %request.1 = (bf16[32,80,128]{2,1,0:T(8,128)(2,1)}, f32[64,128]{1,0:T(8,128)}, f32[8,128]{1,0:T(8,128)}) custom-call(bf16[64,768]{1,0:T(8,128)(2,1)} %bitcast.12, bf16[768,128]{1,0:T(8,128)(2,1)} %weight_hbm.5, f32[2,64]{1,0:T(2,128)} %teacher_hbm.1, s32[2,64]{1,0:T(2,128)} %cand_hbm.1, s32[1,4096]{1,0:T(1,128)} %storage_hbm.1, s32[1,4096]{1,0:T(1,128)} %lengths_hbm.1), custom_call_target="tpu_custom_call" | custom-call | tf_op jit(solution)/shard_map/request/pallas_call | solution.py:482
  3.5 8.6 %all-to-all-start = ((bf16[32,80,128]{2,1,0:T(8,128)(2,1)}), bf16[32,80,128]{2,1,0:T(8,128)(2,1)S(1)}, u32[]{:S(2)}, u32[]{:S(2)}) async-start(bf16[32,80,128]{2,1,0:T(8,128)(2,1)} %get-tuple-element.25), calls=%async_computation | async-start | bytes 1310720 | tf_op jit(solution)/shard_map/all_to_all | solution.py:471
  12.1 7.7 %encode.1 = (bf16[6144,128]{1,0:T(8,128)(2,1)S(1)}, f32[128,128]{1,0:T(8,128)}) custom-call(bf16[6144,768]{1,0:T(8,128)(2,1)} %bitcast.10, bf16[768,128]{1,0:T(8,128)(2,1)} %weight_hbm.5), custom_call_target="tpu_custom_call" | custom-call | flops 1207959552 | bytes 15000000 | tf_op jit(solution)/shard_map/encode/pallas_call | solution.py:513
  19.9 5.2 %all-to-all-done.recv_ref = bf16[32,80,128]{2,1,0:T(8,128)(2,1)S(1)} async-done(((bf16[32,80,128]{2,1,0:T(8,128)(2,1)}), bf16[32,80,128]{2,1,0:T(8,128)(2,1)S(1)}, u32[]{:S(2)}, u32[]{:S(2)}) %all-to-all-start) | async-done | bytes 655392 | tf_op jit(solution)/shard_map/all_to_all | solution.py:471
  25.0 4.5 %score.1 = (f32[1024,576]{1,0:T(8,128)}, f32[1024,128]{1,0:T(8,128)}, f32[32,8,128]{2,1,0:T(8,128)}, f32[3,32,128]{2,1,0:T(8,128)}, f32[32,576]{1,0:T(8,128)}, /...) custom-call(bf16[32,80,128]{2,1,0:T(8,128)(2,1)S(1)} %all-to-all-done.recv_ref, ...), custom_call_target="tpu_custom_call" | custom-call | tf_op jit(solution)/shard_map/score/pallas_call | solution.py:530
  29.6 4.1 %all-to-all-start.1 = ((f32[32,8,128]{2,1,0:T(8,128)}), f32[32,8,128]{2,1,0:T(8,128)S(1)}, u32[]{:S(2)}, u32[]{:S(2)}) async-start(f32[32,8,128]{2,1,0:T(8,128)} %get-tuple-element.27), calls=%async_computation.1 | async-start | bytes 262144 | tf_op jit(solution)/shard_map/all_to_all | solution.py:471
  33.7 2.3 %ahead.1.weights_ref = bf16[1024,576]{1,0:T(8,128)(2,1)S(1)} custom-call(f32[1024,576]{1,0:T(8,128)} %get-tuple-element.31.expo_hbm, f32[1024,128]{1,0:T(8,128)} %get-tuple-element.32.recip_hbm), custom_call_target="tpu_custom_call" | custom-call | flops 1207959552 | bytes 15000000 | tf_op jit(solution)/shard_map/ahead/pallas_call | solution.py:562
  36.0 5.4 %all-to-all-done.1.sums_ref = f32[32,8,128]{2,1,0:T(8,128)S(1)} async-done(((f32[32,8,128]{2,1,0:T(8,128)}), f32[32,8,128]{2,1,0:T(8,128)S(1)}, u32[]{:S(2)}, u32[]{:S(2)}) %all-to-all-start.1) | async-done | bytes 131104 | tf_op jit(solution)/shard_map/all_to_all | solution.py:471
  41.4 3.3 %query.1 = (bf16[32,64,128]{2,1,0:T(8,128)(2,1)}, bf16[1024,576]{1,0:T(8,128)(2,1)}, f32[2,128]{1,0:T(2,128)}) custom-call(f32[32,8,128]{2,1,0:T(8,128)S(1)} %all-to-all-done.1.sums_ref, f32[8,128]{1,0:T(8,128)} %get-tuple-element.28.const_hbm, s32[1]{0:T(128)} %bitcast.2.me_ref, f32[3,32,128]{2,1,0:T(8,128)} %get-tuple-element.29.table_hbm, ...), custom_call_target="tpu_custom_call" | custom-call | tf_op jit(solution)/shard_map/query/pallas_call | solution.py:578
  44.8 4.0 %all-to-all-start.2 = ((bf16[32,64,128]{2,1,0:T(8,128)(2,1)}), bf16[32,64,128]{2,1,0:T(8,128)(2,1)S(1)}, u32[]{:S(2)}, u32[]{:S(2)}) async-start(bf16[32,64,128]{2,1,0:T(8,128)(2,1)} %get-tuple-element.35), calls=%async_computation.2 | async-start | bytes 1048576 | tf_op jit(solution)/shard_map/all_to_all | solution.py:471
  48.7 7.9 %stored.1 = (bf16[6144,128]{1,0:T(8,128)(2,1)}, f32[768,128]{1,0:T(8,128)S(1)}) custom-call(s32[32,128]{1,0:T(8,128)} %get-tuple-element.33.place_hbm, bf16[32,64,128]{2,1,0:T(8,128)(2,1)} %get-tuple-element.37.queries_hbm, f32[32,576]{1,0:T(8,128)} %get-tuple-element.30.second_hbm, bf16[1024,576]{1,0:T(8,128)(2,1)} %get-tuple-element.38.mixed_hbm, ...), custom_call_target="tpu_custom_call" | custom-call | flops 2415919104 | bytes 20000000 | tf_op jit(solution)/shard_map/stored/pallas_call | solution.py:605
  56.7 0.0 copy-start
  56.7 3.7 %all-to-all-done.2.recv_ref = bf16[32,64,128]{2,1,0:T(8,128)(2,1)S(1)} async-done(((bf16[32,64,128]{2,1,0:T(8,128)(2,1)}), bf16[32,64,128]{2,1,0:T(8,128)(2,1)S(1)}, u32[]{:S(2)}, u32[]{:S(2)}) %all-to-all-start.2) | async-done | bytes 524320 | tf_op jit(solution)/shard_map/all_to_all | solution.py:471
  60.4 1.2 %finish.1 = (bf16[64,128]{1,0:T(8,128)(2,1)S(1)}, bf16[128,8,128]{2,1,0:T(8,128)(2,1)S(1)}) custom-call(bf16[32,64,128]{2,1,0:T(8,128)(2,1)S(1)} %all-to-all-done.2.recv_ref, bf16[64,768]{1,0:T(8,128)(2,1)} %bitcast.13, f32[64,128]{1,0:T(8,128)} %get-tuple-element.36.proj_hbm, f32[768,128]{1,0:T(8,128)S(1)} %get-tuple-element.40.head_ref), custom_call_target="tpu_custom_call" | custom-call | tf_op jit(solution)/shard_map/finish/pallas_call | solution.py:631
  61.6 17.8 %all_to_all.25.recv_ref = bf16[128,8,128]{2,1,0:T(8,128)(2,1)S(1)} all-to-all(bf16[128,8,128]{2,1,0:T(8,128)(2,1)S(1)} %get-tuple-element.41), channel_id=1, replica_groups=mesh['group'=4,'dev'=32] {'group','dev'}, dimensions={0} | all-to-all | bytes 524288 | tf_op jit(solution)/shard_map/all_to_all | solution.py:471
  79.4 0.9 reduce.3
  80.2 4.3 %all-to-all-start.4 = ((bf16[128,8,128]{2,1,0:T(8,128)(2,1)}), bf16[128,8,128]{2,1,0:T(8,128)(2,1)S(1)}, u32[]{:S(2)}, u32[]{:S(2)}) async-start(bf16[128,8,128]{2,1,0:T(8,128)(2,1)} %reduce.3), calls=%async_computation.4 | async-start | bytes 524288 | tf_op jit(solution)/shard_map/all_to_all | solution.py:471
  84.5 0.0 copy-done
  84.6 0.6 slice_reduce_fusion
  85.2 5.8 %back.1 = (bf16[6144,768]{1,0:T(8,128)(2,1)}, bf16[64,768]{1,0:T(8,128)(2,1)}) custom-call(bf16[6144,128]{1,0:T(8,128)(2,1)} %get-tuple-element.42.preact_hbm, bf16[768,128]{1,0:T(8,128)(2,1)} %weight_hbm.5, bf16[64,128]{1,0:T(8,128)(2,1)S(1)} %get-tuple-element.43.query_ref), custom_call_target="tpu_custom_call" | custom-call | flops 1207959552 | bytes 15000000 | tf_op jit(solution)/shard_map/back/pallas_call | solution.py:646
  90.9 4.7 %all-to-all-done.4 = bf16[128,8,128]{2,1,0:T(8,128)(2,1)S(1)} async-done(((bf16[128,8,128]{2,1,0:T(8,128)(2,1)}), bf16[128,8,128]{2,1,0:T(8,128)(2,1)S(1)}, u32[]{:S(2)}, u32[]{:S(2)}) %all-to-all-start.4) | async-done | bytes 262176 | tf_op jit(solution)/shard_map/all_to_all | solution.py:471
  95.6 0.8 fusion
Async XLA Ops:
  3.5 21.5 %all-to-all-start = ((bf16[32,80,128]{2,1,0:T(8,128)(2,1)}), bf16[32,80,128]{2,1,0:T(8,128)(2,1)S(1)}, u32[]{:S(2)}, u32[]{:S(2)}) async-start(bf16[32,80,128]{2,1,0:T(8,128)(2,1)} %get-tuple-element.25), calls=%async_computation | async-start | bytes 1310720 | tf_op jit(solution)/shard_map/all_to_all | solution.py:471
  29.6 11.8 %all-to-all-start.1 = ((f32[32,8,128]{2,1,0:T(8,128)}), f32[32,8,128]{2,1,0:T(8,128)S(1)}, u32[]{:S(2)}, u32[]{:S(2)}) async-start(f32[32,8,128]{2,1,0:T(8,128)} %get-tuple-element.27), calls=%async_computation.1 | async-start | bytes 262144 | tf_op jit(solution)/shard_map/all_to_all | solution.py:471
  44.8 15.6 %all-to-all-start.2 = ((bf16[32,64,128]{2,1,0:T(8,128)(2,1)}), bf16[32,64,128]{2,1,0:T(8,128)(2,1)S(1)}, u32[]{:S(2)}, u32[]{:S(2)}) async-start(bf16[32,64,128]{2,1,0:T(8,128)(2,1)} %get-tuple-element.35), calls=%async_computation.2 | async-start | bytes 1048576 | tf_op jit(solution)/shard_map/all_to_all | solution.py:471
  56.7 27.9 %copy-start = (f32[2,128]{1,0:T(2,128)S(1)}, f32[2,128]{1,0:T(2,128)}, u32[]{:S(2)}) copy-start(f32[2,128]{1,0:T(2,128)} %get-tuple-element.34) | copy-start | bytes 3076
  80.2 15.4 %all-to-all-start.4 = ((bf16[128,8,128]{2,1,0:T(8,128)(2,1)}), bf16[128,8,128]{2,1,0:T(8,128)(2,1)S(1)}, u32[]{:S(2)}, u32[]{:S(2)}) async-start(bf16[128,8,128]{2,1,0:T(8,128)(2,1)} %reduce.3), calls=%async_computation.4 | async-start | bytes 524288 | tf_op jit(solution)/shard_map/all_to_all | solution.py:471

commit v6 on v5

--- a/solution.py
+++ b/solution.py
@@ -96,14 +96,6 @@
         ),
         sems,
     )
-    wait_copies(small[4:])
-    proj = dot(hidden_ref[...], weight_ref[...])
-    proj_ref[...] = proj
-    inverse = lax.rsqrt(jnp.sum(proj * proj, axis=-1, keepdims=True) + EPS)
-    embed_ref[...] = (proj * inverse).astype(BF)
-    sends = start_copies(
-        [(embed_ref, send_hbm.at[s, pl.ds(0, QROWS)]) for s in range(N_DEV)], send_sems
-    )
     wait_copies(small[:4])
     for i in range(N_DEV):
         place_ref[i : i + 1, :] = storage_ref[0:1, i * STORED : (i + 1) * STORED]
@@ -115,7 +107,7 @@
     const_ref[...] = jnp.concatenate(
         [jnp.broadcast_to(const, (2, DIM)), jnp.zeros((6, DIM), F32)], axis=0
     )
-    outs = start_copies(((proj_ref, proj_hbm), (const_ref, const_hbm)), out_sems)
+    outs = start_copies(((const_ref, const_hbm),), out_sems)
     prob_row = jnp.concatenate([prob[0:1], prob[1:2]], axis=1)
     cand = cand_ref[...]
     cand_row = jnp.concatenate([cand[0:1], cand[1:2]], axis=1)
@@ -151,6 +143,15 @@
     for s in range(N_DEV):
         meta_ref[s] = jnp.broadcast_to(meta[s : s + 1], (META, DIM)).astype(BF)
     outs += start_copies(((meta_ref, send_hbm.at[:, pl.ds(QROWS, META)]),), out_sems.at[pl.ds(2, 1)])
+    wait_copies(small[4:])
+    proj = dot(hidden_ref[...], weight_ref[...])
+    proj_ref[...] = proj
+    inverse = lax.rsqrt(jnp.sum(proj * proj, axis=-1, keepdims=True) + EPS)
+    embed_ref[...] = (proj * inverse).astype(BF)
+    sends = start_copies(
+        [(embed_ref, send_hbm.at[s, pl.ds(0, QROWS)]) for s in range(N_DEV)], send_sems
+    )
+    outs += start_copies(((proj_ref, proj_hbm),), out_sems.at[pl.ds(1, 1)])
     wait_copies(sends)
     wait_copies(outs)
 
@@ -291,7 +292,8 @@
     )
 
 
-def ahead_kernel(expo_hbm, recip_hbm, weights_ref, recip_ref, expo_ref, sems):
+def ahead_kernel(expo_hbm, recip_hbm, table_hbm, second_hbm, weights_ref, table_ref, second_ref,
+                 recip_ref, expo_ref, sems, small_sems):
     steps = N_DEV // GROUP
     span = GROUP * QLEN
     fetch = []
@@ -302,6 +304,7 @@
                 ((recip_hbm.at[rows], recip_ref.at[rows]), (expo_hbm.at[rows], expo_ref.at[rows])), sems.at[i]
             )
         )
+    small = start_copies(((table_hbm, table_ref), (second_hbm, second_ref)), small_sems)
     spread = expander(2).astype(BF)
     lane = iota((span, DIM), 1)
     for i in range(steps):
@@ -312,30 +315,31 @@
         lo = recip - hi
         factor = jnp.where(lane < SLOTS, hi, jnp.where(lane < 2 * SLOTS, pltpu.roll(lo, SLOTS, 1), 0.0))
         weights_ref[rows, :] = (expo_ref[rows, :] * dot(factor.astype(BF), spread)).astype(BF)
-
-
-def query_kernel(sums_ref, const_hbm, me_ref, table_hbm, second_hbm, weights_ref, embed_ref, place_hbm,
+    wait_copies(small)
+
+
+def query_kernel(sums_ref, const_hbm, me_ref, table_ref, second_ref, weights_ref, embed_ref, place_hbm,
                  send_hbm, mixed_hbm, loss_hbm,
-                 const_ref, table_ref, second_ref, loss_ref, wide_ref, send_ref, mixed_ref, smem_ref,
+                 const_ref, loss_ref, wide_ref, send_ref, mixed_ref, smem_ref,
                  sems, out_sems, part_sems):
     small = start_copies(
-        ((table_hbm, table_ref), (place_hbm, smem_ref), (const_hbm, const_ref), (second_hbm, second_ref)), sems
+        ((place_hbm, smem_ref), (const_hbm, const_ref)), sems
     )
     sums = jnp.sum(sums_ref[...], axis=0)
     log_sum = jnp.log(jnp.where(sums > 0.0, sums, 1.0))
     turned = jnp.transpose(jnp.concatenate([sums, jnp.zeros((DIM - 8, DIM), F32)], axis=0))[0:N_DEV, :]
-    wait_copies(small)
-    loss = const_ref[0:2, :] + log_sum[0:2, :] - sums[2:4, :]
-    picked = jnp.where(iota((2, DIM), 1) == me_ref[0], loss, 0.0)
-    loss_ref[...] = jnp.broadcast_to(jnp.sum(picked, axis=-1, keepdims=True), (2, DIM))
     normal = jnp.where(table_ref[2] > 0.5, turned[:, 1:2], turned[:, 0:1])
     pull = LOSS_SCALE * (table_ref[0] / normal - table_ref[1])
-    outs = start_copies(((loss_ref, loss_hbm),), out_sems)
     hi = pull.astype(BF).astype(F32)
     lo = pull - hi
     lane = iota((N_DEV, DIM), 1)
     factor = jnp.where(lane < SLOTS, hi, jnp.where(lane < 2 * SLOTS, pltpu.roll(lo, SLOTS, 1), 0.0))
     wide_ref[...] = dot(factor.astype(BF), expander(2).astype(BF))
+    wait_copies(small)
+    loss = const_ref[0:2, :] + log_sum[0:2, :] - sums[2:4, :]
+    picked = jnp.where(iota((2, DIM), 1) == me_ref[0], loss, 0.0)
+    loss_ref[...] = jnp.broadcast_to(jnp.sum(picked, axis=-1, keepdims=True), (2, DIM))
+    outs = start_copies(((loss_ref, loss_hbm),), out_sems)
 
     def part_copies(i):
         some = pl.ds(i * CHUNK, CHUNK)
@@ -559,20 +563,25 @@
     )(recv, in_vmem(embed))
     all_sums = exchange(sums, "dev")
 
-    weights = pl.pallas_call(
+    weights, near_table, near_second = pl.pallas_call(
         ahead_kernel,
-        out_shape=pltpu.VMEM((N_DEV * QLEN, WIDE), BF),
-        in_specs=[HBM, HBM],
-        out_specs=VMEM,
+        out_shape=(
+            pltpu.VMEM((N_DEV * QLEN, WIDE), BF),
+            pltpu.VMEM((3, N_DEV, DIM), F32),
+            pltpu.VMEM((N_DEV, WIDE), F32),
+        ),
+        in_specs=[HBM] * 4,
+        out_specs=(VMEM,) * 3,
         scratch_shapes=[
             pltpu.VMEM((N_DEV * QLEN, DIM), F32),
             pltpu.VMEM((N_DEV * QLEN, WIDE), F32),
             pltpu.SemaphoreType.DMA((N_DEV // GROUP, 2)),
+            pltpu.SemaphoreType.DMA((2,)),
         ],
         cost_estimate=estimate(2 * TOKENS * D * DIM, 15_000_000),
         compiler_params=params(12),
         name="ahead",
-    )(in_hbm(expo), in_hbm(recip))
+    )(in_hbm(expo), in_hbm(recip), in_hbm(table), in_hbm(second))
 
     me = lax.axis_index("dev").astype(jnp.int32).reshape(1)
     send_delta, mixed, loss = pl.pallas_call(
@@ -582,24 +591,22 @@
             pltpu.HBM((N_DEV * QLEN, WIDE), BF),
             pltpu.HBM((2, DIM), F32),
         ),
-        in_specs=[VMEM, HBM, SMEM, HBM, HBM, VMEM, VMEM, HBM],
+        in_specs=[VMEM, HBM, SMEM, VMEM, VMEM, VMEM, VMEM, HBM],
         out_specs=(HBM, HBM, HBM),
         scratch_shapes=[
             pltpu.VMEM((8, DIM), F32),
-            pltpu.VMEM((3, N_DEV, DIM), F32),
-            pltpu.VMEM((N_DEV, WIDE), F32),
             pltpu.VMEM((2, DIM), F32),
             pltpu.VMEM((N_DEV, WIDE), F32),
             pltpu.VMEM((N_DEV, QROWS, DIM), BF),
             pltpu.VMEM((N_DEV * QLEN, WIDE), BF),
             pltpu.SMEM((N_DEV, DIM), jnp.int32),
-            pltpu.SemaphoreType.DMA((4,)),
+            pltpu.SemaphoreType.DMA((2,)),
             pltpu.SemaphoreType.DMA((1,)),
             pltpu.SemaphoreType.DMA((N_DEV // CHUNK, 2)),
         ],
         compiler_params=params(12),
         name="query",
-    )(all_sums, in_hbm(const), me, in_hbm(table), in_hbm(second), in_vmem(weights), in_vmem(embed), in_hbm(place))
+    )(all_sums, in_hbm(const), me, in_vmem(near_table), in_vmem(near_second), in_vmem(weights), in_vmem(embed), in_hbm(place))
     recv_delta = exchange(send_delta, "dev")
 
     preact, head = pl.pallas_call(

time: 97 us -> 96.5 us (level)
  no operation moved by 1% of the time
where the time goes in v6:
time: 96.5 us; the launch traced here: 95.9 us
  Pallas kernels  36.1 us (37%)
  starting transfers between devices  20.9 us (22%)
  waiting for transfers between devices  18.9 us (20%)
  blocking collectives  17.8 us (18%)
    all_to_all x4, starting transfers between devices, exchange(): return lax.all_to_all(x, axes, split_axis=0, concat_axis=0, tiled=True)  20.9 us
    all_to_all x4, waiting for transfers between devices, exchange(): return lax.all_to_all(x, axes, split_axis=0, concat_axis=0, tiled=True)  18.9 us
    all_to_all x1, blocking collectives, exchange(): return lax.all_to_all(x, axes, split_axis=0, concat_axis=0, tiled=True)  17.8 us
    pallas_call x1, Pallas kernels, on_device(): pl.pallas_call(stored_kernel, out_shape=(pltpu.HBM((TOKENS, DIM), BF), pl...  7.93 us
    pallas_call x1, Pallas kernels, on_device(): pl.pallas_call(encode_kernel, out_shape=(pltpu.VMEM((TOKENS, DIM), BF), p...  7.74 us
    pallas_call x1, Pallas kernels, on_device(): pl.pallas_call(back_kernel, out_shape=(pltpu.HBM((TOKENS, D), BF), pltpu....  5.75 us
    pallas_call x1, Pallas kernels, on_device(): pl.pallas_call(score_kernel, out_shape=(pltpu.HBM((N_DEV * QLEN, WIDE), F...  4.54 us
    pallas_call x1, Pallas kernels, on_device(): pl.pallas_call(query_kernel, out_shape=(pltpu.HBM((N_DEV, QROWS, DIM), BF...  3 us
  transfers between devices with their start and end apart: 4, of which 4 were waited for; matrix products, arithmetic and copies ran while one was open for 1% of the time, Pallas kernels for 25%

profile of v6, /device:TPU:1, one launch (start us, length us, event | category | flops | bytes accessed | tf_op | source)
XLA Modules:
  0.0 95.9 jit_solution(4793413690803084421)
XLA Ops:
  0.6 2.7 %request.1 = (bf16[32,80,128]{2,1,0:T(8,128)(2,1)}, f32[64,128]{1,0:T(8,128)}, f32[8,128]{1,0:T(8,128)}) custom-call(bf16[64,768]{1,0:T(8,128)(2,1)} %bitcast.12, bf16[768,128]{1,0:T(8,128)(2,1)} %weight_hbm.5, f32[2,64]{1,0:T(2,128)} %teacher_hbm.1, s32[2,64]{1,0:T(2,128)} %cand_hbm.1, s32[1,4096]{1,0:T(1,128)} %storage_hbm.1, s32[1,4096]{1,0:T(1,128)} %lengths_hbm.1), custom_call_target="tpu_custom_call" | custom-call | tf_op jit(solution)/shard_map/request/pallas_call | solution.py:486
  3.3 8.6 %all-to-all-start = ((bf16[32,80,128]{2,1,0:T(8,128)(2,1)}), bf16[32,80,128]{2,1,0:T(8,128)(2,1)S(1)}, u32[]{:S(2)}, u32[]{:S(2)}) async-start(bf16[32,80,128]{2,1,0:T(8,128)(2,1)} %get-tuple-element.28), calls=%async_computation | async-start | bytes 1310720 | tf_op jit(solution)/shard_map/all_to_all | solution.py:475
  11.9 7.7 %encode.1 = (bf16[6144,128]{1,0:T(8,128)(2,1)S(1)}, f32[128,128]{1,0:T(8,128)}) custom-call(bf16[6144,768]{1,0:T(8,128)(2,1)} %bitcast.10, bf16[768,128]{1,0:T(8,128)(2,1)} %weight_hbm.5), custom_call_target="tpu_custom_call" | custom-call | flops 1207959552 | bytes 15000000 | tf_op jit(solution)/shard_map/encode/pallas_call | solution.py:517
  19.7 5.2 %all-to-all-done.recv_ref = bf16[32,80,128]{2,1,0:T(8,128)(2,1)S(1)} async-done(((bf16[32,80,128]{2,1,0:T(8,128)(2,1)}), bf16[32,80,128]{2,1,0:T(8,128)(2,1)S(1)}, u32[]{:S(2)}, u32[]{:S(2)}) %all-to-all-start) | async-done | bytes 655392 | tf_op jit(solution)/shard_map/all_to_all | solution.py:475
  24.8 4.5 %score.1 = (f32[1024,576]{1,0:T(8,128)}, f32[1024,128]{1,0:T(8,128)}, f32[32,8,128]{2,1,0:T(8,128)}, f32[3,32,128]{2,1,0:T(8,128)}, f32[32,576]{1,0:T(8,128)}, /...) custom-call(bf16[32,80,128]{2,1,0:T(8,128)(2,1)S(1)} %all-to-all-done.recv_ref, ...), custom_call_target="tpu_custom_call" | custom-call | tf_op jit(solution)/shard_map/score/pallas_call | solution.py:534
  29.4 4.1 %all-to-all-start.1 = ((f32[32,8,128]{2,1,0:T(8,128)}), f32[32,8,128]{2,1,0:T(8,128)S(1)}, u32[]{:S(2)}, u32[]{:S(2)}) async-start(f32[32,8,128]{2,1,0:T(8,128)} %get-tuple-element.30), calls=%async_computation.1 | async-start | bytes 262144 | tf_op jit(solution)/shard_map/all_to_all | solution.py:475
  33.5 2.4 %ahead.1 = (bf16[1024,576]{1,0:T(8,128)(2,1)S(1)}, f32[3,32,128]{2,1,0:T(8,128)S(1)}, f32[32,576]{1,0:T(8,128)S(1)}) custom-call(f32[1024,576]{1,0:T(8,128)} %get-tuple-element.32.expo_hbm, f32[1024,128]{1,0:T(8,128)} %get-tuple-element.33.recip_hbm, f32[3,32,128]{2,1,0:T(8,128)} %get-tuple-element.34.table_hbm, f32[32,576]{1,0:T(8,128)} %get-tuple-element.35.second_hbm), custom_call_target="tpu_custom_call" | custom-call | flops 1207959552 | bytes 15000000 | tf_op jit(solution)/shard_map/ahead/pallas_call | solution.py:566
  35.9 5.3 %all-to-all-done.1.sums_ref = f32[32,8,128]{2,1,0:T(8,128)S(1)} async-done(((f32[32,8,128]{2,1,0:T(8,128)}), f32[32,8,128]{2,1,0:T(8,128)S(1)}, u32[]{:S(2)}, u32[]{:S(2)}) %all-to-all-start.1) | async-done | bytes 131104 | tf_op jit(solution)/shard_map/all_to_all | solution.py:475
  41.2 3.0 %query.1 = (bf16[32,64,128]{2,1,0:T(8,128)(2,1)}, bf16[1024,576]{1,0:T(8,128)(2,1)}, f32[2,128]{1,0:T(2,128)}) custom-call(f32[32,8,128]{2,1,0:T(8,128)S(1)} %all-to-all-done.1.sums_ref, f32[8,128]{1,0:T(8,128)} %get-tuple-element.31.const_hbm, s32[1]{0:T(128)} %bitcast.2.me_ref, f32[3,32,128]{2,1,0:T(8,128)S(1)} %get-tuple-element.36.table_ref, ...), custom_call_target="tpu_custom_call" | custom-call | tf_op jit(solution)/shard_map/query/pallas_call | solution.py:587
  44.2 4.0 %all-to-all-start.2 = ((bf16[32,64,128]{2,1,0:T(8,128)(2,1)}), bf16[32,64,128]{2,1,0:T(8,128)(2,1)S(1)}, u32[]{:S(2)}, u32[]{:S(2)}) async-start(bf16[32,64,128]{2,1,0:T(8,128)(2,1)} %get-tuple-element.41), calls=%async_computation.2 | async-start | bytes 1048576 | tf_op jit(solution)/shard_map/all_to_all | solution.py:475
  48.2 7.9 %stored.1 = (bf16[6144,128]{1,0:T(8,128)(2,1)}, f32[768,128]{1,0:T(8,128)S(1)}) custom-call(s32[32,128]{1,0:T(8,128)} %get-tuple-element.39.place_hbm, bf16[32,64,128]{2,1,0:T(8,128)(2,1)} %get-tuple-element.43.queries_hbm, f32[32,576]{1,0:T(8,128)} %get-tuple-element.35.second_hbm, bf16[1024,576]{1,0:T(8,128)(2,1)} %get-tuple-element.44.mixed_hbm, ...), custom_call_target="tpu_custom_call" | custom-call | flops 2415919104 | bytes 20000000 | tf_op jit(solution)/shard_map/stored/pallas_call | solution.py:612
  56.1 0.0 copy-start
  56.1 3.7 %all-to-all-done.2.recv_ref = bf16[32,64,128]{2,1,0:T(8,128)(2,1)S(1)} async-done(((bf16[32,64,128]{2,1,0:T(8,128)(2,1)}), bf16[32,64,128]{2,1,0:T(8,128)(2,1)S(1)}, u32[]{:S(2)}, u32[]{:S(2)}) %all-to-all-start.2) | async-done | bytes 524320 | tf_op jit(solution)/shard_map/all_to_all | solution.py:475
  59.8 1.2 %finish.1 = (bf16[64,128]{1,0:T(8,128)(2,1)S(1)}, bf16[128,8,128]{2,1,0:T(8,128)(2,1)S(1)}) custom-call(bf16[32,64,128]{2,1,0:T(8,128)(2,1)S(1)} %all-to-all-done.2.recv_ref, bf16[64,768]{1,0:T(8,128)(2,1)} %bitcast.13, f32[64,128]{1,0:T(8,128)} %get-tuple-element.42.proj_hbm, f32[768,128]{1,0:T(8,128)S(1)} %get-tuple-element.46.head_ref), custom_call_target="tpu_custom_call" | custom-call | tf_op jit(solution)/shard_map/finish/pallas_call | solution.py:638
  61.0 17.8 %all_to_all.25.recv_ref = bf16[128,8,128]{2,1,0:T(8,128)(2,1)S(1)} all-to-all(bf16[128,8,128]{2,1,0:T(8,128)(2,1)S(1)} %get-tuple-element.47), channel_id=1, replica_groups=mesh['group'=4,'dev'=32] {'group','dev'}, dimensions={0} | all-to-all | bytes 524288 | tf_op jit(solution)/shard_map/all_to_all | solution.py:475
  78.9 0.9 reduce.3
  79.7 4.3 %all-to-all-start.4 = ((bf16[128,8,128]{2,1,0:T(8,128)(2,1)}), bf16[128,8,128]{2,1,0:T(8,128)(2,1)S(1)}, u32[]{:S(2)}, u32[]{:S(2)}) async-start(bf16[128,8,128]{2,1,0:T(8,128)(2,1)} %reduce.3), calls=%async_computation.4 | async-start | bytes 524288 | tf_op jit(solution)/shard_map/all_to_all | solution.py:475
  84.0 0.0 copy-done
  84.0 0.6 slice_reduce_fusion
  84.7 5.8 %back.1 = (bf16[6144,768]{1,0:T(8,128)(2,1)}, bf16[64,768]{1,0:T(8,128)(2,1)}) custom-call(bf16[6144,128]{1,0:T(8,128)(2,1)} %get-tuple-element.48.preact_hbm, bf16[768,128]{1,0:T(8,128)(2,1)} %weight_hbm.5, bf16[64,128]{1,0:T(8,128)(2,1)S(1)} %get-tuple-element.49.query_ref), custom_call_target="tpu_custom_call" | custom-call | flops 1207959552 | bytes 15000000 | tf_op jit(solution)/shard_map/back/pallas_call | solution.py:653
  90.4 4.7 %all-to-all-done.4 = bf16[128,8,128]{2,1,0:T(8,128)(2,1)S(1)} async-done(((bf16[128,8,128]{2,1,0:T(8,128)(2,1)}), bf16[128,8,128]{2,1,0:T(8,128)(2,1)S(1)}, u32[]{:S(2)}, u32[]{:S(2)}) %all-to-all-start.4) | async-done | bytes 262176 | tf_op jit(solution)/shard_map/all_to_all | solution.py:475
  95.1 0.8 fusion
Async XLA Ops:
  3.3 21.5 %all-to-all-start = ((bf16[32,80,128]{2,1,0:T(8,128)(2,1)}), bf16[32,80,128]{2,1,0:T(8,128)(2,1)S(1)}, u32[]{:S(2)}, u32[]{:S(2)}) async-start(bf16[32,80,128]{2,1,0:T(8,128)(2,1)} %get-tuple-element.28), calls=%async_computation | async-start | bytes 1310720 | tf_op jit(solution)/shard_map/all_to_all | solution.py:475
  29.4 11.8 %all-to-all-start.1 = ((f32[32,8,128]{2,1,0:T(8,128)}), f32[32,8,128]{2,1,0:T(8,128)S(1)}, u32[]{:S(2)}, u32[]{:S(2)}) async-start(f32[32,8,128]{2,1,0:T(8,128)} %get-tuple-element.30), calls=%async_computation.1 | async-start | bytes 262144 | tf_op jit(solution)/shard_map/all_to_all | solution.py:475
  44.2 15.6 %all-to-all-start.2 = ((bf16[32,64,128]{2,1,0:T(8,128)(2,1)}), bf16[32,64,128]{2,1,0:T(8,128)(2,1)S(1)}, u32[]{:S(2)}, u32[]{:S(2)}) async-start(bf16[32,64,128]{2,1,0:T(8,128)(2,1)} %get-tuple-element.41), calls=%async_computation.2 | async-start | bytes 1048576 | tf_op jit(solution)/shard_map/all_to_all | solution.py:475
  56.1 27.9 %copy-start = (f32[2,128]{1,0:T(2,128)S(1)}, f32[2,128]{1,0:T(2,128)}, u32[]{:S(2)}) copy-start(f32[2,128]{1,0:T(2,128)} %get-tuple-element.40) | copy-start | bytes 3076
  79.7 15.4 %all-to-all-start.4 = ((bf16[128,8,128]{2,1,0:T(8,128)(2,1)}), bf16[128,8,128]{2,1,0:T(8,128)(2,1)S(1)}, u32[]{:S(2)}, u32[]{:S(2)}) async-start(bf16[128,8,128]{2,1,0:T(8,128)(2,1)} %reduce.3), calls=%async_computation.4 | async-start | bytes 524288 | tf_op jit(solution)/shard_map/all_to_all | solution.py:475

commit v7 on v6

--- a/solution.py
+++ b/solution.py
@@ -350,15 +350,19 @@
         ]
 
     def chunk(i, carry):
+        blocks = []
         for u in range(CHUNK):
             s = i * CHUNK + u
             rows = pl.ds(pl.multiple_of(s * QLEN, QLEN), QLEN)
             mixed = weights_ref[rows, :].astype(F32) * wide_ref[pl.ds(s, 1), :]
             mixed_ref[rows, :] = mixed.astype(BF)
-            both = halves(mixed, second_ref[pl.ds(s, 1), :] > 0.5)
+            blocks.append(halves(mixed, second_ref[pl.ds(s, 1), :] > 0.5))
+        send_copy, mixed_copy = part_copies(i)
+        mixed_copy.start()
+        for u, both in enumerate(blocks):
+            s = i * CHUNK + u
             send_ref[s] = dot(both, stored_rows(embed_ref, smem_ref, s)).astype(BF)
-        for copy in part_copies(i):
-            copy.start()
+        send_copy.start()
         return carry
 
     for i in range(N_DEV // CHUNK):

time: 96.5 us -> 96.4 us (level)
  no operation moved by 1% of the time
where the time goes in v7:
time: 96.4 us; the launch traced here: 95.8 us
  Pallas kernels  36 us (37%)
  starting transfers between devices  21 us (22%)
  waiting for transfers between devices  18.9 us (20%)
  blocking collectives  17.8 us (18%)
    all_to_all x4, starting transfers between devices, exchange(): return lax.all_to_all(x, axes, split_axis=0, concat_axis=0, tiled=True)  21 us
    all_to_all x4, waiting for transfers between devices, exchange(): return lax.all_to_all(x, axes, split_axis=0, concat_axis=0, tiled=True)  18.9 us
    all_to_all x1, blocking collectives, exchange(): return lax.all_to_all(x, axes, split_axis=0, concat_axis=0, tiled=True)  17.8 us
    pallas_call x1, Pallas kernels, on_device(): pl.pallas_call(stored_kernel, out_shape=(pltpu.HBM((TOKENS, DIM), BF), pl...  7.93 us
    pallas_call x1, Pallas kernels, on_device(): pl.pallas_call(encode_kernel, out_shape=(pltpu.VMEM((TOKENS, DIM), BF), p...  7.74 us
    pallas_call x1, Pallas kernels, on_device(): pl.pallas_call(back_kernel, out_shape=(pltpu.HBM((TOKENS, D), BF), pltpu....  5.75 us
    pallas_call x1, Pallas kernels, on_device(): pl.pallas_call(score_kernel, out_shape=(pltpu.HBM((N_DEV * QLEN, WIDE), F...  4.54 us
    pallas_call x1, Pallas kernels, on_device(): pl.pallas_call(query_kernel, out_shape=(pltpu.HBM((N_DEV, QROWS, DIM), BF...  2.89 us
  transfers between devices with their start and end apart: 4, of which 4 were waited for; matrix products, arithmetic and copies ran while one was open for 1% of the time, Pallas kernels for 25%

profile of v7, /device:TPU:1, one launch (start us, length us, event | category | flops | bytes accessed | tf_op | source)
XLA Modules:
  0.0 95.8 jit_solution(12580800177805452037)
XLA Ops:
  0.6 2.7 %request.1 = (bf16[32,80,128]{2,1,0:T(8,128)(2,1)}, f32[64,128]{1,0:T(8,128)}, f32[8,128]{1,0:T(8,128)}) custom-call(bf16[64,768]{1,0:T(8,128)(2,1)} %bitcast.12, bf16[768,128]{1,0:T(8,128)(2,1)} %weight_hbm.5, f32[2,64]{1,0:T(2,128)} %teacher_hbm.1, s32[2,64]{1,0:T(2,128)} %cand_hbm.1, s32[1,4096]{1,0:T(1,128)} %storage_hbm.1, s32[1,4096]{1,0:T(1,128)} %lengths_hbm.1), custom_call_target="tpu_custom_call" | custom-call | tf_op jit(solution)/shard_map/request/pallas_call | solution.py:490
  3.3 8.6 %all-to-all-start = ((bf16[32,80,128]{2,1,0:T(8,128)(2,1)}), bf16[32,80,128]{2,1,0:T(8,128)(2,1)S(1)}, u32[]{:S(2)}, u32[]{:S(2)}) async-start(bf16[32,80,128]{2,1,0:T(8,128)(2,1)} %get-tuple-element.28), calls=%async_computation | async-start | bytes 1310720 | tf_op jit(solution)/shard_map/all_to_all | solution.py:479
  11.9 7.7 %encode.1 = (bf16[6144,128]{1,0:T(8,128)(2,1)S(1)}, f32[128,128]{1,0:T(8,128)}) custom-call(bf16[6144,768]{1,0:T(8,128)(2,1)} %bitcast.10, bf16[768,128]{1,0:T(8,128)(2,1)} %weight_hbm.5), custom_call_target="tpu_custom_call" | custom-call | flops 1207959552 | bytes 15000000 | tf_op jit(solution)/shard_map/encode/pallas_call | solution.py:521
  19.7 5.2 %all-to-all-done.recv_ref = bf16[32,80,128]{2,1,0:T(8,128)(2,1)S(1)} async-done(((bf16[32,80,128]{2,1,0:T(8,128)(2,1)}), bf16[32,80,128]{2,1,0:T(8,128)(2,1)S(1)}, u32[]{:S(2)}, u32[]{:S(2)}) %all-to-all-start) | async-done | bytes 655392 | tf_op jit(solution)/shard_map/all_to_all | solution.py:479
  24.8 4.5 %score.1 = (f32[1024,576]{1,0:T(8,128)}, f32[1024,128]{1,0:T(8,128)}, f32[32,8,128]{2,1,0:T(8,128)}, f32[3,32,128]{2,1,0:T(8,128)}, f32[32,576]{1,0:T(8,128)}, /...) custom-call(bf16[32,80,128]{2,1,0:T(8,128)(2,1)S(1)} %all-to-all-done.recv_ref, ...), custom_call_target="tpu_custom_call" | custom-call | tf_op jit(solution)/shard_map/score/pallas_call | solution.py:538
  29.4 4.1 %all-to-all-start.1 = ((f32[32,8,128]{2,1,0:T(8,128)}), f32[32,8,128]{2,1,0:T(8,128)S(1)}, u32[]{:S(2)}, u32[]{:S(2)}) async-start(f32[32,8,128]{2,1,0:T(8,128)} %get-tuple-element.30), calls=%async_computation.1 | async-start | bytes 262144 | tf_op jit(solution)/shard_map/all_to_all | solution.py:479
  33.5 2.4 %ahead.1 = (bf16[1024,576]{1,0:T(8,128)(2,1)S(1)}, f32[3,32,128]{2,1,0:T(8,128)S(1)}, f32[32,576]{1,0:T(8,128)S(1)}) custom-call(f32[1024,576]{1,0:T(8,128)} %get-tuple-element.32.expo_hbm, f32[1024,128]{1,0:T(8,128)} %get-tuple-element.33.recip_hbm, f32[3,32,128]{2,1,0:T(8,128)} %get-tuple-element.34.table_hbm, f32[32,576]{1,0:T(8,128)} %get-tuple-element.35.second_hbm), custom_call_target="tpu_custom_call" | custom-call | flops 1207959552 | bytes 15000000 | tf_op jit(solution)/shard_map/ahead/pallas_call | solution.py:570
  35.9 5.3 %all-to-all-done.1.sums_ref = f32[32,8,128]{2,1,0:T(8,128)S(1)} async-done(((f32[32,8,128]{2,1,0:T(8,128)}), f32[32,8,128]{2,1,0:T(8,128)S(1)}, u32[]{:S(2)}, u32[]{:S(2)}) %all-to-all-start.1) | async-done | bytes 131104 | tf_op jit(solution)/shard_map/all_to_all | solution.py:479
  41.2 2.9 %query.1 = (bf16[32,64,128]{2,1,0:T(8,128)(2,1)}, bf16[1024,576]{1,0:T(8,128)(2,1)}, f32[2,128]{1,0:T(2,128)}) custom-call(f32[32,8,128]{2,1,0:T(8,128)S(1)} %all-to-all-done.1.sums_ref, f32[8,128]{1,0:T(8,128)} %get-tuple-element.31.const_hbm, s32[1]{0:T(128)} %bitcast.2.me_ref, f32[3,32,128]{2,1,0:T(8,128)S(1)} %get-tuple-element.36.table_ref, ...), custom_call_target="tpu_custom_call" | custom-call | tf_op jit(solution)/shard_map/query/pallas_call | solution.py:591
  44.1 4.0 %all-to-all-start.2 = ((bf16[32,64,128]{2,1,0:T(8,128)(2,1)}), bf16[32,64,128]{2,1,0:T(8,128)(2,1)S(1)}, u32[]{:S(2)}, u32[]{:S(2)}) async-start(bf16[32,64,128]{2,1,0:T(8,128)(2,1)} %get-tuple-element.41), calls=%async_computation.2 | async-start | bytes 1048576 | tf_op jit(solution)/shard_map/all_to_all | solution.py:479
  48.1 7.9 %stored.1 = (bf16[6144,128]{1,0:T(8,128)(2,1)}, f32[768,128]{1,0:T(8,128)S(1)}) custom-call(s32[32,128]{1,0:T(8,128)} %get-tuple-element.39.place_hbm, bf16[32,64,128]{2,1,0:T(8,128)(2,1)} %get-tuple-element.43.queries_hbm, f32[32,576]{1,0:T(8,128)} %get-tuple-element.35.second_hbm, bf16[1024,576]{1,0:T(8,128)(2,1)} %get-tuple-element.44.mixed_hbm, ...), custom_call_target="tpu_custom_call" | custom-call | flops 2415919104 | bytes 20000000 | tf_op jit(solution)/shard_map/stored/pallas_call | solution.py:616
  56.0 0.0 copy-start
  56.0 3.7 %all-to-all-done.2.recv_ref = bf16[32,64,128]{2,1,0:T(8,128)(2,1)S(1)} async-done(((bf16[32,64,128]{2,1,0:T(8,128)(2,1)}), bf16[32,64,128]{2,1,0:T(8,128)(2,1)S(1)}, u32[]{:S(2)}, u32[]{:S(2)}) %all-to-all-start.2) | async-done | bytes 524320 | tf_op jit(solution)/shard_map/all_to_all | solution.py:479
  59.7 1.2 %finish.1 = (bf16[64,128]{1,0:T(8,128)(2,1)S(1)}, bf16[128,8,128]{2,1,0:T(8,128)(2,1)S(1)}) custom-call(bf16[32,64,128]{2,1,0:T(8,128)(2,1)S(1)} %all-to-all-done.2.recv_ref, bf16[64,768]{1,0:T(8,128)(2,1)} %bitcast.13, f32[64,128]{1,0:T(8,128)} %get-tuple-element.42.proj_hbm, f32[768,128]{1,0:T(8,128)S(1)} %get-tuple-element.46.head_ref), custom_call_target="tpu_custom_call" | custom-call | tf_op jit(solution)/shard_map/finish/pallas_call | solution.py:642
  60.9 17.8 %all_to_all.25.recv_ref = bf16[128,8,128]{2,1,0:T(8,128)(2,1)S(1)} all-to-all(bf16[128,8,128]{2,1,0:T(8,128)(2,1)S(1)} %get-tuple-element.47), channel_id=1, replica_groups=mesh['group'=4,'dev'=32] {'group','dev'}, dimensions={0} | all-to-all | bytes 524288 | tf_op jit(solution)/shard_map/all_to_all | solution.py:479
  78.7 0.9 reduce.3
  79.6 4.3 %all-to-all-start.4 = ((bf16[128,8,128]{2,1,0:T(8,128)(2,1)}), bf16[128,8,128]{2,1,0:T(8,128)(2,1)S(1)}, u32[]{:S(2)}, u32[]{:S(2)}) async-start(bf16[128,8,128]{2,1,0:T(8,128)(2,1)} %reduce.3), calls=%async_computation.4 | async-start | bytes 524288 | tf_op jit(solution)/shard_map/all_to_all | solution.py:479
  83.9 0.0 copy-done
  83.9 0.6 slice_reduce_fusion
  84.5 5.8 %back.1 = (bf16[6144,768]{1,0:T(8,128)(2,1)}, bf16[64,768]{1,0:T(8,128)(2,1)}) custom-call(bf16[6144,128]{1,0:T(8,128)(2,1)} %get-tuple-element.48.preact_hbm, bf16[768,128]{1,0:T(8,128)(2,1)} %weight_hbm.5, bf16[64,128]{1,0:T(8,128)(2,1)S(1)} %get-tuple-element.49.query_ref), custom_call_target="tpu_custom_call" | custom-call | flops 1207959552 | bytes 15000000 | tf_op jit(solution)/shard_map/back/pallas_call | solution.py:657
  90.3 4.7 %all-to-all-done.4 = bf16[128,8,128]{2,1,0:T(8,128)(2,1)S(1)} async-done(((bf16[128,8,128]{2,1,0:T(8,128)(2,1)}), bf16[128,8,128]{2,1,0:T(8,128)(2,1)S(1)}, u32[]{:S(2)}, u32[]{:S(2)}) %all-to-all-start.4) | async-done | bytes 262176 | tf_op jit(solution)/shard_map/all_to_all | solution.py:479
  95.0 0.8 fusion
Async XLA Ops:
  3.3 21.5 %all-to-all-start = ((bf16[32,80,128]{2,1,0:T(8,128)(2,1)}), bf16[32,80,128]{2,1,0:T(8,128)(2,1)S(1)}, u32[]{:S(2)}, u32[]{:S(2)}) async-start(bf16[32,80,128]{2,1,0:T(8,128)(2,1)} %get-tuple-element.28), calls=%async_computation | async-start | bytes 1310720 | tf_op jit(solution)/shard_map/all_to_all | solution.py:479
  29.4 11.8 %all-to-all-start.1 = ((f32[32,8,128]{2,1,0:T(8,128)}), f32[32,8,128]{2,1,0:T(8,128)S(1)}, u32[]{:S(2)}, u32[]{:S(2)}) async-start(f32[32,8,128]{2,1,0:T(8,128)} %get-tuple-element.30), calls=%async_computation.1 | async-start | bytes 262144 | tf_op jit(solution)/shard_map/all_to_all | solution.py:479
  44.1 15.6 %all-to-all-start.2 = ((bf16[32,64,128]{2,1,0:T(8,128)(2,1)}), bf16[32,64,128]{2,1,0:T(8,128)(2,1)S(1)}, u32[]{:S(2)}, u32[]{:S(2)}) async-start(bf16[32,64,128]{2,1,0:T(8,128)(2,1)} %get-tuple-element.41), calls=%async_computation.2 | async-start | bytes 1048576 | tf_op jit(solution)/shard_map/all_to_all | solution.py:479
  56.0 27.9 %copy-start = (f32[2,128]{1,0:T(2,128)S(1)}, f32[2,128]{1,0:T(2,128)}, u32[]{:S(2)}) copy-start(f32[2,128]{1,0:T(2,128)} %get-tuple-element.40) | copy-start | bytes 3076
  79.6 15.4 %all-to-all-start.4 = ((bf16[128,8,128]{2,1,0:T(8,128)(2,1)}), bf16[128,8,128]{2,1,0:T(8,128)(2,1)S(1)}, u32[]{:S(2)}, u32[]{:S(2)}) async-start(bf16[128,8,128]{2,1,0:T(8,128)(2,1)} %reduce.3), calls=%async_computation.4 | async-start | bytes 524288 | tf_op jit(solution)/shard_map/all_to_all | solution.py:479
